TPU v7x, 256 devices: a whole 4x4x8 slice. The times are simulated.
256 devices in a mesh: bx: 4 (over x_hi, core), by: 32 (over y, z), ka: 2 (over x_lo).
Axes of the slice: x: 4 (x_hi: 2, x_lo: 2; x = x_hi * 2 + x_lo), y: 4, z: 8, core: 2. Of those that a mesh axis runs over, the one named last changes fastest.
Arguments:
- positions: float32 [3, 32768], P(None, ('bx', 'by', 'ka')), may hold values from 0 to 1024, as said below
- species: int32 [32768], P(('bx', 'by', 'ka')), may hold values from 0 to 5
- send_x: int32 [2, 8192], P(None, ('bx', 'by', 'ka')), may hold values from 0 to 127, as said below
- send_y: int32 [2, 12288], P(None, ('bx', 'by', 'ka')), may hold values from 0 to 191, as said below
- neighbours: int32 [24, 32768], P(None, ('bx', 'by', 'ka')), may hold values from 0 to 287, as said below
- live_slots: int32 [24, 32768], P(None, ('bx', 'by', 'ka')), may hold values from 0 to 1, as said below
- embedding: bfloat16 [128, 6], replicated, may hold values from -6 to 6
- radial_in: bfloat16 [2, 64, 8], replicated, may hold values from -2 to 2
- radial_mid: bfloat16 [2, 64, 64], replicated, may hold values from -0.75 to 0.75
- radial_out: bfloat16 [2, 384, 64], replicated, may hold values from -0.75 to 0.75
- mixing: bfloat16 [2, 128, 384], replicated, may hold values from -0.3125 to 0.3125
- read_first: float32 [128], replicated, may hold values from -0.5 to 0.5
- read_hidden: bfloat16 [16, 128], replicated, may hold values from -0.5 to 0.5
- read_last: float32 [16], replicated, may hold values from -1.5 to 1.5
- w_charge: bfloat16 [64, 128], replicated, may hold values from -0.5 to 0.5
- spectral: float32 [64, 1024], replicated, may hold values from 0.3 to 3
- wave_ids: int32 [3, 1024], replicated, may hold values from -7 to 8, as said below
Outputs:
- energies: float32 [32768], P(('bx', 'by', 'ka'))
- forces: float32 [3, 32768], P(None, ('bx', 'by', 'ka'))
Inputs may be any that keep to these rules, and one draw needn't show every extreme that they name: `positions`: the atoms of device (bx, by, ka) lie in x from 16 bx to 16 bx + 16, y from 16 (by 2 + ka) to that plus 16, z from 0 to 16. `send_x`: row 0 lists every own atom within 4 of the device's lower face along x, row 1 every own atom within 4 of its upper face. `send_y`: indices into the device's own atoms followed by those received from the lower and then the upper device along bx; row 0 lists every such entry within 4 of the device's lower face along y, row 1 every one within 4 of its upper face. `neighbours`: indices into the device's atom table: own atoms, then those from the lower and upper device along bx, then those from the lower and upper device along by+ka; a live slot names a table atom within the cutoff of 4, never the atom itself, each at most once; live slots come first in each atom's list. `live_slots`: the share of live slots differs from device to device. The 1024 columns are distinct k-vectors of one half-space: wave_ids[2] runs from 1 to 8 and the other two rows from -7 to 7, so no two columns are equal or opposite.
All inputs are finite; a program needn't handle non-finite values.
Results may differ from a plain program's by a relative error of at most 0.006.
Values sent between devices are 32-bit elements; how exact they have to be, the bound alone decides.
No kernel may reach another device: no remote copies, remote signals or barrier semaphores. Data moves between devices by JAX's collectives and lax.ppermute only.
A program may use at most 128 MiB of HBM per device.

v0:
```python
import math

import jax
import jax.numpy as jnp
from jax import lax
from jax.sharding import PartitionSpec as P

CUTOFF = 4.0
SOFTEN = 0.25
WIDTH_X = 16.0
WIDTH_Y = 16.0
DEPTH_Z = 16.0
ACT_GAIN = 1.679
ROOT_THREE = math.sqrt(3.0)
HIGHEST_PRECISION = lax.Precision.HIGHEST


def from_behind(array, axis, by):
    count = lax.axis_size(axis)
    return lax.ppermute(array, axis, [(i, (i + by) % count) for i in range(count)])


def partner(value, axis, distance):
    mask = 2**distance
    pairs = [(source, source ^ mask) for source in range(lax.axis_size(axis))]
    return lax.ppermute(value, axis, pairs)


def activate(inputs):
    return ACT_GAIN * jax.nn.silu(inputs)


def edge_geometry(pos_table, neighbours, live_slots, box_x, box_y):
    atom_count = neighbours.shape[1]
    centre = pos_table[:, :atom_count]
    others = jnp.take(pos_table, neighbours, axis=1)
    offsets = others - centre[:, None, :]
    step_x = offsets[0] - box_x * jnp.floor(offsets[0] / box_x + 0.5)
    step_y = offsets[1] - box_y * jnp.floor(offsets[1] / box_y + 0.5)
    step_z = offsets[2]
    square = step_x * step_x + step_y * step_y + step_z * step_z
    distance = jnp.sqrt(square + SOFTEN)
    envelope = jnp.square(jnp.maximum(1.0 - square / (CUTOFF * CUTOFF), 0.0)) * live_slots.astype(
        jnp.float32
    )
    unit_x = step_x / CUTOFF
    unit_y = step_y / CUTOFF
    unit_z = step_z / CUTOFF
    harmonics = jnp.stack(
        [
            jnp.ones_like(unit_x),
            unit_x,
            unit_y,
            unit_z,
            unit_x * unit_y,
            unit_y * unit_z,
            unit_z * unit_x,
            unit_x * unit_x - unit_y * unit_y,
            (2.0 * unit_z * unit_z - unit_x * unit_x - unit_y * unit_y) / ROOT_THREE,
        ]
    )
    return (distance, envelope, harmonics)


def interaction(
    radial_in,
    radial_mid,
    radial_out,
    mixing,
    pos_table,
    feat_table,
    neighbours,
    live_slots,
    box_x,
    box_y,
):
    slot_count, atom_count = neighbours.shape
    distance, envelope, harmonics = edge_geometry(pos_table, neighbours, live_slots, box_x, box_y)
    basis_count = radial_in.shape[1]
    spacing = CUTOFF / (basis_count - 1)
    centres = jnp.arange(basis_count, dtype=jnp.float32) * spacing
    basis_rows = jnp.exp(-jnp.square((distance[None] - centres[:, None, None]) / spacing))
    basis_rows = basis_rows.reshape(basis_count, slot_count * atom_count).astype(jnp.bfloat16)
    first_hidden = activate(
        jnp.dot(radial_in, basis_rows, preferred_element_type=jnp.float32)
    ).astype(jnp.bfloat16)
    second_hidden = activate(
        jnp.dot(radial_mid, first_hidden, preferred_element_type=jnp.float32)
    ).astype(jnp.bfloat16)
    radial = jnp.dot(radial_out, second_hidden, preferred_element_type=jnp.float32)
    channels = mixing.shape[0]
    radial = radial.reshape(3, channels, slot_count, atom_count) * envelope[None, None]
    source = jnp.take(feat_table, neighbours, axis=1)
    scalar = jnp.einsum(
        "cni,cni,ni->ci", radial[0], source, harmonics[0], precision=HIGHEST_PRECISION
    )
    vector = jnp.einsum(
        "cni,cni,mni->mci", radial[1], source, harmonics[1:4], precision=HIGHEST_PRECISION
    )
    tensor = jnp.einsum(
        "cni,cni,mni->mci", radial[2], source, harmonics[4:9], precision=HIGHEST_PRECISION
    )
    invariants = jnp.concatenate(
        [scalar, jnp.sum(vector * vector, 0), jnp.sum(tensor * tensor, 0)], 0
    ).astype(jnp.bfloat16)
    return feat_table[:, :atom_count] + jnp.dot(
        mixing, invariants, preferred_element_type=jnp.float32
    )


def readout(h_one, h_two, read_first, read_hidden, read_last, w_charge):
    rounded = h_two.astype(jnp.bfloat16)
    hidden = activate(jnp.dot(read_hidden, rounded, preferred_element_type=jnp.float32))
    site_local = jnp.sum(read_first[:, None] * h_one, 0) + jnp.sum(read_last[:, None] * hidden, 0)
    charge = jnp.dot(w_charge, rounded, preferred_element_type=jnp.float32)
    return (site_local, charge)


def structure(positions, charge, wave_ids, box_x, box_y):
    wave = wave_ids.astype(jnp.float32) * (2.0 * math.pi)
    phase = (
        wave[0][:, None] * (positions[0] / box_x)[None]
        + wave[1][:, None] * (positions[1] / box_y)[None]
        + wave[2][:, None] * (positions[2] / DEPTH_Z)[None]
    )
    cosine_sum = jnp.einsum("cm,km->ck", charge, jnp.cos(phase), precision=HIGHEST_PRECISION)
    sine_sum = jnp.einsum("cm,km->ck", charge, jnp.sin(phase), precision=HIGHEST_PRECISION)
    return (cosine_sum, sine_sum)


def spread_x(block_rows, step_by):
    return from_behind(block_rows, "bx", step_by)


def spread_y(block_rows, step_by):
    return from_behind(block_rows, ("by", "ka"), step_by)


def swap_partner(block_rows):
    return partner(block_rows, "ka", 0)


def ghost_table(local_rows, send_x, send_y):
    extended = jnp.concatenate(
        [
            local_rows,
            spread_x(jnp.take(local_rows, send_x[1], axis=1), 1),
            spread_x(jnp.take(local_rows, send_x[0], axis=1), -1),
        ],
        axis=1,
    )
    return jnp.concatenate(
        [
            extended,
            spread_y(jnp.take(extended, send_y[1], axis=1), 1),
            spread_y(jnp.take(extended, send_y[0], axis=1), -1),
        ],
        axis=1,
    )


def ghost_return(table_grads, send_x, send_y, atom_count):
    ghost_x = send_x.shape[1]
    ghost_y = send_y.shape[1]
    ext_count = atom_count + 2 * ghost_x
    extended = table_grads[:, :ext_count]
    from_lower = table_grads[:, ext_count : ext_count + ghost_y]
    from_upper = table_grads[:, ext_count + ghost_y :]
    extended = extended.at[:, send_y[1]].add(spread_y(from_lower, -1))
    extended = extended.at[:, send_y[0]].add(spread_y(from_upper, 1))
    own_rows = extended[:, :atom_count]
    own_rows = own_rows.at[:, send_x[1]].add(
        spread_x(extended[:, atom_count : atom_count + ghost_x], -1)
    )
    own_rows = own_rows.at[:, send_x[0]].add(spread_x(extended[:, atom_count + ghost_x :], 1))
    return own_rows


def body(
    positions,
    species,
    send_x,
    send_y,
    neighbours,
    live_slots,
    embedding,
    radial_in,
    radial_mid,
    radial_out,
    mixing,
    read_first,
    read_hidden,
    read_last,
    w_charge,
    spectral,
    wave_ids,
):
    atom_count = positions.shape[1]
    count_x = lax.axis_size("bx")
    count_y = lax.axis_size("by") * lax.axis_size("ka")
    box_x = count_x * WIDTH_X
    box_y = count_y * WIDTH_Y
    wave_count = wave_ids.shape[1]
    spectral_scale = 1.0 / math.sqrt(wave_count * atom_count * count_x * count_y)
    payload = jnp.concatenate([positions, species.astype(jnp.float32)[None]], 0)
    atom_table = ghost_table(payload, send_x, send_y)
    pos_table = atom_table[:3]
    species_ids = jnp.arange(embedding.shape[1], dtype=jnp.float32)
    onehot = (atom_table[3][None, :] == species_ids[:, None]).astype(jnp.bfloat16)
    h_zero = jnp.dot(embedding, onehot, preferred_element_type=jnp.float32)

    def first_layer(pos_rows):
        return interaction(
            radial_in[0],
            radial_mid[0],
            radial_out[0],
            mixing[0],
            pos_rows,
            h_zero,
            neighbours,
            live_slots,
            box_x,
            box_y,
        )

    h_one, pull_first = jax.vjp(first_layer, pos_table)
    feat_table = ghost_table(h_one, send_x, send_y)

    def second_layer(pos_rows, feat_rows):
        h_two = interaction(
            radial_in[1],
            radial_mid[1],
            radial_out[1],
            mixing[1],
            pos_rows,
            feat_rows,
            neighbours,
            live_slots,
            box_x,
            box_y,
        )
        return readout(
            feat_rows[:, :atom_count], h_two, read_first, read_hidden, read_last, w_charge
        )

    (site_local, charge), pull_second = jax.vjp(second_layer, pos_table, feat_table)
    half_count = wave_count // 2
    offset = lax.axis_index("ka") * half_count
    wave_half = lax.dynamic_slice_in_dim(wave_ids, offset, half_count, 1)
    filter_half = lax.dynamic_slice_in_dim(spectral, offset, half_count, 1) * spectral_scale
    own_rows = jnp.concatenate([positions, charge], 0)
    brick_rows = jnp.concatenate([own_rows, swap_partner(own_rows)], 1)

    def brick_factor(brick_pos, brick_charge):
        return structure(brick_pos, brick_charge, wave_half, box_x, box_y)

    factor_parts, pull_ewald = jax.vjp(brick_factor, brick_rows[:3], brick_rows[3:])
    cosine_sum, sine_sum = lax.psum(factor_parts, ("bx", "by"))
    grad_pos, grad_charge = pull_ewald((filter_half * cosine_sum, filter_half * sine_sum))
    partner_grads = jnp.concatenate([grad_pos[:, atom_count:], grad_charge[:, atom_count:]], 0)
    returned = swap_partner(partner_grads)
    ewald_pos = grad_pos[:, :atom_count] + returned[:3]
    potential = grad_charge[:, :atom_count] + returned[3:]
    grad_pos_two, grad_feat = pull_second((jnp.ones_like(site_local), potential))
    feat_grads = ghost_return(grad_feat, send_x, send_y, atom_count)
    (grad_pos_one,) = pull_first(feat_grads)
    pos_grads = ghost_return(grad_pos_one + grad_pos_two, send_x, send_y, atom_count) + ewald_pos
    energies = site_local + 0.5 * jnp.sum(charge * potential, 0)
    return (energies, -pos_grads)


def solution(mesh):
    placed = (
        P(None, ("bx", "by", "ka")),
        P(("bx", "by", "ka")),
        P(None, ("bx", "by", "ka")),
        P(None, ("bx", "by", "ka")),
        P(None, ("bx", "by", "ka")),
        P(None, ("bx", "by", "ka")),
        P(),
        P(),
        P(),
        P(),
        P(),
        P(),
        P(),
        P(),
        P(),
        P(),
        P(),
    )
    return jax.shard_map(
        body,
        mesh=mesh,
        in_specs=placed,
        out_specs=(P(("bx", "by", "ka")), P(None, ("bx", "by", "ka"))),
        check_vma=False,
    )
```

profile of v0, /device:TPU:1, one launch (start us, length us, event | category | flops | bytes accessed | tf_op | source)
XLA Modules:
  0.0 1491.4 jit_solution(15484185230742582929)
XLA Ops:
  20.9 8.1 collective-permute-start.3
  30.0 6.2 collective-permute-done.2
  36.6 8.1 gather_fusion.6
  50.1 8.1 gather_fusion
  62.1 8.1 reshape.465
  73.9 8.0 reshape.466
  81.9 11.6 copy_multiply_fusion
  106.3 4.9 collective-permute-start.4
  119.0 5.5 collective-permute-done.6
  124.5 8.1 gather_fusion.1
  157.8 1092.9 %all-reduce.28.cloned.1.call-done = (f32[64,512]{1,0:T(8,128)}, f32[64,512]{1,0:T(8,128)}) async-done(((f32[64,512]{1,0:T(8,128)}, f32[64,512]{1,0:T(8,128)}), (f32[64,512]{1,0:T(8,128)}, f32[64,512]{1,0:T(8,128)})) %all-reduce.28.cloned.1.call-update) | async-done | bytes 262160 | tf_op jit(solution)/shard_map/psum | solution.py:258
  1268.2 5.7 fusion.109
  1276.7 7.9 fusion.60
  1286.0 17.3 %scatter_fusion = f32[128,288]{0,1:T(8,128)S(1)} fusion(f32[128,288]{0,1:T(8,128)S(1)} %convert_add_fusion, s32[3072]{0:T(1024)S(1)} %fusion.293, f32[3072,128]{1,0:T(8,128)} %bitcast.678), kind=kCustom, calls=%fused_computation.11 | custom fusion | flops 393216 | bytes 4730880 | tf_op jit(solution)/shard_map/transpose(jvp(jit(_take)))/scatter-add | solution.py:93
  1304.5 38.1 %collective-permute-start.10 = (f32[128,48]{0,1:T(8,128)S(1)}, f32[128,48]{0,1:T(8,128)S(1)}, u32[]{:S(2)}, u32[]{:S(2)}) collective-permute-start(f32[128,48]{0,1:T(8,128)S(1)} %get-tuple-element.54), channel_id=1, source_target_pairs={{0,63},{1,0},{2,1},{3,2},{4,3},{5,4},{6,5},{7,6},{8,7},{9,8},{10,9... | collective-permute-start | bytes 73736 | tf_op jit(solution)/shard_map/ppermute | solution.py:20
  1342.6 7.6 multiply_reduce_fusion
  1350.2 5.5 fusion.107
  1363.3 5.8 collective-permute-start.13
  1377.5 5.9 fusion.115
  1387.2 5.6 fusion.111
  1396.8 6.6 fusion.52
  1429.4 17.2 %scatter_fusion.2 = f32[3,288]{0,1:T(8,128)S(1)} fusion(f32[3,288]{0,1:T(8,128)S(1)} %pad.103.clone, s32[3072]{0:T(1024)S(1)} %fusion.293, f32[3072,3]{1,0:T(8,128)S(1)} %bitcast.683), kind=kCustom, calls=%fused_computation.17 | custom fusion | flops 9216 | bytes 122880 | tf_op jit(solution)/shard_map/transpose(jvp(jit(_take)))/scatter-add | solution.py:36
  1446.6 17.0 %scatter_fusion.1 = f32[3,288]{0,1:T(8,128)S(1)} fusion(f32[3,288]{0,1:T(8,128)S(1)} %pad.93.clone, s32[3072]{0:T(1024)S(1)} %fusion.293, f32[3072,3]{1,0:T(8,128)S(1)} %bitcast.684), kind=kCustom, calls=%fused_computation.16 | custom fusion | flops 9216 | bytes 122880 | tf_op jit(solution)/shard_map/transpose(jvp(jit(_take)))/scatter-add | solution.py:36
  1463.7 5.7 collective-permute-start.14
  (389 shorter events, 159.8 us)
Async XLA Ops:
  7.2 1243.4 %all-reduce.28.cloned.1.call-start = ((), (), s32[]{:S(2)}) async-start(), calls=%async_computation | async-start | bytes 524288 | tf_op jit(solution)/shard_map/psum | solution.py:258
  10.2 9.1 collective-permute-start
  15.0 4.7 collective-permute-start.1
  20.9 9.0 collective-permute-start.3
  29.1 7.1 collective-permute-start.2
  106.3 5.8 collective-permute-start.4
  111.2 4.7 collective-permute-start.5
  117.5 7.0 collective-permute-start.7
  117.5 7.0 collective-permute-start.6
  145.5 3.1 collective-permute-start.8
  148.6 1105.4 %copy-start.79 = (f32[1,256]{1,0:T(1,128)}, f32[1,256]{1,0:T(1,128)S(1)}, u32[]{:S(2)}) copy-start(f32[1,256]{1,0:T(1,128)S(1)} %get-tuple-element.59) | copy-start | bytes 3076
  148.6 1105.4 %copy-start.80 = (f32[1,256]{1,0:T(1,128)}, f32[1,256]{1,0:T(1,128)S(1)}, u32[]{:S(2)}) copy-start(f32[1,256]{1,0:T(1,128)S(1)} %get-tuple-element.60) | copy-start | bytes 3076
  148.6 1105.4 %copy-start.81 = (f32[1,256]{1,0:T(1,128)}, f32[1,256]{1,0:T(1,128)S(1)}, u32[]{:S(2)}) copy-start(f32[1,256]{1,0:T(1,128)S(1)} %get-tuple-element.61) | copy-start | bytes 3076
  148.6 1105.3 %copy-start.72 = (f32[1,512]{1,0:T(1,128)S(1)}, f32[1,512]{1,0:T(1,128)}, u32[]{:S(2)}) copy-start(f32[1,512]{1,0:T(1,128)} %get-tuple-element.77) | copy-start | bytes 6148
  148.6 1105.3 %copy-start.74 = (f32[1,512]{1,0:T(1,128)S(1)}, f32[1,512]{1,0:T(1,128)}, u32[]{:S(2)}) copy-start(f32[1,512]{1,0:T(1,128)} %get-tuple-element.78) | copy-start | bytes 6148
  1264.7 3.1 collective-permute-start.9
  1303.3 56.2 %collective-permute-start.11 = (f32[128,48]{0,1:T(8,128)S(1)}, f32[128,48]{0,1:T(8,128)}, u32[]{:S(2)}, u32[]{:S(2)}) collective-permute-start(f32[128,48]{0,1:T(8,128)S(1)} %get-tuple-element.53), channel_id=1, source_target_pairs={{0,1},{1,2},{2,3},{3,4},{4,5},{5,6},{6,7},{7,8},{8,9},{9,10},{10,1... | collective-permute-start | bytes 73736 | tf_op jit(solution)/shard_map/ppermute | solution.py:20
  1304.5 51.8 %collective-permute-start.10 = (f32[128,48]{0,1:T(8,128)S(1)}, f32[128,48]{0,1:T(8,128)S(1)}, u32[]{:S(2)}, u32[]{:S(2)}) collective-permute-start(f32[128,48]{0,1:T(8,128)S(1)} %get-tuple-element.54), channel_id=1, source_target_pairs={{0,63},{1,0},{2,1},{3,2},{4,3},{5,4},{6,5},{7,6},{8,7},{9,8},{10,9... | collective-permute-start | bytes 73736 | tf_op jit(solution)/shard_map/ppermute | solution.py:20
  1363.3 12.0 collective-permute-start.13
  1369.1 5.3 collective-permute-start.12
  1463.6 7.7 collective-permute-start.15
  1463.7 6.6 collective-permute-start.14
  1472.5 10.0 collective-permute-start.17
  1476.9 4.7 collective-permute-start.16
  (92 other events, 3330.5 us)
Sparse Core Ops, SparseCore 0:
  155.3 1095.2 all-reduce.27
where the time goes:
time: 1500 us; the launch traced here: 1490 us
  waiting for transfers between devices  1120 us (75%)
  other arithmetic  112 us (7%)
  matrix products  103 us (7%)
  starting transfers between devices  75.9 us (5%)
  local copies, waits for them, and re-layouts  67.3 us (4%)
  between operations  16.1 us (1%)
    psum x1, waiting for transfers between devices, body(): cosine_sum, sine_sum = lax.psum(factor_parts, ('bx', 'by'))  1090 us
    ppermute x16, starting transfers between devices, from_behind(): lax.ppermute(array, axis, [(i, (i + by) % count) for i in range(count)])  74.2 us
    scatter-add x2, other arithmetic, edge_geometry(): others = jnp.take(pos_table, neighbours, axis=1)  34.2 us
    dot_general x6, matrix products, interaction(): jnp.einsum('cni,cni,mni->mci', radial[1], source, harmonics[1:4], precisi...  31.6 us
  transfers between devices with their start and end apart: 19, of which 11 were waited for; matrix products, arithmetic and copies ran while one was open for 2% of the time, Pallas kernels for 0%

commit v1 on v0

v1 whole, which is shorter than its diff:
```python
import functools
import math

import jax
import jax.numpy as jnp
from jax import lax
from jax.experimental import pallas as pl
from jax.experimental.pallas import tpu as pltpu
from jax.sharding import Mesh, PartitionSpec as P

CUTOFF = 4.0
SOFTEN = 0.25
WIDTH_X = 16.0
WIDTH_Y = 16.0
DEPTH_Z = 16.0
ACT_GAIN = 1.679
ROOT_THREE = math.sqrt(3.0)
HIGHEST = lax.Precision.HIGHEST
F32 = jnp.float32
BF16 = jnp.bfloat16

C = 128
NB = 24
ATOMS = 128
EDGES = NB * ATOMS
TABLE = 384
NBASIS = 8
K = 1024
KC = 64
TILES = 2 * K // 128
AXES = ("xh", "co", "y", "z", "xl")
WIDE = ("xh", "co", "y", "xl")
NWIDE = 32

NN = (((1,), (0,)), ((), ()))
NT = (((1,), (1,)), ((), ()))
TN = (((0,), (0,)), ((), ()))


def dot(a, b, dims=NN, precision=None):
    return lax.dot_general(a, b, dims, precision=precision, preferred_element_type=F32)


def split(a):
    high = a.astype(BF16)
    return high, (a - high.astype(F32)).astype(BF16)


def dot3(a, b, dims=NN):
    a_hi, a_lo = split(a)
    b_hi, b_lo = split(b)
    return dot(a_hi, b_hi, dims) + (dot(a_lo, b_hi, dims) + dot(a_hi, b_lo, dims))


def gate(v):
    s = 0.5 + 0.5 * jnp.tanh(0.5 * v)
    return s, (ACT_GAIN * v) * s


def gate_slope(v, s):
    return ACT_GAIN * s * (1.0 + v * (1.0 - s))


def onehot_columns(index_row, count, dtype):
    rows = lax.broadcasted_iota(jnp.int32, (count, index_row.shape[1]), 0)
    return (rows == index_row).astype(F32).astype(dtype)


def merge(a, b, split_lane):
    lane = lax.broadcasted_iota(jnp.int32, a.shape, 1)
    return jnp.where(lane < split_lane, a, b)


def pick(values, index_row):
    return dot(values, onehot_columns(index_row, values.shape[1], F32), NN, HIGHEST)


def give_back(grads, index_row, count):
    return dot(grads, onehot_columns(index_row, count, F32), NT, HIGHEST)


def strip_x_kernel(rows_ref, ix_ref, out_ref):
    out_ref[...] = pick(rows_ref[...], ix_ref[...])


def strip_y_kernel(rows_ref, a_ref, b_ref, iy_ref, part_ref, out_ref):
    part = merge(a_ref[...], b_ref[...], 32)
    part_ref[...] = part
    out_ref[...] = pick(jnp.concatenate([rows_ref[...], part], 1), iy_ref[...])


def radial_tile(g, geo_ref, w1, w2, w3, r_ref, p_ref):
    spacing = CUTOFF / (NBASIS - 1)
    centre = lax.broadcasted_iota(jnp.int32, (NBASIS, 512), 0).astype(F32) * spacing

    def row(k):
        return jnp.concatenate([geo_ref[k, pl.ds(4 * g + j, 1), :] for j in range(4)], 1)

    d = row(3)
    gap = (d - centre) * (1.0 / spacing)
    basis = jnp.exp(-gap * gap)
    z1 = dot(w1, basis.astype(BF16))
    s1, h1 = gate(z1)
    z2 = dot(w2, h1.astype(BF16))
    s2, h2 = gate(z2)
    env = row(4)
    cols = pl.ds(pl.multiple_of(g * 512, 512), 512)
    r_ref[:, cols] = dot(w3, (h2 * env).astype(BF16)).astype(BF16)
    slope = basis * gap * (-2.0 / spacing)
    h1p = gate_slope(z1, s1) * dot(w1, slope.astype(BF16))
    h2p = gate_slope(z2, s2) * dot(w2, h1p.astype(BF16))
    p_ref[:, cols] = dot(w3, (h2p * row(6) + h2 * row(5)).astype(BF16)).astype(BF16)


def aggregate(r_ref, get_f, y_ref, a_ref):
    def body(cc, carry):
        r0 = pl.multiple_of(cc * 16, 16)
        acc = [jnp.zeros((16, 128), F32) for _ in range(9)]
        state = get_f(r0)
        for n in range(NB):
            cols = slice(n * 128, (n + 1) * 128)
            f = state(n)
            g0 = r_ref[pl.ds(r0, 16), cols].astype(F32) * f
            g1 = r_ref[pl.ds(128 + r0, 16), cols].astype(F32) * f
            g2 = r_ref[pl.ds(256 + r0, 16), cols].astype(F32) * f
            acc[0] = acc[0] + g0
            for m in range(3):
                acc[1 + m] = acc[1 + m] + g1 * y_ref[m, n : n + 1, :]
            for m in range(5):
                acc[4 + m] = acc[4 + m] + g2 * y_ref[3 + m, n : n + 1, :]
        for k in range(9):
            a_ref[k, pl.ds(r0, 16), :] = acc[k]
        return carry

    lax.fori_loop(0, 8, body, 0)


def invariants(a_ref):
    a1 = a_ref[1] * a_ref[1] + a_ref[2] * a_ref[2] + a_ref[3] * a_ref[3]
    a2 = a_ref[4] * a_ref[4] + a_ref[5] * a_ref[5] + a_ref[6] * a_ref[6]
    a2 = a2 + a_ref[7] * a_ref[7] + a_ref[8] * a_ref[8]
    return jnp.concatenate([a_ref[0].astype(BF16), a1.astype(BF16), a2.astype(BF16)], 0)


def take_lanes(tables, lane, group):
    got = [jnp.take_along_axis(t, lane, axis=1, mode="promise_in_bounds") for t in tables]
    return jnp.where(group == 0, got[0], jnp.where(group == 1, got[1], got[2]))


def first_kernel(
    box_x, box_y, rows_ref, part_ref, a_in, b_in, nb_ref, live_ref, ix_ref, emb_ref, w1_ref, w2_ref,
    w3_ref, mix_ref, geo_ref, y_ref, r_ref, p_ref, f_ref, a_ref, h_ref, strip_ref,
):
    own = rows_ref[...]
    tables = [own, part_ref[...], merge(a_in[...], b_in[...], 64)]
    nb = nb_ref[...]
    lane, group = nb & 127, nb >> 7

    def gathered(row):
        return jnp.concatenate(
            [
                take_lanes(
                    [jnp.broadcast_to(t[row : row + 1], (8, 128)) for t in tables],
                    lane[8 * b : 8 * b + 8],
                    group[8 * b : 8 * b + 8],
                )
                for b in range(NB // 8)
            ],
            0,
        )

    off_x = gathered(0) - own[0:1]
    off_y = gathered(1) - own[1:2]
    step_z = gathered(2) - own[2:3]
    step_x = off_x - box_x * jnp.floor(off_x * (1.0 / box_x) + 0.5)
    step_y = off_y - box_y * jnp.floor(off_y * (1.0 / box_y) + 0.5)
    square = step_x * step_x + step_y * step_y + step_z * step_z
    shifted = square + SOFTEN
    inverse = lax.rsqrt(shifted)
    live = live_ref[...].astype(F32)
    inside = jnp.maximum(1.0 - square * (1.0 / (CUTOFF * CUTOFF)), 0.0)
    env = inside * inside * live
    ux, uy, uz = step_x * (1.0 / CUTOFF), step_y * (1.0 / CUTOFF), step_z * (1.0 / CUTOFF)
    geo_ref[0] = ux
    geo_ref[1] = uy
    geo_ref[2] = uz
    geo_ref[3] = jnp.sqrt(shifted)
    geo_ref[4] = env
    geo_ref[5] = inside * live * (-2.0 / (CUTOFF * CUTOFF))
    geo_ref[6] = 0.5 * env * inverse
    y_ref[0] = ux
    y_ref[1] = uy
    y_ref[2] = uz
    y_ref[3] = ux * uy
    y_ref[4] = uy * uz
    y_ref[5] = uz * ux
    y_ref[6] = ux * ux - uy * uy
    y_ref[7] = (2.0 * uz * uz - ux * ux - uy * uy) * (1.0 / ROOT_THREE)

    species = gathered(3)
    emb = emb_ref[...]
    w1, w2, w3 = w1_ref[0], w2_ref[0], w3_ref[0]
    geo_ref[7] = species

    def tile(g, carry):
        radial_tile(g, geo_ref, w1, w2, w3, r_ref, p_ref)
        kinds = lax.broadcasted_iota(jnp.int32, (8, 512), 0).astype(F32)
        kind = jnp.concatenate([geo_ref[7, pl.ds(4 * g + j, 1), :] for j in range(4)], 1)
        cols = pl.ds(pl.multiple_of(g * 512, 512), 512)
        f_ref[:, cols] = dot(emb, (kinds == kind).astype(F32).astype(BF16)).astype(BF16)
        return carry

    lax.fori_loop(0, NB // 4, tile, 0)

    def get_f(r0):
        return lambda n: f_ref[pl.ds(r0, 16), n * 128 : (n + 1) * 128].astype(F32)

    aggregate(r_ref, get_f, y_ref, a_ref)
    kinds = lax.broadcasted_iota(jnp.int32, (8, 128), 0).astype(F32)
    h_zero = dot(emb, (kinds == own[3:4]).astype(F32).astype(BF16))
    h_one = h_zero + dot(mix_ref[0], invariants(a_ref))
    h_ref[...] = h_one
    strip_ref[...] = pick(h_one, ix_ref[...])


def radial_kernel(geo_ref, w1_ref, w2_ref, w3_ref, r_ref, p_ref):
    w1, w2, w3 = w1_ref[1], w2_ref[1], w3_ref[1]

    def tile(g, carry):
        radial_tile(g, geo_ref, w1, w2, w3, r_ref, p_ref)
        return carry

    lax.fori_loop(0, NB // 4, tile, 0)


def waves_kernel(box_x, box_y, rows_ref, wave_ref, cs_ref):
    own = rows_ref[...]
    x, y, z = own[0:1] * (1.0 / box_x), own[1:2] * (1.0 / box_y), own[2:3] * (1.0 / DEPTH_Z)
    x, y, z = x - jnp.floor(x), y - jnp.floor(y), z - jnp.floor(z)
    turns = jnp.concatenate([x, y, z, jnp.zeros((5, 128), F32)], 0)

    def tile(t, carry):
        cols = pl.ds(pl.multiple_of(t * 128, 128), 128)
        phase = dot(turns, wave_ref[:, cols], TN, HIGHEST)
        quarter = jnp.floor(4.0 * phase + 0.5)
        angle = (phase - 0.25 * quarter) * (2.0 * math.pi)
        sq = angle * angle
        sin = angle * (1.0 + sq * (-1.0 / 6 + sq * (1.0 / 120 + sq * (-1.0 / 5040 + sq * (1.0 / 362880)))))
        cos = 1.0 + sq * (-0.5 + sq * (1.0 / 24 + sq * (-1.0 / 720 + sq * (1.0 / 40320 - sq * (1.0 / 3628800)))))
        turn = quarter.astype(jnp.int32) & 3
        odd = (turn & 1) == 1
        c = jnp.where(odd, sin, cos)
        s = jnp.where(odd, cos, sin)
        c = jnp.where((turn == 1) | (turn == 2), -c, c)
        s = jnp.where(turn >= 2, -s, s)
        cs_ref[:, cols] = c
        cs_ref[:, pl.ds(pl.multiple_of(K + t * 128, 128), 128)] = s
        return carry

    lax.fori_loop(0, K // 128, tile, 0)


def feature_strip_kernel(h_ref, a_in, b_in, iy_ref, part_ref, out_ref):
    part = merge(a_in[...], b_in[...], 32)
    part_ref[...] = part
    out_ref[...] = pick(jnp.concatenate([h_ref[...], part], 1), iy_ref[...])


def second_kernel(
    h_ref, part_ref, a_in, b_in, nb_ref, y_ref, r_ref, cs_ref, mix_ref, read_hidden_ref,
    w_charge_ref, f_ref, a_ref, h2_ref, charge_ref, s_ref, ypart_ref,
):
    ypart_ref[...] = merge(a_in[...], b_in[...], 64)

    def get_f(r0):
        rows = pl.ds(r0, 16)
        tables = [h_ref[rows, :], part_ref[rows, :], ypart_ref[rows, :]]

        def state(n):
            nb = jnp.broadcast_to(nb_ref[n : n + 1, :], (16, 128))
            f = take_lanes(tables, nb & 127, nb >> 7)
            f_ref[rows, n * 128 : (n + 1) * 128] = f
            return f

        return state

    aggregate(r_ref, get_f, y_ref, a_ref)
    h_two = h_ref[...] + dot(mix_ref[1], invariants(a_ref))
    h2_ref[...] = h_two
    charge = dot(w_charge_ref[...], h_two.astype(BF16))
    charge_ref[...] = charge
    q_hi, q_lo = split(charge)
    q_both = jnp.concatenate([q_hi, q_lo], 0)
    for t in range(TILES // 2):
        c_hi, c_lo = split(cs_ref[:, t * 256 : (t + 1) * 256])
        both = dot(q_both, c_hi)
        part = both[:KC] + (both[KC:] + dot(q_hi, c_lo))
        s_ref[2 * t * KC : (2 * t + 1) * KC, :] = part[:, :128]
        s_ref[(2 * t + 1) * KC : (2 * t + 2) * KC, :] = part[:, 128:]


def backward(ga_ref, r_ref, p_ref, f_ref, y_ref, gf_ref, t_ref):
    def body(n, carry):
        cols = pl.ds(pl.multiple_of(n * 128, 128), 128)
        y = [y_ref[m, pl.ds(n, 1), :] for m in range(8)]
        acc = [jnp.zeros((16, 128), F32) for _ in range(9)]
        for cc in range(8):
            rows = slice(cc * 16, cc * 16 + 16)
            ga = [ga_ref[k, rows, :] for k in range(9)]
            f = f_ref[rows, cols].astype(F32)
            r = [r_ref[l * 128 + cc * 16 : l * 128 + cc * 16 + 16, cols].astype(F32) for l in range(3)]
            p = [p_ref[l * 128 + cc * 16 : l * 128 + cc * 16 + 16, cols].astype(F32) for l in range(3)]
            q1 = ga[1] * y[0] + ga[2] * y[1] + ga[3] * y[2]
            q2 = ga[4] * y[3] + ga[5] * y[4] + ga[6] * y[5] + ga[7] * y[6] + ga[8] * y[7]
            if gf_ref is not None:
                gf_ref[rows, cols] = (ga[0] * r[0] + q1 * r[1] + q2 * r[2]).astype(BF16)
            acc[0] = acc[0] + f * (ga[0] * p[0] + q1 * p[1] + q2 * p[2])
            g1, g2 = f * r[1], f * r[2]
            for m in range(3):
                acc[1 + m] = acc[1 + m] + g1 * ga[1 + m]
            for m in range(5):
                acc[4 + m] = acc[4 + m] + g2 * ga[4 + m]
        for k in range(9):
            t_ref[k, pl.ds(n, 1), :] = jnp.sum(acc[k], 0, keepdims=True)
        return carry

    lax.fori_loop(0, NB, body, 0)


def pull_invariants(g_inv, a_ref, ga_ref):
    ga_ref[0] = g_inv[:C]
    for k in range(1, 4):
        ga_ref[k] = 2.0 * a_ref[k] * g_inv[C : 2 * C]
    for k in range(4, 9):
        ga_ref[k] = 2.0 * a_ref[k] * g_inv[2 * C :]


def fill_onehot(nb_ref, oh_ref):
    for n in range(NB):
        oh_ref[:, n * 128 : (n + 1) * 128] = onehot_columns(nb_ref[n : n + 1, :], TABLE, BF16)


def ewald_kernel(
    box_x, box_y, scale, s_ref, spectral_ref, cs_ref, wave_ref, charge_ref, h_ref, h2_ref, a_ref, y_ref, r_ref, p_ref,
    f_ref, nb_ref, iy_ref, mix_ref, read_first_ref, read_hidden_ref, read_last_ref, w_charge_ref,
    energy_ref, gpos_ref, gown_ref, gpart_ref, gy_ref, t_ref, ga_ref, gf_ref, oh_ref,
):
    charge = charge_ref[...]
    q_t = charge.T
    qt_hi, qt_lo = split(q_t)
    potential = jnp.zeros((KC, ATOMS), F32)
    gpos = jnp.zeros((8, ATOMS), F32)
    for t in range(TILES // 2):
        cols = slice(t * 128, (t + 1) * 128)
        late = slice(K + t * 128, K + (t + 1) * 128)
        filt = spectral_ref[:, cols] * scale
        gc = filt * s_ref[t * KC : (t + 1) * KC, :]
        gs = filt * s_ref[(TILES // 2 + t) * KC : (TILES // 2 + t + 1) * KC, :]
        cos, sin = cs_ref[:, cols], cs_ref[:, late]
        potential = potential + dot3(gc, cos, NT) + dot3(gs, sin, NT)
        gphase = dot3(q_t, gs) * cos - dot3(q_t, gc) * sin
        gpos = gpos + dot3(wave_ref[:, cols], gphase, NT)
    gpos_ref[...] = jnp.concatenate(
        [
            gpos[0:1] * (2.0 * math.pi / box_x),
            gpos[1:2] * (2.0 * math.pi / box_y),
            gpos[2:3] * (2.0 * math.pi / DEPTH_Z),
            jnp.zeros((5, ATOMS), F32),
        ],
        0,
    )
    h_two = h2_ref[...].astype(BF16)
    z = dot(read_hidden_ref[...], h_two)
    s, hidden = gate(z)
    last = read_last_ref[...]
    site = jnp.sum(read_first_ref[...] * h_ref[...], 0, keepdims=True) + jnp.sum(last * hidden, 0, keepdims=True)
    energy_ref[...] = site + 0.5 * jnp.sum(charge * potential, 0, keepdims=True)
    g_hidden = (last * gate_slope(z, s)).astype(BF16)
    g_two = dot(w_charge_ref[...], potential.astype(BF16), TN) + dot(read_hidden_ref[...], g_hidden, TN)
    g_two = g_two.astype(BF16)
    g_inv = dot(mix_ref[1], g_two, TN).astype(BF16).astype(F32)
    pull_invariants(g_inv, a_ref, ga_ref)
    backward(ga_ref, r_ref, p_ref, f_ref, y_ref, gf_ref, t_ref)
    fill_onehot(nb_ref, oh_ref)
    grads = dot(gf_ref[...], oh_ref[...], NT)
    gown_ref[...] = grads[:, :128] + g_two.astype(F32) + read_first_ref[...]
    gpart_ref[...] = grads[:, 128:256]
    gy_ref[...] = grads[:, 256:]


def return_y_kernel(gown_ref, gpart_ref, a_in, b_in, iy_ref, own_ref, part_ref):
    back = give_back(merge(a_in[...], b_in[...], 64), iy_ref[...], 256)
    own_ref[...] = gown_ref[...] + back[:, :128]
    part_ref[...] = gpart_ref[...] + back[:, 128:]


def last_kernel(
    gown_ref, a_in, b_in, ix_ref, mix_ref, a_ref, r_ref, p_ref, f_ref, y_ref, t1_ref, geo_ref, nb_ref, gpos_ref,
    own_ref, part_ref, gy_ref, ga_ref, t_ref, oh_ref, rows_ref,
):
    g_one = gown_ref[...] + give_back(merge(a_in[...], b_in[...], 32), ix_ref[...], 128)
    g_inv = dot(mix_ref[0], g_one.astype(BF16), TN).astype(BF16).astype(F32)
    pull_invariants(g_inv, a_ref, ga_ref)
    backward(ga_ref, r_ref, p_ref, f_ref, y_ref, None, t_ref)
    t = [t_ref[k] + t1_ref[k] for k in range(9)]
    ux, uy, uz = geo_ref[0], geo_ref[1], geo_ref[2]
    root = 2.0 / ROOT_THREE
    gx = t[1] + t[4] * uy + t[6] * uz + ux * (2.0 * t[7] - root * t[8])
    gy = t[2] + t[4] * ux + t[5] * uz - uy * (2.0 * t[7] + root * t[8])
    gz = t[3] + t[5] * uy + t[6] * ux + (2.0 * root) * uz * t[8]
    steps = [g * (1.0 / CUTOFF) + (2.0 * CUTOFF) * u * t[0] for g, u in ((gx, ux), (gy, uy), (gz, uz))]
    rows_ref[...] = jnp.zeros(rows_ref.shape, F32)
    for k in range(3):
        high = steps[k].astype(BF16).astype(F32)
        low = steps[k] - high
        for n in range(NB):
            rows_ref[k : k + 1, n * 128 : (n + 1) * 128] = high[n : n + 1]
            rows_ref[8 + k : 9 + k, n * 128 : (n + 1) * 128] = low[n : n + 1]
    fill_onehot(nb_ref, oh_ref)
    both = dot(rows_ref[...].astype(BF16), oh_ref[...], NT)
    grads = both[:8] + both[8:]
    centre = jnp.concatenate([jnp.sum(g, 0, keepdims=True) for g in steps] + [jnp.zeros((5, 128), F32)], 0)
    own_ref[...] = grads[:, :128] - centre + gpos_ref[...]
    part_ref[...] = grads[:, 128:256]
    gy_ref[...] = grads[:, 256:]


def final_kernel(own_ref, a_in, b_in, ix_ref, out_ref):
    total = own_ref[...] + give_back(merge(a_in[...], b_in[...], 32), ix_ref[...], 128)
    out_ref[...] = -total[:3]


def sum_kernel(in_ref, out_ref):
    rows = out_ref.shape[0]
    total = in_ref[0:rows, :]
    for g in range(1, in_ref.shape[0] // rows):
        total = total + in_ref[g * rows : (g + 1) * rows, :]
    out_ref[...] = total


def call(kernel, outs, *operands, scratch=(), flops=0, moved=0):
    return pl.pallas_call(
        kernel,
        out_shape=[jax.ShapeDtypeStruct(s, d) for s, d in outs],
        scratch_shapes=[pltpu.VMEM(s, d) for s, d in scratch],
        compiler_params=pltpu.CompilerParams(vmem_limit_bytes=48 * 1024 * 1024),
        cost_estimate=pl.CostEstimate(flops=flops, bytes_accessed=moved, transcendentals=0),
    )(*operands)


def swap(value, axes, of):
    count = 1
    for axis in axes:
        count *= lax.axis_size(axis)
    return lax.ppermute(value, axes, [(i, of(i)) for i in range(count)])


BX = ("xh", "co")
CELL = ("y", "z", "xl")


def swap_x(rows):
    return swap(rows, BX, lambda i: i ^ 1), swap(rows, BX, lambda i: i ^ 3)


def swap_y(rows):
    def other(c):
        return (c - 1) % 64 if c % 2 == 0 else (c + 1) % 64

    return swap(rows, CELL, lambda c: c ^ 1), swap(rows, CELL, other)


def reduce_all(partial):
    rows = partial.shape[0] // NWIDE
    pieces = lax.all_to_all(partial, WIDE, 0, 0, tiled=True)
    (mine,) = call(sum_kernel, [((rows, 128), F32)], pieces)
    for mask in (1, 2, 4):
        mine = mine + swap(mine, ("z",), lambda i, mask=mask: i ^ mask)
    spread = jnp.broadcast_to(mine[None], (NWIDE, rows, 128)).reshape(NWIDE * rows, 128)
    return lax.all_to_all(spread, WIDE, 0, 0, tiled=True)


def body(
    positions, species, send_x, send_y, neighbours, live_slots, embedding, radial_in, radial_mid, radial_out, mixing,
    read_first, read_hidden, read_last, w_charge, spectral, wave_ids,
):
    count_x = lax.axis_size("xh") * lax.axis_size("co")
    count_y = lax.axis_size("y") * lax.axis_size("z") * lax.axis_size("xl")
    box_x = count_x * WIDTH_X
    box_y = count_y * WIDTH_Y
    scale = 1.0 / math.sqrt(K * ATOMS * count_x * count_y)
    px = lax.axis_index("co")
    py = lax.axis_index("xl")
    lower_x, upper_x = 160 - 32 * px, 128 + 32 * px
    lower_y, upper_y = 320 - 64 * py, 256 + 64 * py

    def place(index):
        far = jnp.where(index < 240, index - 192 + lower_y, index - 240 + upper_y)
        near = jnp.where(index < 160, index - 128 + lower_x, index - 160 + upper_x)
        return jnp.where(index < 128, index, jnp.where(index < 192, near, far))

    nb = place(neighbours)
    odd_x, odd_y = px == 1, py == 1
    none = jnp.full((64,), -1, jnp.int32)
    ix = jnp.concatenate(
        [jnp.where(odd_x, send_x[0], send_x[1]), jnp.where(odd_x, send_x[1], send_x[0]), none]
    )[None]
    sy = place(send_y)
    iy = jnp.concatenate(
        [jnp.where(odd_y, sy[0], sy[1]), none[:16], jnp.where(odd_y, sy[1], sy[0]), none[:16]]
    )[None]
    rows = jnp.concatenate([positions, species.astype(F32)[None], jnp.zeros((4, ATOMS), F32)], 0)
    wave = jnp.concatenate([wave_ids.astype(F32), jnp.zeros((5, K), F32)], 0)
    emb = jnp.pad(embedding, ((0, 0), (0, 8 - embedding.shape[1])))
    small = ((8, 128), F32)
    square = ((C, 128), F32)
    edge3 = ((3 * C, EDGES), BF16)

    (strip,) = call(strip_x_kernel, [small], rows, ix)
    xa, xb = swap_x(strip)
    part, strip = call(strip_y_kernel, [small, small], rows, xa, xb, iy)
    ya, yb = swap_y(strip)
    (cs,) = call(
        functools.partial(waves_kernel, box_x, box_y), [((ATOMS, 2 * K), F32)], rows, wave, flops=10**8, moved=10**6
    )
    geo, ylm, r_zero, p_zero, f_zero, a_zero, h_one, strip = call(
        functools.partial(first_kernel, box_x, box_y),
        [((8, NB, 128), F32), ((8, NB, 128), F32), edge3, edge3, ((C, EDGES), BF16), ((9, C, 128), F32), square, square],
        rows, part, ya, yb, nb, live_slots, ix, emb, radial_in, radial_mid, radial_out, mixing,
    )
    xa, xb = swap_x(strip)
    r_one, p_one = call(radial_kernel, [edge3, edge3], geo, radial_in, radial_mid, radial_out, flops=10**9, moved=10**7)
    fpart, strip = call(feature_strip_kernel, [square, square], h_one, xa, xb, iy)
    ya, yb = swap_y(strip)
    f_one, a_one, h_two, charge, s_part = call(
        second_kernel,
        [((C, EDGES), F32), ((9, C, 128), F32), square, ((KC, ATOMS), F32), ((TILES * KC, 128), F32)],
        h_one, fpart, ya, yb, nb, ylm, r_one, cs, mixing, read_hidden, w_charge,
        scratch=[square],
    )
    s_all = reduce_all(s_part)
    energy, gpos, gown, gpart, gy, t_one = call(
        functools.partial(ewald_kernel, box_x, box_y, scale),
        [((1, 128), F32), small, square, square, square, ((9, NB, 128), F32)],
        s_all, spectral, cs, wave, charge, h_one, h_two, a_one, ylm, r_one, p_one, f_one, nb, iy, mixing,
        read_first[:, None], read_hidden, read_last[:, None], w_charge,
        scratch=[((9, C, 128), F32), ((C, EDGES), BF16), ((TABLE, EDGES), BF16)],
    )
    ya, yb = swap_y(gy)
    gown, gpart = call(return_y_kernel, [square, square], gown, gpart, ya, yb, iy)
    xa, xb = swap_x(gpart)
    own, part, gy = call(
        last_kernel,
        [small, small, small],
        gown, xa, xb, ix, mixing, a_zero, r_zero, p_zero, f_zero, ylm, t_one, geo, nb, gpos,
        scratch=[((9, C, 128), F32), ((9, NB, 128), F32), ((TABLE, EDGES), BF16), ((16, EDGES), F32)],
    )
    ya, yb = swap_y(gy)
    own, part = call(return_y_kernel, [small, small], own, part, ya, yb, iy)
    xa, xb = swap_x(part)
    (forces,) = call(final_kernel, [((3, ATOMS), F32)], own, xa, xb, ix)
    return energy[0], forces


def solution(mesh):
    fine = Mesh(mesh.devices.reshape(2, 2, 4, 8, 2), AXES)
    rows, columns = P(AXES), P(None, AXES)
    placed = (columns, rows) + (columns,) * 4 + (P(),) * 11
    return jax.shard_map(body, mesh=fine, in_specs=placed, out_specs=(rows, columns), check_vma=False)
```

time: 1500 us -> 164 us (0.11)
  waiting for transfers between devices: 1120 us -> 38.5 us
  other arithmetic: 112 us -> 4.46 us
  matrix products: 103 us -> 0 us
  local copies, waits for them, and re-layouts: 67.3 us -> 22.5 us
  Pallas kernels: 0 us -> 41.4 us
  starting transfers between devices: 75.9 us -> 39.5 us
  blocking collectives: 0 us -> 15.3 us
  between operations: 16.1 us -> 0.93 us
    psum x1 -> x0, waiting for transfers between devices: 1090 us -> none  [body(): cosine_sum, sine_sum = lax.psum(factor_parts, ('bx', 'by'))]
    dot_general x37 -> x0, matrix products: 103 us -> none  [the longest x6 31.6 us: interaction(): jnp.einsum('cni,cni,mni->mci', radial[1], source, harmonics[1:4], precisi...]
    scatter-add x11 -> x0, other arithmetic: 62.3 us -> none  [the longest x2 34.2 us: edge_geometry(): others = jnp.take(pos_table, neighbours, axis=1)]
    ppermute x18 -> x19, starting transfers between devices: 75.8 us -> 31.5 us  [swap(): return lax.ppermute(value, axes, [(i, of(i)) for i in range(count)])]
    pallas_call x0 -> x13, Pallas kernels: none -> 41.4 us  [call(): pl.pallas_call(kernel, out_shape=[jax.ShapeDtypeStruct(s, d) for s, d in...]
    gather x12 -> x0, local copies, waits for them, and re-layouts: 30 us -> none  [the longest x2 16.2 us: interaction(): source = jnp.take(feat_table, neighbours, axis=1)]
    unnamed x201 -> x63, local copies, waits for them, and re-layouts: 2.55 us -> 18.8 us
    reshape x2 -> x0, local copies, waits for them, and re-layouts: 16 us -> none  [interaction(): radial.reshape(3, channels, slot_count, atom_count) * envelope[None, None]]
  transfers between devices with their start and end apart: 19 -> 20, of which waited for: 11 -> 10; matrix products, arithmetic and copies ran while one was open for 2% -> 5% of each run, Pallas kernels for 0% -> 5%
where the time goes in v1:
time: 164 us; the launch traced here: 163 us
  Pallas kernels  41.4 us (25%)
  starting transfers between devices  39.5 us (24%)
  waiting for transfers between devices  38.5 us (23%)
  local copies, waits for them, and re-layouts  22.5 us (14%)
  blocking collectives  15.3 us (9%)
  other arithmetic  4.46 us (3%)
    pallas_call x13, Pallas kernels, call(): pl.pallas_call(kernel, out_shape=[jax.ShapeDtypeStruct(s, d) for s, d in...  41.4 us
    ppermute x19, starting transfers between devices, swap(): return lax.ppermute(value, axes, [(i, of(i)) for i in range(count)])  31.5 us
    ppermute x19, waiting for transfers between devices, swap(): return lax.ppermute(value, axes, [(i, of(i)) for i in range(count)])  30.1 us
    unnamed x63, local copies, waits for them, and re-layouts  18.8 us
    all_to_all x1, blocking collectives, reduce_all(): pieces = lax.all_to_all(partial, WIDE, 0, 0, tiled=True)  15.3 us
    all_to_all x1, waiting for transfers between devices, reduce_all(): return lax.all_to_all(spread, WIDE, 0, 0, tiled=True)  8.39 us
    all_to_all x1, starting transfers between devices, reduce_all(): return lax.all_to_all(spread, WIDE, 0, 0, tiled=True)  8.06 us
  transfers between devices with their start and end apart: 20, of which 10 were waited for; matrix products, arithmetic and copies ran while one was open for 5% of the time, Pallas kernels for 5%

profile of v1, /device:TPU:1, one launch (start us, length us, event | category | flops | bytes accessed | tf_op | source)
XLA Modules:
  0.0 162.7 jit_solution(8404573534054750863)
XLA Ops:
  3.1 3.3 %collective-permute-start = (f32[8,128]{1,0:T(8,128)S(1)}, f32[8,128]{1,0:T(8,128)S(1)}, u32[]{:S(2)}, u32[]{:S(2)}) collective-permute-start(f32[8,128]{1,0:T(8,128)S(1)} %shard_map.176), channel_id=1, source_target_pairs={{0,64},{64,0},{128,192},{192,128},{1,65},{65,1},{129,193},{193,129... | collective-permute-start | bytes 12296 | tf_op jit(solution)/shard_map/ppermute | solution.py:455
  8.1 2.8 %collective-permute-done.1.b_ref = f32[8,128]{1,0:T(8,128)S(1)} collective-permute-done((f32[8,128]{1,0:T(8,128)S(1)}, f32[8,128]{1,0:T(8,128)S(1)}, u32[]{:S(2)}, u32[]{:S(2)}) %collective-permute-start.1) | collective-permute-done | bytes 4128 | tf_op jit(solution)/shard_map/ppermute | solution.py:455
  11.2 7.5 %collective-permute-start.3 = (f32[8,128]{1,0:T(8,128)S(1)}, f32[8,128]{1,0:T(8,128)S(1)}, u32[]{:S(2)}, u32[]{:S(2)}) collective-permute-start(f32[8,128]{1,0:T(8,128)S(1)} %get-tuple-element.35), channel_id=1, source_target_pairs={{0,63},{1,2},{2,1},{3,4},{4,3},{5,6},{6,5},{7,8},{8,7},{9,10},{10,... | collective-permute-start | bytes 12296 | tf_op jit(solution)/shard_map/ppermute | solution.py:455
  24.5 9.1 %shard_map.178 = (f32[8,24,128]{2,1,0:T(8,128)S(1)}, f32[8,24,128]{2,1,0:T(8,128)S(1)}, bf16[384,3072]{1,0:T(8,128)(2,1)S(1)}, bf16[384,3072]{1,0:T(8,128)(2,1)}...) custom-call(f32[8,128]{1,0:T(8,128)S(1)} %maximum_maximum_fusion.row, ...), custom_call_target="tpu_custom_call" | custom-call | tf_op jit(solution)/shard_map/pallas_call | solution.py:442
  36.5 2.6 %collective-permute-start.5 = (f32[128,128]{1,0:T(8,128)S(1)}, f32[128,128]{1,0:T(8,128)S(1)}, u32[]{:S(2)}, u32[]{:S(2)}) collective-permute-start(f32[128,128]{1,0:T(8,128)S(1)} %get-tuple-element.37), channel_id=1, source_target_pairs={{0,192},{64,128},{128,64},{192,0},{1,193},{65,129},{129,65},{193,1... | collective-permute-start | bytes 196616 | tf_op jit(solution)/shard_map/ppermute | solution.py:455
  39.9 2.7 %shard_map.181.cs_ref = f32[128,2048]{1,0:T(8,128)S(1)} custom-call(f32[8,128]{1,0:T(8,128)S(1)} %maximum_maximum_fusion.rows_ref, f32[8,1024]{1,0:T(8,128)S(1)} %concatenate.15.wave_ref), custom_call_target="tpu_custom_call" | custom-call | flops 100000000 | bytes 1000000 | tf_op jit(solution)/shard_map/pallas_call | solution.py:442
  43.0 3.6 %collective-permute-start.7 = (f32[128,128]{1,0:T(8,128)S(1)}, f32[128,128]{1,0:T(8,128)S(1)}, u32[]{:S(2)}, u32[]{:S(2)}) collective-permute-start(f32[128,128]{1,0:T(8,128)S(1)} %get-tuple-element.39), channel_id=1, source_target_pairs={{0,63},{1,2},{2,1},{3,4},{4,3},{5,6},{6,5},{7,8},{8,7},{9,10},{10,... | collective-permute-start | bytes 196616 | tf_op jit(solution)/shard_map/ppermute | solution.py:455
  46.7 6.0 %shard_map.180 = (bf16[384,3072]{1,0:T(8,128)(2,1)S(1)}, bf16[384,3072]{1,0:T(8,128)(2,1)S(1)}) custom-call(f32[8,24,128]{2,1,0:T(8,128)S(1)} %get-tuple-element.41.geo_ref, bf16[2,64,8]{2,1,0:T(8,128)(2,1)S(1)} %copy.20.w1_ref, bf16[2,64,64]{2,1,0:T(8,128)(2,1)S(1)} %copy-done.23, bf16[2,384,64]{2,1,0:T(8,128)(2,1)S(1)} %copy.21.w3_ref), custom_call_target="tpu_custom_call" | custom-call | flops 1000000000 | bytes 10000000 | tf_op jit(solution)/shard_map/pallas_call | solution.py:442
  55.6 4.8 %shard_map.182 = (f32[128,3072]{1,0:T(8,128)S(1)}, f32[9,128,128]{2,1,0:T(8,128)S(1)}, f32[128,128]{1,0:T(8,128)S(1)}, f32[64,128]{1,0:T(8,128)S(1)}, f32[1024,128]{1,0:T(8,128)S(1)}) custom-call(f32[128,128]{1,0:T(8,128)S(1)} %get-tuple-element.36.h_ref, f32[128,128]{1,0:T(8,128)S(1)} %get-tuple-element.38.part_ref, ...), custom_call_target="tpu_custom_call" | custom-call | tf_op jit(solution)/shard_map/pallas_call | solution.py:442
  62.4 15.3 %all_to_all.19 = f32[32,32,128]{2,1,0:T(8,128)S(1)} all-to-all(f32[32,32,128]{2,1,0:T(8,128)S(1)} %bitcast.22), channel_id=1, replica_groups=mesh['xh'=2,'co'=2,'y'=4,'z'=8,'xl'=2] {'xh','co','y','xl'}, dimensions={0} | all-to-all | bytes 1048576 | tf_op jit(solution)/shard_map/all_to_all | solution.py:475
  77.8 2.6 %collective-permute-done.8 = f32[32,128]{1,0:T(8,128)S(1)} collective-permute-done((f32[32,128]{1,0:T(8,128)S(1)}, f32[32,128]{1,0:T(8,128)S(1)}, u32[]{:S(2)}, u32[]{:S(2)}) %collective-permute-start.8) | collective-permute-done | bytes 16416 | tf_op jit(solution)/shard_map/ppermute | solution.py:455
  80.4 3.5 %collective-permute-done.9 = f32[32,128]{1,0:T(8,128)S(1)} collective-permute-done((f32[32,128]{1,0:T(8,128)S(1)}, f32[32,128]{1,0:T(8,128)S(1)}, u32[]{:S(2)}, u32[]{:S(2)}) %collective-permute-start.9) | collective-permute-done | bytes 16416 | tf_op jit(solution)/shard_map/ppermute | solution.py:455
  85.3 5.1 %collective-permute-done.10 = f32[32,128]{1,0:T(8,128)S(1)} collective-permute-done((f32[32,128]{1,0:T(8,128)S(1)}, f32[32,128]{1,0:T(8,128)S(1)}, u32[]{:S(2)}, u32[]{:S(2)}) %collective-permute-start.10) | collective-permute-done | bytes 16416 | tf_op jit(solution)/shard_map/ppermute | solution.py:455
  91.3 8.1 %all-to-all-start.1 = ((f32[32,32,128]{2,1,0:T(8,128)}), f32[32,32,128]{2,1,0:T(8,128)S(1)}, u32[]{:S(2)}, u32[]{:S(2)}) async-start(f32[32,32,128]{2,1,0:T(8,128)} %broadcast_in_dim.33), calls=%async_computation.1 | async-start | bytes 1048576 | tf_op jit(solution)/shard_map/all_to_all | solution.py:480
  102.1 8.4 %all-to-all-done.1 = f32[32,32,128]{2,1,0:T(8,128)S(1)} async-done(((f32[32,32,128]{2,1,0:T(8,128)}), f32[32,32,128]{2,1,0:T(8,128)S(1)}, u32[]{:S(2)}, u32[]{:S(2)}) %all-to-all-start.1) | async-done | bytes 524320 | tf_op jit(solution)/shard_map/all_to_all | solution.py:480
  117.0 10.4 %shard_map.184 = (f32[1,128]{1,0:T(1,128)}, f32[8,128]{1,0:T(8,128)S(1)}, f32[128,128]{1,0:T(8,128)S(1)}, f32[128,128]{1,0:T(8,128)S(1)}, f32[128,128]{1,0:T(8,128)S(1)}, /*index=5*/f32[9,24,128]{2,1,0:T(8,128)S(1)}) custom-call(f32[1024,128]{1,0:T(8,128)S(1)} %bitcast.21, f32[64,1024]{1,0:T(8,128)S(1)} %copy-done.13, f32[128,2048]{1,0:T(8,128)S(1)} %shard_map.181.cs_ref, ...), custom_call_target="tpu_custom_call" | custom-call | tf_op jit(solution)/shard_map/pallas_call | solution.py:442
  127.8 2.0 %collective-permute-start.12 = (f32[128,128]{1,0:T(8,128)S(1)}, f32[128,128]{1,0:T(8,128)S(1)}, u32[]{:S(2)}, u32[]{:S(2)}) collective-permute-start(f32[128,128]{1,0:T(8,128)S(1)} %get-tuple-element.52), channel_id=1, source_target_pairs={{0,63},{1,2},{2,1},{3,4},{4,3},{5,6},{6,5},{7,8},{8,7},{9,10},{10,... | collective-permute-start | bytes 196616 | tf_op jit(solution)/shard_map/ppermute | solution.py:455
  130.9 4.2 %collective-permute-done.12.b_in = f32[128,128]{1,0:T(8,128)S(1)} collective-permute-done((f32[128,128]{1,0:T(8,128)S(1)}, f32[128,128]{1,0:T(8,128)S(1)}, u32[]{:S(2)}, u32[]{:S(2)}) %collective-permute-start.12) | collective-permute-done | bytes 65568 | tf_op jit(solution)/shard_map/ppermute | solution.py:455
  135.4 1.8 %collective-permute-start.13 = (f32[128,128]{1,0:T(8,128)S(1)}, f32[128,128]{1,0:T(8,128)S(1)}, u32[]{:S(2)}, u32[]{:S(2)}) collective-permute-start(f32[128,128]{1,0:T(8,128)S(1)} %get-tuple-element.54), channel_id=1, source_target_pairs={{0,64},{64,0},{128,192},{192,128},{1,65},{65,1},{129,193},{193,129... | collective-permute-start | bytes 196616 | tf_op jit(solution)/shard_map/ppermute | solution.py:455
  138.9 3.7 %collective-permute-done.14.b_in = f32[128,128]{1,0:T(8,128)S(1)} collective-permute-done((f32[128,128]{1,0:T(8,128)S(1)}, f32[128,128]{1,0:T(8,128)S(1)}, u32[]{:S(2)}, u32[]{:S(2)}) %collective-permute-start.14) | collective-permute-done | bytes 65568 | tf_op jit(solution)/shard_map/ppermute | solution.py:455
  142.6 6.5 %shard_map.186 = (f32[8,128]{1,0:T(8,128)S(1)}, f32[8,128]{1,0:T(8,128)S(1)}, f32[8,128]{1,0:T(8,128)S(1)}) custom-call(f32[128,128]{1,0:T(8,128)S(1)} %get-tuple-element.53.gown_ref, f32[128,128]{1,0:T(8,128)S(1)} %collective-permute-done.13.a_in, f32[128,128]{1,0:T(8,128)S(1)} %collective-permute-done.14.b_in, s32[1,128]{1,0:T(1,128)S(1)} %copy-done.28, ...), custom_call_target="tpu_custom_call" | custom-call | tf_op jit(solution)/shard_map/pallas_call | solution.py:442
  149.0 2.6 %collective-permute-start.16 = (f32[8,128]{1,0:T(8,128)S(1)}, f32[8,128]{1,0:T(8,128)S(1)}, u32[]{:S(2)}, u32[]{:S(2)}) collective-permute-start(f32[8,128]{1,0:T(8,128)S(1)} %get-tuple-element.63), channel_id=1, source_target_pairs={{0,63},{1,2},{2,1},{3,4},{4,3},{5,6},{6,5},{7,8},{8,7},{9,10},{10,... | collective-permute-start | bytes 12296 | tf_op jit(solution)/shard_map/ppermute | solution.py:455
  151.6 4.2 %collective-permute-done.16.b_in = f32[8,128]{1,0:T(8,128)S(1)} collective-permute-done((f32[8,128]{1,0:T(8,128)S(1)}, f32[8,128]{1,0:T(8,128)S(1)}, u32[]{:S(2)}, u32[]{:S(2)}) %collective-permute-start.16) | collective-permute-done | bytes 4128 | tf_op jit(solution)/shard_map/ppermute | solution.py:455
  158.9 2.9 %collective-permute-done.18.b_in = f32[8,128]{1,0:T(8,128)S(1)} collective-permute-done((f32[8,128]{1,0:T(8,128)S(1)}, f32[8,128]{1,0:T(8,128)S(1)}, u32[]{:S(2)}, u32[]{:S(2)}) %collective-permute-start.18) | collective-permute-done | bytes 4128 | tf_op jit(solution)/shard_map/ppermute | solution.py:455
  (114 shorter events, 38.1 us)
Async XLA Ops:
  0.6 46.0 %copy-start.23 = (bf16[2,64,64]{2,1,0:T(8,128)(2,1)S(1)}, bf16[2,64,64]{2,1,0:T(8,128)(2,1)}, u32[]{:S(2)}) copy-start(bf16[2,64,64]{2,1,0:T(8,128)(2,1)} %w2_ref.3) | copy-start | bytes 49156
  2.2 36.9 %copy-start.27 = (s32[1,128]{1,0:T(1,128)}, s32[1,128]{1,0:T(1,128)S(1)}, u32[]{:S(2)}) copy-start(s32[1,128]{1,0:T(1,128)S(1)} %add_bitcast_fusion.ix_ref) | copy-start | bytes 1540
  3.1 5.0 %collective-permute-start = (f32[8,128]{1,0:T(8,128)S(1)}, f32[8,128]{1,0:T(8,128)S(1)}, u32[]{:S(2)}, u32[]{:S(2)}) collective-permute-start(f32[8,128]{1,0:T(8,128)S(1)} %shard_map.176), channel_id=1, source_target_pairs={{0,64},{64,0},{128,192},{192,128},{1,65},{65,1},{129,193},{193,129... | collective-permute-start | bytes 12296 | tf_op jit(solution)/shard_map/ppermute | solution.py:455
  6.4 4.5 %collective-permute-start.1 = (f32[8,128]{1,0:T(8,128)S(1)}, f32[8,128]{1,0:T(8,128)S(1)}, u32[]{:S(2)}, u32[]{:S(2)}) collective-permute-start(f32[8,128]{1,0:T(8,128)S(1)} %shard_map.176), channel_id=1, source_target_pairs={{0,192},{64,128},{128,64},{192,0},{1,193},{65,129},{129,65},{193,1... | collective-permute-start | bytes 12296 | tf_op jit(solution)/shard_map/ppermute | solution.py:455
  11.1 11.0 %collective-permute-start.2 = (f32[8,128]{1,0:T(8,128)S(1)}, f32[8,128]{1,0:T(8,128)S(1)}, u32[]{:S(2)}, u32[]{:S(2)}) collective-permute-start(f32[8,128]{1,0:T(8,128)S(1)} %get-tuple-element.35), channel_id=1, source_target_pairs={{0,1},{1,0},{2,3},{3,2},{4,5},{5,4},{6,7},{7,6},{8,9},{9,8},{10,11... | collective-permute-start | bytes 12296 | tf_op jit(solution)/shard_map/ppermute | solution.py:455
  11.2 10.9 %collective-permute-start.3 = (f32[8,128]{1,0:T(8,128)S(1)}, f32[8,128]{1,0:T(8,128)S(1)}, u32[]{:S(2)}, u32[]{:S(2)}) collective-permute-start(f32[8,128]{1,0:T(8,128)S(1)} %get-tuple-element.35), channel_id=1, source_target_pairs={{0,63},{1,2},{2,1},{3,4},{4,3},{5,6},{6,5},{7,8},{8,7},{9,10},{10,... | collective-permute-start | bytes 12296 | tf_op jit(solution)/shard_map/ppermute | solution.py:455
  35.9 6.7 %collective-permute-start.4 = (f32[128,128]{1,0:T(8,128)S(1)}, f32[128,128]{1,0:T(8,128)S(1)}, u32[]{:S(2)}, u32[]{:S(2)}) collective-permute-start(f32[128,128]{1,0:T(8,128)S(1)} %get-tuple-element.37), channel_id=1, source_target_pairs={{0,64},{64,0},{128,192},{192,128},{1,65},{65,1},{129,193},{193,129... | collective-permute-start | bytes 196616 | tf_op jit(solution)/shard_map/ppermute | solution.py:455
  36.5 6.2 %collective-permute-start.5 = (f32[128,128]{1,0:T(8,128)S(1)}, f32[128,128]{1,0:T(8,128)S(1)}, u32[]{:S(2)}, u32[]{:S(2)}) collective-permute-start(f32[128,128]{1,0:T(8,128)S(1)} %get-tuple-element.37), channel_id=1, source_target_pairs={{0,192},{64,128},{128,64},{192,0},{1,193},{65,129},{129,65},{193,1... | collective-permute-start | bytes 196616 | tf_op jit(solution)/shard_map/ppermute | solution.py:455
  42.9 12.6 %collective-permute-start.6 = (f32[128,128]{1,0:T(8,128)S(1)}, f32[128,128]{1,0:T(8,128)S(1)}, u32[]{:S(2)}, u32[]{:S(2)}) collective-permute-start(f32[128,128]{1,0:T(8,128)S(1)} %get-tuple-element.39), channel_id=1, source_target_pairs={{0,1},{1,0},{2,3},{3,2},{4,5},{5,4},{6,7},{7,6},{8,9},{9,8},{10,11... | collective-permute-start | bytes 196616 | tf_op jit(solution)/shard_map/ppermute | solution.py:455
  43.0 12.5 %collective-permute-start.7 = (f32[128,128]{1,0:T(8,128)S(1)}, f32[128,128]{1,0:T(8,128)S(1)}, u32[]{:S(2)}, u32[]{:S(2)}) collective-permute-start(f32[128,128]{1,0:T(8,128)S(1)} %get-tuple-element.39), channel_id=1, source_target_pairs={{0,63},{1,2},{2,1},{3,4},{4,3},{5,6},{6,5},{7,8},{8,7},{9,10},{10,... | collective-permute-start | bytes 196616 | tf_op jit(solution)/shard_map/ppermute | solution.py:455
  77.7 2.7 %collective-permute-start.8 = (f32[32,128]{1,0:T(8,128)S(1)}, f32[32,128]{1,0:T(8,128)S(1)}, u32[]{:S(2)}, u32[]{:S(2)}) collective-permute-start(f32[32,128]{1,0:T(8,128)S(1)} %shard_map.183), channel_id=1, source_target_pairs={{0,2},{2,0},{4,6},{6,4},{8,10},{10,8},{12,14},{14,12},{1,3},{3,1},... | collective-permute-start | bytes 49160 | tf_op jit(solution)/shard_map/ppermute | solution.py:455
  80.4 3.5 %collective-permute-start.9 = (f32[32,128]{1,0:T(8,128)S(1)}, f32[32,128]{1,0:T(8,128)S(1)}, u32[]{:S(2)}, u32[]{:S(2)}) collective-permute-start(f32[32,128]{1,0:T(8,128)S(1)} %add.89), channel_id=1, source_target_pairs={{0,4},{2,6},{4,0},{6,2},{8,12},{10,14},{12,8},{14,10},{1,5},{3,7},... | collective-permute-start | bytes 49160 | tf_op jit(solution)/shard_map/ppermute | solution.py:455
  83.9 6.5 %collective-permute-start.10 = (f32[32,128]{1,0:T(8,128)S(1)}, f32[32,128]{1,0:T(8,128)S(1)}, u32[]{:S(2)}, u32[]{:S(2)}) collective-permute-start(f32[32,128]{1,0:T(8,128)S(1)} %add.90), channel_id=1, source_target_pairs={{0,8},{2,10},{4,12},{6,14},{8,0},{10,2},{12,4},{14,6},{1,9},{3,11}... | collective-permute-start | bytes 49160 | tf_op jit(solution)/shard_map/ppermute | solution.py:455
  91.3 19.2 %all-to-all-start.1 = ((f32[32,32,128]{2,1,0:T(8,128)}), f32[32,32,128]{2,1,0:T(8,128)S(1)}, u32[]{:S(2)}, u32[]{:S(2)}) async-start(f32[32,32,128]{2,1,0:T(8,128)} %broadcast_in_dim.33), calls=%async_computation.1 | async-start | bytes 1048576 | tf_op jit(solution)/shard_map/all_to_all | solution.py:480
  117.0 25.5 %copy-start.15 = (f32[8,24,128]{2,1,0:T(8,128)S(1)}, f32[8,24,128]{2,1,0:T(8,128)}, u32[]{:S(2)}) copy-start(f32[8,24,128]{2,1,0:T(8,128)} %copy-done.14) | copy-start | bytes 294916
  117.0 25.5 %copy-start.28 = (s32[1,128]{1,0:T(1,128)S(1)}, s32[1,128]{1,0:T(1,128)}, u32[]{:S(2)}) copy-start(s32[1,128]{1,0:T(1,128)} %copy-done.27) | copy-start | bytes 1540
  127.5 3.5 %collective-permute-start.11 = (f32[128,128]{1,0:T(8,128)S(1)}, f32[128,128]{1,0:T(8,128)S(1)}, u32[]{:S(2)}, u32[]{:S(2)}) collective-permute-start(f32[128,128]{1,0:T(8,128)S(1)} %get-tuple-element.52), channel_id=1, source_target_pairs={{0,1},{1,0},{2,3},{3,2},{4,5},{5,4},{6,7},{7,6},{8,9},{9,8},{10,11... | collective-permute-start | bytes 196616 | tf_op jit(solution)/shard_map/ppermute | solution.py:455
  127.8 7.3 %collective-permute-start.12 = (f32[128,128]{1,0:T(8,128)S(1)}, f32[128,128]{1,0:T(8,128)S(1)}, u32[]{:S(2)}, u32[]{:S(2)}) collective-permute-start(f32[128,128]{1,0:T(8,128)S(1)} %get-tuple-element.52), channel_id=1, source_target_pairs={{0,63},{1,2},{2,1},{3,4},{4,3},{5,6},{6,5},{7,8},{8,7},{9,10},{10,... | collective-permute-start | bytes 196616 | tf_op jit(solution)/shard_map/ppermute | solution.py:455
  135.4 3.5 %collective-permute-start.13 = (f32[128,128]{1,0:T(8,128)S(1)}, f32[128,128]{1,0:T(8,128)S(1)}, u32[]{:S(2)}, u32[]{:S(2)}) collective-permute-start(f32[128,128]{1,0:T(8,128)S(1)} %get-tuple-element.54), channel_id=1, source_target_pairs={{0,64},{64,0},{128,192},{192,128},{1,65},{65,1},{129,193},{193,129... | collective-permute-start | bytes 196616 | tf_op jit(solution)/shard_map/ppermute | solution.py:455
  137.2 5.3 %collective-permute-start.14 = (f32[128,128]{1,0:T(8,128)S(1)}, f32[128,128]{1,0:T(8,128)S(1)}, u32[]{:S(2)}, u32[]{:S(2)}) collective-permute-start(f32[128,128]{1,0:T(8,128)S(1)} %get-tuple-element.54), channel_id=1, source_target_pairs={{0,192},{64,128},{128,64},{192,0},{1,193},{65,129},{129,65},{193,1... | collective-permute-start | bytes 196616 | tf_op jit(solution)/shard_map/ppermute | solution.py:455
  149.0 2.6 %collective-permute-start.15 = (f32[8,128]{1,0:T(8,128)S(1)}, f32[8,128]{1,0:T(8,128)S(1)}, u32[]{:S(2)}, u32[]{:S(2)}) collective-permute-start(f32[8,128]{1,0:T(8,128)S(1)} %get-tuple-element.63), channel_id=1, source_target_pairs={{0,1},{1,0},{2,3},{3,2},{4,5},{5,4},{6,7},{7,6},{8,9},{9,8},{10,11... | collective-permute-start | bytes 12296 | tf_op jit(solution)/shard_map/ppermute | solution.py:455
  149.0 6.8 %collective-permute-start.16 = (f32[8,128]{1,0:T(8,128)S(1)}, f32[8,128]{1,0:T(8,128)S(1)}, u32[]{:S(2)}, u32[]{:S(2)}) collective-permute-start(f32[8,128]{1,0:T(8,128)S(1)} %get-tuple-element.63), channel_id=1, source_target_pairs={{0,63},{1,2},{2,1},{3,4},{4,3},{5,6},{6,5},{7,8},{8,7},{9,10},{10,... | collective-permute-start | bytes 12296 | tf_op jit(solution)/shard_map/ppermute | solution.py:455
  156.0 2.9 %collective-permute-start.17 = (f32[8,128]{1,0:T(8,128)S(1)}, f32[8,128]{1,0:T(8,128)S(1)}, u32[]{:S(2)}, u32[]{:S(2)}) collective-permute-start(f32[8,128]{1,0:T(8,128)S(1)} %get-tuple-element.65), channel_id=1, source_target_pairs={{0,64},{64,0},{128,192},{192,128},{1,65},{65,1},{129,193},{193,129... | collective-permute-start | bytes 12296 | tf_op jit(solution)/shard_map/ppermute | solution.py:455
  157.3 4.5 %collective-permute-start.18 = (f32[8,128]{1,0:T(8,128)S(1)}, f32[8,128]{1,0:T(8,128)S(1)}, u32[]{:S(2)}, u32[]{:S(2)}) collective-permute-start(f32[8,128]{1,0:T(8,128)S(1)} %get-tuple-element.65), channel_id=1, source_target_pairs={{0,192},{64,128},{128,64},{192,0},{1,193},{65,129},{129,65},{193,1... | collective-permute-start | bytes 12296 | tf_op jit(solution)/shard_map/ppermute | solution.py:455
  (26 other events, 167.5 us)

commit v2 on v1

--- a/solution.py
+++ b/solution.py
@@ -79,37 +79,83 @@
     return dot(grads, onehot_columns(index_row, count, F32), NT, HIGHEST)
 
 
-def strip_x_kernel(rows_ref, ix_ref, out_ref):
-    out_ref[...] = pick(rows_ref[...], ix_ref[...])
-
-
-def strip_y_kernel(rows_ref, a_ref, b_ref, iy_ref, part_ref, out_ref):
+def send_rows(values, count, gap, a_ref, b_ref):
+    rows = values.T
+    a_ref[...] = rows[:count]
+    b_ref[...] = rows[gap : gap + count]
+
+
+def received(a_ref, b_ref, gap):
+    a, b = a_ref[...], b_ref[...]
+    pieces = [a, b, jnp.zeros((128 - gap - b.shape[0], 128), F32)]
+    if gap > a.shape[0]:
+        pieces.insert(1, jnp.zeros((gap - a.shape[0], 128), F32))
+    return jnp.concatenate(pieces, 0).T
+
+
+def place(index):
+    px, py = lax.axis_index("co"), lax.axis_index("xl")
+    far = jnp.where(index < 240, index + (128 - 64 * py), index + (16 + 64 * py))
+    near = jnp.where(index < 160, index + (32 - 32 * px), index + (32 * px - 32))
+    return jnp.where(index < 128, index, jnp.where(index < 192, near, far))
+
+
+def strip_x_kernel(pos_ref, species_ref, send_ref, rows_ref, ix_ref, out_ref):
+    odd = lax.axis_index("co")
+    lower, upper = send_ref[0:1, :], send_ref[1:2, :]
+    first = upper + (lower - upper) * odd
+    second = lower + (upper - lower) * odd
+    index = jnp.concatenate([first, second, jnp.full((1, 64), -1, jnp.int32)], 1)
+    rows = jnp.concatenate([pos_ref[...], species_ref[...].astype(F32), jnp.zeros((4, ATOMS), F32)], 0)
+    ix_ref[...] = index
+    rows_ref[...] = rows
+    out_ref[...] = pick(rows, index)
+
+
+def strip_y_kernel(rows_ref, a_ref, b_ref, send_ref, part_ref, iy_ref, out_ref):
+    odd = lax.axis_index("xl")
+    send = place(send_ref[...])
+    lower, upper = send[0:1], send[1:2]
+    first = upper + (lower - upper) * odd
+    second = lower + (upper - lower) * odd
+    none = jnp.full((1, 16), -1, jnp.int32)
+    index = jnp.concatenate([first, none, second, none], 1)
     part = merge(a_ref[...], b_ref[...], 32)
     part_ref[...] = part
-    out_ref[...] = pick(jnp.concatenate([rows_ref[...], part], 1), iy_ref[...])
-
-
-def radial_tile(g, geo_ref, w1, w2, w3, r_ref, p_ref):
+    iy_ref[...] = index
+    out_ref[...] = pick(jnp.concatenate([rows_ref[...], part], 1), index)
+
+
+WIDE_TILE = 1024
+
+
+def flat(ref, k, g):
+    count = WIDE_TILE // 128
+    return jnp.concatenate([ref[k, count * g + j : count * g + j + 1, :] for j in range(count)], 1)
+
+
+def radial(layer, geo_ref, w1_ref, w2_ref, w3_ref, r_ref, p_ref):
+    w1 = w1_ref[layer].astype(BF16)
+    w2 = w2_ref[layer]
+    w3 = w3_ref[layer].astype(F32).T.astype(BF16)
     spacing = CUTOFF / (NBASIS - 1)
-    centre = lax.broadcasted_iota(jnp.int32, (NBASIS, 512), 0).astype(F32) * spacing
-
-    def row(k):
-        return jnp.concatenate([geo_ref[k, pl.ds(4 * g + j, 1), :] for j in range(4)], 1)
-
-    d = row(3)
-    gap = (d - centre) * (1.0 / spacing)
-    basis = jnp.exp(-gap * gap)
-    z1 = dot(w1, basis.astype(BF16))
-    s1, h1 = gate(z1)
-    z2 = dot(w2, h1.astype(BF16))
-    s2, h2 = gate(z2)
-    env = row(4)
-    cols = pl.ds(pl.multiple_of(g * 512, 512), 512)
-    r_ref[:, cols] = dot(w3, (h2 * env).astype(BF16)).astype(BF16)
-    slope = basis * gap * (-2.0 / spacing)
-    h1p = gate_slope(z1, s1) * dot(w1, slope.astype(BF16))
-    h2p = gate_slope(z2, s2) * dot(w2, h1p.astype(BF16))
-    p_ref[:, cols] = dot(w3, (h2p * row(6) + h2 * row(5)).astype(BF16)).astype(BF16)
+    centre = lax.broadcasted_iota(jnp.int32, (NBASIS, WIDE_TILE), 0).astype(F32) * spacing
+    for g in range(EDGES // WIDE_TILE):
+        cols = slice(g * WIDE_TILE, (g + 1) * WIDE_TILE)
+        gap = (flat(geo_ref, 3, g) - centre) * (1.0 / spacing)
+        basis = jnp.exp(-gap * gap)
+        z1 = dot(w1, basis.astype(BF16), TN)
+        s1, h1 = gate(z1)
+        z2 = dot(w2, h1.astype(BF16))
+        s2, h2 = gate(z2)
+        if r_ref is not None:
+            r_ref[:, cols] = dot(w3, (h2 * flat(geo_ref, 4, g)).astype(BF16)).astype(BF16)
+        if p_ref is not None:
+            slope = basis * gap * (-2.0 / spacing)
+            h1p = gate_slope(z1, s1) * dot(w1, slope.astype(BF16), TN)
+            h2p = gate_slope(z2, s2) * dot(w2, h1p.astype(BF16))
+            mixed = h2p * flat(geo_ref, 6, g) + h2 * flat(geo_ref, 5, g)
+            p_ref[:, cols] = dot(w3, mixed.astype(BF16)).astype(BF16)
 
 
 def aggregate(r_ref, get_f, y_ref, a_ref):
@@ -148,12 +194,14 @@
 
 
 def first_kernel(
-    box_x, box_y, rows_ref, part_ref, a_in, b_in, nb_ref, live_ref, ix_ref, emb_ref, w1_ref, w2_ref,
-    w3_ref, mix_ref, geo_ref, y_ref, r_ref, p_ref, f_ref, a_ref, h_ref, strip_ref,
+    box_x, box_y, rows_ref, part_ref, a_in, b_in, raw_ref, live_ref, ix_ref, emb_ref, w1_ref, w2_ref,
+    w3_ref, mix_ref, nb_ref, geo_out, y_out, f_out, a_out, h_ref, h_out, xa_ref, xb_ref, r_ref,
 ):
+    geo_ref, y_ref, f_ref, a_ref = geo_out.ref, y_out.ref, f_out.ref, a_out.ref
     own = rows_ref[...]
     tables = [own, part_ref[...], merge(a_in[...], b_in[...], 64)]
-    nb = nb_ref[...]
+    nb = place(raw_ref[...])
+    nb_ref[...] = nb
     lane, group = nb & 127, nb >> 7
 
     def gathered(row):
@@ -197,51 +245,62 @@
     y_ref[6] = ux * ux - uy * uy
     y_ref[7] = (2.0 * uz * uz - ux * ux - uy * uy) * (1.0 / ROOT_THREE)
 
-    species = gathered(3)
-    emb = emb_ref[...]
-    w1, w2, w3 = w1_ref[0], w2_ref[0], w3_ref[0]
-    geo_ref[7] = species
-
-    def tile(g, carry):
-        radial_tile(g, geo_ref, w1, w2, w3, r_ref, p_ref)
-        kinds = lax.broadcasted_iota(jnp.int32, (8, 512), 0).astype(F32)
-        kind = jnp.concatenate([geo_ref[7, pl.ds(4 * g + j, 1), :] for j in range(4)], 1)
-        cols = pl.ds(pl.multiple_of(g * 512, 512), 512)
-        f_ref[:, cols] = dot(emb, (kinds == kind).astype(F32).astype(BF16)).astype(BF16)
-        return carry
-
-    lax.fori_loop(0, NB // 4, tile, 0)
+    geo_ref[7] = gathered(3)
+    geo_out.send()
+    y_out.send()
+    emb = jnp.concatenate([emb_ref[...], jnp.zeros((8 - emb_ref.shape[0], C), F32)], 0).astype(BF16)
+    kinds = lax.broadcasted_iota(jnp.int32, (8, WIDE_TILE), 0).astype(F32)
+    for g in range(EDGES // WIDE_TILE):
+        cols = slice(g * WIDE_TILE, (g + 1) * WIDE_TILE)
+        f_ref[:, cols] = dot(emb, (kinds == flat(geo_ref, 7, g)).astype(F32).astype(BF16), TN).astype(BF16)
+    f_out.send()
+    radial(0, geo_ref, w1_ref, w2_ref, w3_ref, r_ref, None)
 
     def get_f(r0):
         return lambda n: f_ref[pl.ds(r0, 16), n * 128 : (n + 1) * 128].astype(F32)
 
     aggregate(r_ref, get_f, y_ref, a_ref)
-    kinds = lax.broadcasted_iota(jnp.int32, (8, 128), 0).astype(F32)
-    h_zero = dot(emb, (kinds == own[3:4]).astype(F32).astype(BF16))
+    a_out.send()
+    h_zero = dot(emb, (kinds[:, :128] == own[3:4]).astype(F32).astype(BF16), TN)
     h_one = h_zero + dot(mix_ref[0], invariants(a_ref))
     h_ref[...] = h_one
-    strip_ref[...] = pick(h_one, ix_ref[...])
-
-
-def radial_kernel(geo_ref, w1_ref, w2_ref, w3_ref, r_ref, p_ref):
-    w1, w2, w3 = w1_ref[1], w2_ref[1], w3_ref[1]
-
-    def tile(g, carry):
-        radial_tile(g, geo_ref, w1, w2, w3, r_ref, p_ref)
-        return carry
-
-    lax.fori_loop(0, NB // 4, tile, 0)
-
-
-def waves_kernel(box_x, box_y, rows_ref, wave_ref, cs_ref):
+    h_out.ref[...] = h_one
+    h_out.send()
+    send_rows(pick(h_one, ix_ref[...]), 32, 32, xa_ref, xb_ref)
+
+
+def radial_kernel(geo_ref, w1_ref, w2_ref, w3_ref, r_ref, r_out):
+    radial(1, geo_ref, w1_ref, w2_ref, w3_ref, r_ref, None)
+    r_out.ref[...] = r_ref[...]
+
+
+def slope_one_kernel(geo_ref, w1_ref, w2_ref, w3_ref, nb_ref, p_out, oh_out):
+    fill_onehot(nb_ref, oh_out.ref)
+    oh_out.send()
+    radial(1, geo_ref, w1_ref, w2_ref, w3_ref, None, p_out.ref)
+
+
+def slope_zero_kernel(geo_ref, w1_ref, w2_ref, w3_ref, r_ref, p_ref):
+    radial(0, geo_ref, w1_ref, w2_ref, w3_ref, r_ref, p_ref)
+
+
+def waves_kernel(box_x, box_y, rows_ref, wave_ref, cs_out):
+    cs_ref = cs_out.ref
     own = rows_ref[...]
     x, y, z = own[0:1] * (1.0 / box_x), own[1:2] * (1.0 / box_y), own[2:3] * (1.0 / DEPTH_Z)
-    x, y, z = x - jnp.floor(x), y - jnp.floor(y), z - jnp.floor(z)
-    turns = jnp.concatenate([x, y, z, jnp.zeros((5, 128), F32)], 0)
+    turns = jnp.concatenate([x, y, z, jnp.zeros((5, ATOMS), F32)], 0)
+    turns = turns - jnp.floor(turns)
+    high = turns.astype(BF16).astype(F32)
+    middle = (turns - high).astype(BF16).astype(F32)
+    low = turns - high - middle
+    parts = jnp.concatenate([high, middle, low, jnp.zeros((8, ATOMS), F32)], 0).astype(BF16)
+    wave = jnp.concatenate([wave_ref[...].astype(F32), jnp.zeros((5, K), F32)], 0)
+    wave = jnp.concatenate([wave, wave, wave, jnp.zeros((8, K), F32)], 0).astype(BF16)
+    cs_ref[:, :K] = dot(parts, wave, TN)
 
     def tile(t, carry):
         cols = pl.ds(pl.multiple_of(t * 128, 128), 128)
-        phase = dot(turns, wave_ref[:, cols], TN, HIGHEST)
+        phase = cs_ref[:, cols]
         quarter = jnp.floor(4.0 * phase + 0.5)
         angle = (phase - 0.25 * quarter) * (2.0 * math.pi)
         sq = angle * angle
@@ -260,17 +319,18 @@
     lax.fori_loop(0, K // 128, tile, 0)
 
 
-def feature_strip_kernel(h_ref, a_in, b_in, iy_ref, part_ref, out_ref):
-    part = merge(a_in[...], b_in[...], 32)
+def feature_strip_kernel(h_ref, a_in, b_in, iy_ref, part_ref, ya_ref, yb_ref):
+    part = received(a_in, b_in, 32)
     part_ref[...] = part
-    out_ref[...] = pick(jnp.concatenate([h_ref[...], part], 1), iy_ref[...])
+    send_rows(pick(jnp.concatenate([h_ref[...], part], 1), iy_ref[...]), 48, 64, ya_ref, yb_ref)
 
 
 def second_kernel(
-    h_ref, part_ref, a_in, b_in, nb_ref, y_ref, r_ref, cs_ref, mix_ref, read_hidden_ref,
-    w_charge_ref, f_ref, a_ref, h2_ref, charge_ref, s_ref, ypart_ref,
+    h_ref, part_ref, a_in, b_in, nb_ref, y_ref, r_ref, cs_in, mix_in,
+    w_charge_ref, f_out, a_out, h2_out, charge_out, s_ref, ypart_ref,
 ):
-    ypart_ref[...] = merge(a_in[...], b_in[...], 64)
+    f_ref, a_ref, h2_ref, charge_ref = f_out.ref, a_out.ref, h2_out.ref, charge_out.ref
+    ypart_ref[...] = received(a_in, b_in, 64)
 
     def get_f(r0):
         rows = pl.ds(r0, 16)
@@ -285,10 +345,15 @@
         return state
 
     aggregate(r_ref, get_f, y_ref, a_ref)
+    f_out.send()
+    a_out.send()
+    mix_ref, cs_ref = mix_in.ready(), cs_in.ready()
     h_two = h_ref[...] + dot(mix_ref[1], invariants(a_ref))
     h2_ref[...] = h_two
     charge = dot(w_charge_ref[...], h_two.astype(BF16))
     charge_ref[...] = charge
+    h2_out.send()
+    charge_out.send()
     q_hi, q_lo = split(charge)
     q_both = jnp.concatenate([q_hi, q_lo], 0)
     for t in range(TILES // 2):
@@ -341,15 +406,14 @@
 
 
 def ewald_kernel(
-    box_x, box_y, scale, s_ref, spectral_ref, cs_ref, wave_ref, charge_ref, h_ref, h2_ref, a_ref, y_ref, r_ref, p_ref,
-    f_ref, nb_ref, iy_ref, mix_ref, read_first_ref, read_hidden_ref, read_last_ref, w_charge_ref,
-    energy_ref, gpos_ref, gown_ref, gpart_ref, gy_ref, t_ref, ga_ref, gf_ref, oh_ref,
+    box_x, box_y, scale, s_ref, spectral_ref, cs_ref, wave_ref, charge_ref, h_in, h2_in, a_in, y_in, r_in, p_in,
+    f_in, oh_in, mix_in, first_in, last_in, read_hidden_in, w_charge_in,
+    energy_ref, gpos_ref, gown_ref, gpart_ref, ya_ref, yb_ref, t_ref, ga_ref, gf_ref, gphase_ref,
 ):
     charge = charge_ref[...]
-    q_t = charge.T
-    qt_hi, qt_lo = split(q_t)
-    potential = jnp.zeros((KC, ATOMS), F32)
-    gpos = jnp.zeros((8, ATOMS), F32)
+    qt_hi, qt_lo = split(charge.T)
+    q_three = jnp.concatenate([qt_hi.astype(F32), qt_lo.astype(F32), qt_hi.astype(F32)], 1).astype(BF16)
+    total = jnp.zeros((2 * KC, 2 * ATOMS), F32)
     for t in range(TILES // 2):
         cols = slice(t * 128, (t + 1) * 128)
         late = slice(K + t * 128, K + (t + 1) * 128)
@@ -357,9 +421,17 @@
         gc = filt * s_ref[t * KC : (t + 1) * KC, :]
         gs = filt * s_ref[(TILES // 2 + t) * KC : (TILES // 2 + t + 1) * KC, :]
         cos, sin = cs_ref[:, cols], cs_ref[:, late]
-        potential = potential + dot3(gc, cos, NT) + dot3(gs, sin, NT)
-        gphase = dot3(q_t, gs) * cos - dot3(q_t, gc) * sin
-        gpos = gpos + dot3(wave_ref[:, cols], gphase, NT)
+        g_hi, g_lo = split(jnp.concatenate([gc, gs], 1))
+        c_hi, c_lo = split(jnp.concatenate([cos, sin], 1))
+        total = total + dot(jnp.concatenate([g_hi, g_lo], 0), jnp.concatenate([c_hi, c_lo], 0), NT)
+        phase = dot(q_three, jnp.concatenate([g_hi, g_hi, g_lo], 0))
+        p_hi, p_lo = split(phase[:, 128:] * cos - phase[:, :128] * sin)
+        gphase_ref[:ATOMS, cols] = p_hi
+        gphase_ref[ATOMS:, cols] = p_lo
+    potential = total[:KC, :ATOMS] + (total[KC:, :ATOMS] + total[:KC, ATOMS:])
+    wave = jnp.concatenate([wave_ref[...].astype(F32), jnp.zeros((5, K), F32)], 0).astype(BF16)
+    gpos = dot(wave, gphase_ref[...], NT)
+    gpos = gpos[:, :ATOMS] + gpos[:, ATOMS:]
     gpos_ref[...] = jnp.concatenate(
         [
             gpos[0:1] * (2.0 * math.pi / box_x),
@@ -369,23 +441,33 @@
         ],
         0,
     )
+    h_ref, h2_ref, first_ref, last_ref = h_in.ready(), h2_in.ready(), first_in.ready(), last_in.ready()
+    read_hidden_ref, w_charge_ref, mix_ref = read_hidden_in.ready(), w_charge_in.ready(), mix_in.ready()
     h_two = h2_ref[...].astype(BF16)
     z = dot(read_hidden_ref[...], h_two)
     s, hidden = gate(z)
-    last = read_last_ref[...]
-    site = jnp.sum(read_first_ref[...] * h_ref[...], 0, keepdims=True) + jnp.sum(last * hidden, 0, keepdims=True)
+    last = jnp.broadcast_to(last_ref[...], (128, last_ref.shape[1])).T
+    first = jnp.broadcast_to(first_ref[...], (128, 128)).T
+    site = jnp.sum(first * h_ref[...], 0, keepdims=True) + jnp.sum(last * hidden, 0, keepdims=True)
     energy_ref[...] = site + 0.5 * jnp.sum(charge * potential, 0, keepdims=True)
     g_hidden = (last * gate_slope(z, s)).astype(BF16)
     g_two = dot(w_charge_ref[...], potential.astype(BF16), TN) + dot(read_hidden_ref[...], g_hidden, TN)
     g_two = g_two.astype(BF16)
     g_inv = dot(mix_ref[1], g_two, TN).astype(BF16).astype(F32)
+    a_ref, y_ref, r_ref, p_ref, f_ref = a_in.ready(), y_in.ready(), r_in.ready(), p_in.ready(), f_in.ready()
     pull_invariants(g_inv, a_ref, ga_ref)
     backward(ga_ref, r_ref, p_ref, f_ref, y_ref, gf_ref, t_ref)
-    fill_onehot(nb_ref, oh_ref)
+    oh_ref = oh_in.ready()
     grads = dot(gf_ref[...], oh_ref[...], NT)
-    gown_ref[...] = grads[:, :128] + g_two.astype(F32) + read_first_ref[...]
+    gown_ref[...] = grads[:, :128] + g_two.astype(F32) + first
     gpart_ref[...] = grads[:, 128:256]
-    gy_ref[...] = grads[:, 256:]
+    send_rows(grads[:, 256:], 48, 64, ya_ref, yb_ref)
+
+
+def return_features_kernel(gown_ref, gpart_ref, a_in, b_in, iy_ref, own_ref, xa_ref, xb_ref):
+    back = give_back(received(a_in, b_in, 64), iy_ref[...], 256)
+    own_ref[...] = gown_ref[...] + back[:, :128]
+    send_rows(gpart_ref[...] + back[:, 128:], 32, 32, xa_ref, xb_ref)
 
 
 def return_y_kernel(gown_ref, gpart_ref, a_in, b_in, iy_ref, own_ref, part_ref):
@@ -395,10 +477,10 @@
 
 
 def last_kernel(
-    gown_ref, a_in, b_in, ix_ref, mix_ref, a_ref, r_ref, p_ref, f_ref, y_ref, t1_ref, geo_ref, nb_ref, gpos_ref,
-    own_ref, part_ref, gy_ref, ga_ref, t_ref, oh_ref, rows_ref,
+    gown_ref, a_in, b_in, ix_ref, mix_ref, a_ref, r_ref, p_ref, f_ref, y_ref, t1_ref, geo_ref, oh_ref, gpos_ref,
+    own_ref, part_ref, gy_ref, ga_ref, t_ref, rows_ref,
 ):
-    g_one = gown_ref[...] + give_back(merge(a_in[...], b_in[...], 32), ix_ref[...], 128)
+    g_one = gown_ref[...] + give_back(received(a_in, b_in, 32), ix_ref[...], 128)
     g_inv = dot(mix_ref[0], g_one.astype(BF16), TN).astype(BF16).astype(F32)
     pull_invariants(g_inv, a_ref, ga_ref)
     backward(ga_ref, r_ref, p_ref, f_ref, y_ref, None, t_ref)
@@ -416,7 +498,6 @@
         for n in range(NB):
             rows_ref[k : k + 1, n * 128 : (n + 1) * 128] = high[n : n + 1]
             rows_ref[8 + k : 9 + k, n * 128 : (n + 1) * 128] = low[n : n + 1]
-    fill_onehot(nb_ref, oh_ref)
     both = dot(rows_ref[...].astype(BF16), oh_ref[...], NT)
     grads = both[:8] + both[8:]
     centre = jnp.concatenate([jnp.sum(g, 0, keepdims=True) for g in steps] + [jnp.zeros((5, 128), F32)], 0)
@@ -430,22 +511,90 @@
     out_ref[...] = -total[:3]
 
 
-def sum_kernel(in_ref, out_ref):
-    rows = out_ref.shape[0]
+def sum_kernel(pieces, copies, in_ref, out_ref):
+    out_ref = getattr(out_ref, "ref", out_ref)
+    rows = in_ref.shape[0] // pieces
     total = in_ref[0:rows, :]
-    for g in range(1, in_ref.shape[0] // rows):
+    for g in range(1, pieces):
         total = total + in_ref[g * rows : (g + 1) * rows, :]
-    out_ref[...] = total
+    for g in range(copies):
+        out_ref[g * rows : (g + 1) * rows, :] = total
+
+
+class Far:
+    def __init__(self, array, late=False):
+        self.array = array
+        self.late = late
+
+
+class Late:
+    def __init__(self, copy, ref):
+        self.copy = copy
+        self.ref = ref
+
+    def ready(self):
+        self.copy.wait()
+        return self.ref
+
+
+class Out:
+    def __init__(self, copy, ref):
+        self.copy = copy
+        self.ref = ref
+        self.sent = False
+
+    def send(self):
+        self.copy.start()
+        self.sent = True
 
 
 def call(kernel, outs, *operands, scratch=(), flops=0, moved=0):
+    n_in, n_out = len(operands), len(outs)
+    far_in = [i for i, o in enumerate(operands) if isinstance(o, Far)]
+    far_out = [i for i, o in enumerate(outs) if len(o) == 3]
+    arrays = [pltpu.with_memory_space_constraint(o.array, pltpu.HBM) if isinstance(o, Far) else o for o in operands]
+    n_far = len(far_in) + len(far_out)
+    buffers = [pltpu.VMEM(arrays[i].shape, arrays[i].dtype) for i in far_in]
+    buffers += [pltpu.VMEM(outs[i][0], outs[i][1]) for i in far_out]
+
+    def wrapped(*refs):
+        ins, results, rest = list(refs[:n_in]), list(refs[n_in : n_in + n_out]), refs[n_in + n_out :]
+        own, held = rest[: len(scratch)], rest[len(scratch) : len(scratch) + n_far]
+        sems = rest[-1]
+        waits = []
+        for k, i in enumerate(far_in):
+            copy = pltpu.make_async_copy(ins[i], held[k], sems.at[k])
+            copy.start()
+            if operands[i].late:
+                ins[i] = Late(copy, held[k])
+            else:
+                waits.append(copy)
+                ins[i] = held[k]
+        sent = []
+        for k, i in enumerate(far_out, len(far_in)):
+            results[i] = Out(pltpu.make_async_copy(held[k], results[i], sems.at[k]), held[k])
+            sent.append(results[i])
+        for copy in waits:
+            copy.wait()
+        kernel(*ins, *results, *own)
+        for out in sent:
+            if not out.sent:
+                out.send()
+        for out in sent:
+            out.copy.wait()
+
+    def place_of(far):
+        return pl.BlockSpec(memory_space=pltpu.HBM if far else pltpu.VMEM)
+
     return pl.pallas_call(
-        kernel,
-        out_shape=[jax.ShapeDtypeStruct(s, d) for s, d in outs],
-        scratch_shapes=[pltpu.VMEM(s, d) for s, d in scratch],
-        compiler_params=pltpu.CompilerParams(vmem_limit_bytes=48 * 1024 * 1024),
+        wrapped,
+        out_shape=[pltpu.HBM(o[0], o[1]) if len(o) == 3 else jax.ShapeDtypeStruct(o[0], o[1]) for o in outs],
+        in_specs=[place_of(isinstance(o, Far)) for o in operands],
+        out_specs=[place_of(len(o) == 3) for o in outs],
+        scratch_shapes=[pltpu.VMEM(s, d) for s, d in scratch] + buffers + [pltpu.SemaphoreType.DMA((max(n_far, 1),))],
+        compiler_params=pltpu.CompilerParams(vmem_limit_bytes=24 * 1024 * 1024),
         cost_estimate=pl.CostEstimate(flops=flops, bytes_accessed=moved, transcendentals=0),
-    )(*operands)
+    )(*arrays)
 
 
 def swap(value, axes, of):
@@ -459,24 +608,23 @@
 CELL = ("y", "z", "xl")
 
 
-def swap_x(rows):
-    return swap(rows, BX, lambda i: i ^ 1), swap(rows, BX, lambda i: i ^ 3)
-
-
-def swap_y(rows):
+def swap_x(a, b):
+    return swap(a, BX, lambda i: i ^ 1), swap(b, BX, lambda i: i ^ 3)
+
+
+def swap_y(a, b):
     def other(c):
         return (c - 1) % 64 if c % 2 == 0 else (c + 1) % 64
 
-    return swap(rows, CELL, lambda c: c ^ 1), swap(rows, CELL, other)
+    return swap(a, CELL, lambda c: c ^ 1), swap(b, CELL, other)
 
 
 def reduce_all(partial):
     rows = partial.shape[0] // NWIDE
     pieces = lax.all_to_all(partial, WIDE, 0, 0, tiled=True)
-    (mine,) = call(sum_kernel, [((rows, 128), F32)], pieces)
-    for mask in (1, 2, 4):
-        mine = mine + swap(mine, ("z",), lambda i, mask=mask: i ^ mask)
-    spread = jnp.broadcast_to(mine[None], (NWIDE, rows, 128)).reshape(NWIDE * rows, 128)
+    (mine,) = call(functools.partial(sum_kernel, NWIDE, 8), [((8 * rows, 128), F32)], pieces)
+    mine = lax.all_to_all(mine, ("z",), 0, 0, tiled=True)
+    (spread,) = call(functools.partial(sum_kernel, 8, NWIDE), [((NWIDE * rows, 128), F32, True)], mine)
     return lax.all_to_all(spread, WIDE, 0, 0, tiled=True)
 
 
@@ -489,75 +637,72 @@
     box_x = count_x * WIDTH_X
     box_y = count_y * WIDTH_Y
     scale = 1.0 / math.sqrt(K * ATOMS * count_x * count_y)
-    px = lax.axis_index("co")
-    py = lax.axis_index("xl")
-    lower_x, upper_x = 160 - 32 * px, 128 + 32 * px
-    lower_y, upper_y = 320 - 64 * py, 256 + 64 * py
-
-    def place(index):
-        far = jnp.where(index < 240, index - 192 + lower_y, index - 240 + upper_y)
-        near = jnp.where(index < 160, index - 128 + lower_x, index - 160 + upper_x)
-        return jnp.where(index < 128, index, jnp.where(index < 192, near, far))
-
-    nb = place(neighbours)
-    odd_x, odd_y = px == 1, py == 1
-    none = jnp.full((64,), -1, jnp.int32)
-    ix = jnp.concatenate(
-        [jnp.where(odd_x, send_x[0], send_x[1]), jnp.where(odd_x, send_x[1], send_x[0]), none]
-    )[None]
-    sy = place(send_y)
-    iy = jnp.concatenate(
-        [jnp.where(odd_y, sy[0], sy[1]), none[:16], jnp.where(odd_y, sy[1], sy[0]), none[:16]]
-    )[None]
-    rows = jnp.concatenate([positions, species.astype(F32)[None], jnp.zeros((4, ATOMS), F32)], 0)
-    wave = jnp.concatenate([wave_ids.astype(F32), jnp.zeros((5, K), F32)], 0)
-    emb = jnp.pad(embedding, ((0, 0), (0, 8 - embedding.shape[1])))
     small = ((8, 128), F32)
     square = ((C, 128), F32)
     edge3 = ((3 * C, EDGES), BF16)
-
-    (strip,) = call(strip_x_kernel, [small], rows, ix)
-    xa, xb = swap_x(strip)
-    part, strip = call(strip_y_kernel, [small, small], rows, xa, xb, iy)
-    ya, yb = swap_y(strip)
+    index = ((1, 128), jnp.int32)
+    strip_32, strip_48 = ((32, 128), F32), ((48, 128), F32)
+    w1, w3, emb = radial_in.swapaxes(1, 2).astype(F32), radial_out.swapaxes(1, 2), embedding.T.astype(F32)
+
+    with_box = functools.partial
+
+    rows, ix, strip = call(strip_x_kernel, [small, index, small], Far(positions), Far(species[None]), Far(send_x))
+    xa, xb = swap_x(strip, strip)
+    part, iy, strip = call(strip_y_kernel, [small, index, small], rows, xa, xb, Far(send_y))
+    ya, yb = swap_y(strip, strip)
+    nets = (Far(w1), Far(radial_mid), Far(w3))
+    nb, geo, ylm, f_zero, a_zero, h_one, h_far, xa, xb = call(
+        with_box(first_kernel, box_x, box_y),
+        [
+            ((NB, 128), jnp.int32), ((8, NB, 128), F32, True), ((8, NB, 128), F32, True),
+            ((C, EDGES), BF16, True), ((9, C, 128), F32, True), square, square + (True,), strip_32, strip_32,
+        ],
+        rows, part, ya, yb, Far(neighbours), Far(live_slots), ix, Far(emb), *nets, Far(mixing),
+        scratch=[edge3],
+    )
+    rows_later, geo_soon, _, _ = lax.optimization_barrier((rows, geo, xa, xb))
+    xa, xb = swap_x(xa, xb)
     (cs,) = call(
-        functools.partial(waves_kernel, box_x, box_y), [((ATOMS, 2 * K), F32)], rows, wave, flops=10**8, moved=10**6
+        with_box(waves_kernel, box_x, box_y), [((ATOMS, 2 * K), F32, True)], rows_later, Far(wave_ids), flops=10**8, moved=10**6
     )
-    geo, ylm, r_zero, p_zero, f_zero, a_zero, h_one, strip = call(
-        functools.partial(first_kernel, box_x, box_y),
-        [((8, NB, 128), F32), ((8, NB, 128), F32), edge3, edge3, ((C, EDGES), BF16), ((9, C, 128), F32), square, square],
-        rows, part, ya, yb, nb, live_slots, ix, emb, radial_in, radial_mid, radial_out, mixing,
-    )
-    xa, xb = swap_x(strip)
-    r_one, p_one = call(radial_kernel, [edge3, edge3], geo, radial_in, radial_mid, radial_out, flops=10**9, moved=10**7)
-    fpart, strip = call(feature_strip_kernel, [square, square], h_one, xa, xb, iy)
-    ya, yb = swap_y(strip)
+    xa, xb, cs = lax.optimization_barrier((xa, xb, cs))
+    fpart, ya, yb = call(feature_strip_kernel, [square, strip_48, strip_48], h_one, xa, xb, iy)
+    geo_soon, _, _ = lax.optimization_barrier((geo_soon, ya, yb))
+    ya, yb = swap_y(ya, yb)
+    r_one, r_far = call(radial_kernel, [edge3, edge3 + (True,)], Far(geo_soon), *nets, flops=5 * 10**8, moved=10**7)
     f_one, a_one, h_two, charge, s_part = call(
         second_kernel,
-        [((C, EDGES), F32), ((9, C, 128), F32), square, ((KC, ATOMS), F32), ((TILES * KC, 128), F32)],
-        h_one, fpart, ya, yb, nb, ylm, r_one, cs, mixing, read_hidden, w_charge,
+        [((C, EDGES), F32, True), ((9, C, 128), F32, True), square + (True,), ((KC, ATOMS), F32, True), ((TILES * KC, 128), F32)],
+        h_one, fpart, ya, yb, nb, Far(ylm), r_one, Far(cs, True), Far(mixing, True), Far(w_charge),
         scratch=[square],
     )
+    geo_later, _ = lax.optimization_barrier((geo, s_part))
+    p_one, oh = call(
+        slope_one_kernel, [edge3 + (True,), ((TABLE, EDGES), BF16, True)], Far(geo_later), *nets, Far(nb), flops=10**9, moved=10**7
+    )
     s_all = reduce_all(s_part)
-    energy, gpos, gown, gpart, gy, t_one = call(
-        functools.partial(ewald_kernel, box_x, box_y, scale),
-        [((1, 128), F32), small, square, square, square, ((9, NB, 128), F32)],
-        s_all, spectral, cs, wave, charge, h_one, h_two, a_one, ylm, r_one, p_one, f_one, nb, iy, mixing,
-        read_first[:, None], read_hidden, read_last[:, None], w_charge,
-        scratch=[((9, C, 128), F32), ((C, EDGES), BF16), ((TABLE, EDGES), BF16)],
+    late = lambda array: Far(array, True)
+    energy, gpos, gown, gpart, ya, yb, t_one = call(
+        with_box(ewald_kernel, box_x, box_y, scale),
+        [((1, 128), F32), small, square, square, strip_48, strip_48, ((9, NB, 128), F32)],
+        Far(s_all), Far(spectral), Far(cs), Far(wave_ids), Far(charge), late(h_far), late(h_two), late(a_one), late(ylm), late(r_far),
+        late(p_one), late(f_one), late(oh), late(mixing), late(read_first[None]), late(read_last[None]), late(read_hidden), late(w_charge),
+        scratch=[((9, C, 128), F32), ((C, EDGES), BF16), ((2 * ATOMS, K), BF16)],
     )
-    ya, yb = swap_y(gy)
-    gown, gpart = call(return_y_kernel, [square, square], gown, gpart, ya, yb, iy)
-    xa, xb = swap_x(gpart)
+    geo_last, _, _ = lax.optimization_barrier((geo, ya, yb))
+    ya, yb = swap_y(ya, yb)
+    r_zero, p_zero = call(slope_zero_kernel, [edge3, edge3], Far(geo_last), *nets, flops=10**9, moved=10**7)
+    gown, xa, xb = call(return_features_kernel, [square, strip_32, strip_32], gown, gpart, ya, yb, iy)
+    xa, xb = swap_x(xa, xb)
     own, part, gy = call(
         last_kernel,
         [small, small, small],
-        gown, xa, xb, ix, mixing, a_zero, r_zero, p_zero, f_zero, ylm, t_one, geo, nb, gpos,
-        scratch=[((9, C, 128), F32), ((9, NB, 128), F32), ((TABLE, EDGES), BF16), ((16, EDGES), F32)],
+        gown, xa, xb, ix, mixing, a_zero, r_zero, p_zero, f_zero, ylm, t_one, geo, oh, gpos,
+        scratch=[((9, C, 128), F32), ((9, NB, 128), F32), ((16, EDGES), F32)],
     )
-    ya, yb = swap_y(gy)
+    ya, yb = swap_y(gy, gy)
     own, part = call(return_y_kernel, [small, small], own, part, ya, yb, iy)
-    xa, xb = swap_x(part)
+    xa, xb = swap_x(part, part)
     (forces,) = call(final_kernel, [((3, ATOMS), F32)], own, xa, xb, ix)
     return energy[0], forces
 

time: 164 us -> 135 us (0.82)
  local copies, waits for them, and re-layouts: 22.5 us -> 0.83 us
  waiting for transfers between devices: 38.5 us -> 18.2 us
  blocking collectives: 15.3 us -> 27.3 us
  Pallas kernels: 41.4 us -> 47.5 us
  starting transfers between devices: 39.5 us -> 36.7 us
  other arithmetic: 4.46 us -> 2.55 us
    unnamed x63 -> x16, local copies, waits for them, and re-layouts: 18.8 us -> 0.83 us
    ppermute x19 -> x16, waiting for transfers between devices: 30.1 us -> 13.9 us  [swap(): return lax.ppermute(value, axes, [(i, of(i)) for i in range(count)])]
    all_to_all x0 -> x1, blocking collectives: none -> 11.8 us  [reduce_all(): mine = lax.all_to_all(mine, ('z',), 0, 0, tiled=True)]
    pallas_call x13 -> x16, Pallas kernels: 41.4 us -> 47.5 us  [call(): pl.pallas_call(wrapped, out_shape=[pltpu.HBM(o[0], o[1]) if len(o) == 3 e...]
    all_to_all x1, waiting for transfers between devices: 8.39 us -> 4.39 us  [reduce_all(): return lax.all_to_all(spread, WIDE, 0, 0, tiled=True)]
    broadcast_in_dim x5 -> x0, local copies, waits for them, and re-layouts: 3.58 us -> none  [the longest x1 1.38 us: body(): read_first[:, None]]
    all_to_all x1, starting transfers between devices: 8.06 us -> 5.77 us  [reduce_all(): return lax.all_to_all(spread, WIDE, 0, 0, tiled=True)]
    select_n x4 -> x0, other arithmetic: 2.16 us -> none  [the longest x2 1.4 us: place(): return jnp.where(index < 128, index, jnp.where(index < 192, near, far))]
  transfers between devices with their start and end apart: 20 -> 17, of which waited for: 10 -> 6; matrix products, arithmetic and copies ran while one was open for 5% -> 2% of each run, Pallas kernels for 5% -> 13%
where the time goes in v2:
time: 135 us; the launch traced here: 134 us
  Pallas kernels  47.5 us (35%)
  starting transfers between devices  36.7 us (27%)
  blocking collectives  27.3 us (20%)
  waiting for transfers between devices  18.2 us (13%)
  other arithmetic  2.55 us (2%)
    pallas_call x16, Pallas kernels, call(): pl.pallas_call(wrapped, out_shape=[pltpu.HBM(o[0], o[1]) if len(o) == 3 e...  47.5 us
    ppermute x16, starting transfers between devices, swap(): return lax.ppermute(value, axes, [(i, of(i)) for i in range(count)])  30.9 us
    all_to_all x1, blocking collectives, reduce_all(): pieces = lax.all_to_all(partial, WIDE, 0, 0, tiled=True)  15.4 us
    ppermute x16, waiting for transfers between devices, swap(): return lax.ppermute(value, axes, [(i, of(i)) for i in range(count)])  13.9 us
    all_to_all x1, blocking collectives, reduce_all(): mine = lax.all_to_all(mine, ('z',), 0, 0, tiled=True)  11.8 us
    all_to_all x1, starting transfers between devices, reduce_all(): return lax.all_to_all(spread, WIDE, 0, 0, tiled=True)  5.77 us
    all_to_all x1, waiting for transfers between devices, reduce_all(): return lax.all_to_all(spread, WIDE, 0, 0, tiled=True)  4.39 us
  transfers between devices with their start and end apart: 17, of which 6 were waited for; matrix products, arithmetic and copies ran while one was open for 2% of the time, Pallas kernels for 13%

profile of v2, /device:TPU:1, one launch (start us, length us, event | category | flops | bytes accessed | tf_op | source)
XLA Modules:
  0.0 134.2 jit_solution(13962520755715080165)
XLA Ops:
  1.6 4.2 %collective-permute-start.1 = (f32[8,128]{1,0:T(8,128)S(1)}, f32[8,128]{1,0:T(8,128)S(1)}, u32[]{:S(2)}, u32[]{:S(2)}) collective-permute-start(f32[8,128]{1,0:T(8,128)S(1)} %get-tuple-element.55), channel_id=1, source_target_pairs={{0,192},{64,128},{128,64},{192,0},{1,193},{65,129},{129,65},{193,1... | collective-permute-start | bytes 12296 | tf_op jit(solution)/shard_map/ppermute | solution.py:604
  8.1 9.3 %collective-permute-start.3 = (f32[8,128]{1,0:T(8,128)S(1)}, f32[8,128]{1,0:T(8,128)S(1)}, u32[]{:S(2)}, u32[]{:S(2)}) collective-permute-start(f32[8,128]{1,0:T(8,128)S(1)} %get-tuple-element.57), channel_id=1, source_target_pairs={{0,63},{1,2},{2,1},{3,4},{4,3},{5,6},{6,5},{7,8},{8,7},{9,10},{10,... | collective-permute-start | bytes 12296 | tf_op jit(solution)/shard_map/ppermute | solution.py:604
  19.9 5.6 %shard_map.178 = (s32[24,128]{1,0:T(8,128)S(1)}, f32[8,24,128]{2,1,0:T(8,128)}, f32[8,24,128]{2,1,0:T(8,128)}, bf16[128,3072]{1,0:T(8,128)(2,1)}, f32[9,128,128]...) custom-call(f32[8,128]{1,0:T(8,128)S(1)} %get-tuple-element.63.refs_, ...), custom_call_target="tpu_custom_call" | custom-call | tf_op jit(solution)/shard_map/pallas_call | solution.py:589
  25.5 1.9 %collective-permute-start.4 = (f32[32,128]{1,0:T(8,128)S(1)}, f32[32,128]{1,0:T(8,128)S(1)}, u32[]{:S(2)}, u32[]{:S(2)}) collective-permute-start(f32[32,128]{1,0:T(8,128)S(1)} %get-tuple-element.60), channel_id=1, source_target_pairs={{0,64},{64,0},{128,192},{192,128},{1,65},{65,1},{129,193},{193,129... | collective-permute-start | bytes 49160 | tf_op jit(solution)/shard_map/ppermute | solution.py:604
  27.4 2.4 %collective-permute-start.5 = (f32[32,128]{1,0:T(8,128)S(1)}, f32[32,128]{1,0:T(8,128)S(1)}, u32[]{:S(2)}, u32[]{:S(2)}) collective-permute-start(f32[32,128]{1,0:T(8,128)S(1)} %get-tuple-element.61), channel_id=1, source_target_pairs={{0,192},{64,128},{128,64},{192,0},{1,193},{65,129},{129,65},{193,1... | collective-permute-start | bytes 49160 | tf_op jit(solution)/shard_map/ppermute | solution.py:604
  29.9 2.7 %shard_map.179.refs_7_.refs_2_ = f32[128,2048]{1,0:T(8,128)} custom-call(f32[8,128]{1,0:T(8,128)S(1)} %get-tuple-element.63.refs_0_, s32[3,1024]{1,0:T(4,128)} %refs_3_.3), custom_call_target="tpu_custom_call" | custom-call | flops 100000000 | bytes 1000000 | tf_op jit(solution)/shard_map/pallas_call | solution.py:589
  33.1 3.5 %collective-permute-start.7 = (f32[48,128]{1,0:T(8,128)S(1)}, f32[48,128]{1,0:T(8,128)S(1)}, u32[]{:S(2)}, u32[]{:S(2)}) collective-permute-start(f32[48,128]{1,0:T(8,128)S(1)} %get-tuple-element.69), channel_id=1, source_target_pairs={{0,63},{1,2},{2,1},{3,4},{4,3},{5,6},{6,5},{7,8},{8,7},{9,10},{10,... | collective-permute-start | bytes 73736 | tf_op jit(solution)/shard_map/ppermute | solution.py:604
  36.6 4.3 %shard_map.181 = (bf16[384,3072]{1,0:T(8,128)(2,1)S(1)}, bf16[384,3072]{1,0:T(8,128)(2,1)}) custom-call(f32[8,24,128]{2,1,0:T(8,128)} %get-tuple-element.95.refs_0_.refs_11_, f32[2,8,64]{2,1,0:T(8,128)} %convert_bitcast_fusion.refs_8_.refs_1_, bf16[2,64,64]{2,1,0:T(8,128)(2,1)} %refs_2_.7, bf16[2,64,384]{2,1,0:T(8,128)(2,1)} %bitcast.22), custom_call_target="tpu_custom_call" | custom-call | flops 500000000 | bytes 10000000 | tf_op jit(solution)/shard_map/pallas_call | solution.py:589
  40.9 5.2 %shard_map.182 = (f32[128,3072]{1,0:T(8,128)}, f32[9,128,128]{2,1,0:T(8,128)}, f32[128,128]{1,0:T(8,128)}, f32[64,128]{1,0:T(8,128)}, f32[1024,128]{1,0:T(8,128)S(1)}) custom-call(f32[128,128]{1,0:T(8,128)S(1)} %get-tuple-element.59.refs_0_, f32[128,128]{1,0:T(8,128)S(1)} %get-tuple-element.67.refs_1_, f32[48,128]{1,0:T(8,128)S(1)} %collective-permute-done.6.refs_2_, ...), custom_call_target="tpu_custom_call" | custom-call | tf_op jit(solution)/shard_map/pallas_call | solution.py:589
  46.2 15.4 %all_to_all.33 = f32[32,32,128]{2,1,0:T(8,128)S(1)} all-to-all(f32[32,32,128]{2,1,0:T(8,128)S(1)} %bitcast.18), channel_id=1, replica_groups=mesh['xh'=2,'co'=2,'y'=4,'z'=8,'xl'=2] {'xh','co','y','xl'}, dimensions={0} | all-to-all | bytes 1048576 | tf_op jit(solution)/shard_map/all_to_all | solution.py:624
  61.6 11.8 %all_to_all.34 = f32[8,32,128]{2,1,0:T(8,128)S(1)} all-to-all(f32[8,32,128]{2,1,0:T(8,128)S(1)} %bitcast.16), channel_id=1, replica_groups=mesh['xh'=2,'co'=2,'y'=4,'z'=8,'xl'=2] {'z'}, dimensions={0} | all-to-all | bytes 262144 | tf_op jit(solution)/shard_map/all_to_all | solution.py:626
  74.4 5.8 %all-to-all-start.2 = ((f32[32,32,128]{2,1,0:T(8,128)}), f32[32,32,128]{2,1,0:T(8,128)S(1)}, u32[]{:S(2)}, u32[]{:S(2)}) async-start(f32[32,32,128]{2,1,0:T(8,128)} %bitcast.20), calls=%async_computation.2 | async-start | bytes 1048576 | tf_op jit(solution)/shard_map/all_to_all | solution.py:628
  80.1 6.7 %shard_map.185 = (bf16[384,3072]{1,0:T(8,128)(2,1)}, bf16[384,3072]{1,0:T(8,128)(2,1)}) custom-call(f32[8,24,128]{2,1,0:T(8,128)} %get-tuple-element.95.refs_0_.refs_11_, f32[2,8,64]{2,1,0:T(8,128)} %convert_bitcast_fusion.refs_8_.refs_1_, bf16[2,64,64]{2,1,0:T(8,128)(2,1)} %refs_2_.7, bf16[2,64,384]{2,1,0:T(8,128)(2,1)} %bitcast.23, s32[24,128]{1,0:T(8,128)} %copy-done.6), custom_call_target="tpu_custom_call" | custom-call | flops 1000000000 | bytes 10000000 | tf_op jit(solution)/shard_map/pallas_call | solution.py:589
  86.8 4.4 %all-to-all-done.2 = f32[32,32,128]{2,1,0:T(8,128)S(1)} async-done(((f32[32,32,128]{2,1,0:T(8,128)}), f32[32,32,128]{2,1,0:T(8,128)S(1)}, u32[]{:S(2)}, u32[]{:S(2)}) %all-to-all-start.2) | async-done | bytes 524320 | tf_op jit(solution)/shard_map/all_to_all | solution.py:628
  92.0 9.2 %shard_map.186 = (f32[1,128]{1,0:T(1,128)}, f32[8,128]{1,0:T(8,128)S(1)}, f32[128,128]{1,0:T(8,128)S(1)}, f32[128,128]{1,0:T(8,128)S(1)}, f32[48,128]{1,0:T(8,12...) custom-call(f32[1024,128]{1,0:T(8,128)} %bitcast.19, f32[64,1024]{1,0:T(8,128)} %refs_1_.3, ...), custom_call_target="tpu_custom_call" | custom-call | tf_op jit(solution)/shard_map/pallas_call | solution.py:589
  101.7 1.4 %collective-permute-start.9 = (f32[48,128]{1,0:T(8,128)S(1)}, f32[48,128]{1,0:T(8,128)S(1)}, u32[]{:S(2)}, u32[]{:S(2)}) collective-permute-start(f32[48,128]{1,0:T(8,128)S(1)} %get-tuple-element.90), channel_id=1, source_target_pairs={{0,63},{1,2},{2,1},{3,4},{4,3},{5,6},{6,5},{7,8},{8,7},{9,10},{10,... | collective-permute-start | bytes 73736 | tf_op jit(solution)/shard_map/ppermute | solution.py:604
  104.1 4.5 %collective-permute-done.9.refs_3_ = f32[48,128]{1,0:T(8,128)S(1)} collective-permute-done((f32[48,128]{1,0:T(8,128)S(1)}, f32[48,128]{1,0:T(8,128)S(1)}, u32[]{:S(2)}, u32[]{:S(2)}) %collective-permute-start.9) | collective-permute-done | bytes 24608 | tf_op jit(solution)/shard_map/ppermute | solution.py:604
  109.0 1.8 %collective-permute-start.10 = (f32[32,128]{1,0:T(8,128)S(1)}, f32[32,128]{1,0:T(8,128)S(1)}, u32[]{:S(2)}, u32[]{:S(2)}) collective-permute-start(f32[32,128]{1,0:T(8,128)S(1)} %get-tuple-element.92), channel_id=1, source_target_pairs={{0,64},{64,0},{128,192},{192,128},{1,65},{65,1},{129,193},{193,129... | collective-permute-start | bytes 49160 | tf_op jit(solution)/shard_map/ppermute | solution.py:604
  110.8 1.6 %collective-permute-start.11 = (f32[32,128]{1,0:T(8,128)S(1)}, f32[32,128]{1,0:T(8,128)S(1)}, u32[]{:S(2)}, u32[]{:S(2)}) collective-permute-start(f32[32,128]{1,0:T(8,128)S(1)} %get-tuple-element.93), channel_id=1, source_target_pairs={{0,192},{64,128},{128,64},{192,0},{1,193},{65,129},{129,65},{193,1... | collective-permute-start | bytes 49160 | tf_op jit(solution)/shard_map/ppermute | solution.py:604
  112.5 4.4 %shard_map.188 = (bf16[384,3072]{1,0:T(8,128)(2,1)S(1)}, bf16[384,3072]{1,0:T(8,128)(2,1)S(1)}) custom-call(f32[8,24,128]{2,1,0:T(8,128)} %get-tuple-element.95.refs_0_.refs_11_, f32[2,8,64]{2,1,0:T(8,128)} %convert_bitcast_fusion.refs_8_.refs_1_, bf16[2,64,64]{2,1,0:T(8,128)(2,1)} %refs_2_.7, bf16[2,64,384]{2,1,0:T(8,128)(2,1)} %bitcast.24), custom_call_target="tpu_custom_call" | custom-call | flops 1000000000 | bytes 10000000 | tf_op jit(solution)/shard_map/pallas_call | solution.py:589
  116.9 4.7 %shard_map.189 = (f32[8,128]{1,0:T(8,128)S(1)}, f32[8,128]{1,0:T(8,128)S(1)}, f32[8,128]{1,0:T(8,128)S(1)}) custom-call(f32[128,128]{1,0:T(8,128)S(1)} %get-tuple-element.91.refs_0_, f32[32,128]{1,0:T(8,128)S(1)} %collective-permute-done.10.refs_1_, f32[32,128]{1,0:T(8,128)S(1)} %collective-permute-done.11.refs_2_, ...), custom_call_target="tpu_custom_call" | custom-call | tf_op jit(solution)/shard_map/pallas_call | solution.py:589
  122.9 5.5 %collective-permute-done.13.refs_3_ = f32[8,128]{1,0:T(8,128)S(1)} collective-permute-done((f32[8,128]{1,0:T(8,128)S(1)}, f32[8,128]{1,0:T(8,128)S(1)}, u32[]{:S(2)}, u32[]{:S(2)}) %collective-permute-start.13) | collective-permute-done | bytes 4128 | tf_op jit(solution)/shard_map/ppermute | solution.py:604
  128.6 2.9 %collective-permute-start.15 = (f32[8,128]{1,0:T(8,128)S(1)}, f32[8,128]{1,0:T(8,128)S(1)}, u32[]{:S(2)}, u32[]{:S(2)}) collective-permute-start(f32[8,128]{1,0:T(8,128)S(1)} %get-tuple-element.105), channel_id=1, source_target_pairs={{0,192},{64,128},{128,64},{192,0},{1,193},{65,129},{129,65},{193,1... | collective-permute-start | bytes 12296 | tf_op jit(solution)/shard_map/ppermute | solution.py:604
  131.5 1.7 %collective-permute-done.15.refs_2_ = f32[8,128]{1,0:T(8,128)S(1)} collective-permute-done((f32[8,128]{1,0:T(8,128)S(1)}, f32[8,128]{1,0:T(8,128)S(1)}, u32[]{:S(2)}, u32[]{:S(2)}) %collective-permute-start.15) | collective-permute-done | bytes 4128 | tf_op jit(solution)/shard_map/ppermute | solution.py:604
  (46 shorter events, 12.0 us)
Async XLA Ops:
  1.6 5.5 %collective-permute-start.1 = (f32[8,128]{1,0:T(8,128)S(1)}, f32[8,128]{1,0:T(8,128)S(1)}, u32[]{:S(2)}, u32[]{:S(2)}) collective-permute-start(f32[8,128]{1,0:T(8,128)S(1)} %get-tuple-element.55), channel_id=1, source_target_pairs={{0,192},{64,128},{128,64},{192,0},{1,193},{65,129},{129,65},{193,1... | collective-permute-start | bytes 12296 | tf_op jit(solution)/shard_map/ppermute | solution.py:604
  5.8 1.3 collective-permute-start
  8.1 10.6 %collective-permute-start.3 = (f32[8,128]{1,0:T(8,128)S(1)}, f32[8,128]{1,0:T(8,128)S(1)}, u32[]{:S(2)}, u32[]{:S(2)}) collective-permute-start(f32[8,128]{1,0:T(8,128)S(1)} %get-tuple-element.57), channel_id=1, source_target_pairs={{0,63},{1,2},{2,1},{3,4},{4,3},{5,6},{6,5},{7,8},{8,7},{9,10},{10,... | collective-permute-start | bytes 12296 | tf_op jit(solution)/shard_map/ppermute | solution.py:604
  17.4 2.5 %collective-permute-start.2 = (f32[8,128]{1,0:T(8,128)S(1)}, f32[8,128]{1,0:T(8,128)S(1)}, u32[]{:S(2)}, u32[]{:S(2)}) collective-permute-start(f32[8,128]{1,0:T(8,128)S(1)} %get-tuple-element.57), channel_id=1, source_target_pairs={{0,1},{1,0},{2,3},{3,2},{4,5},{5,4},{6,7},{7,6},{8,9},{9,8},{10,11... | collective-permute-start | bytes 12296 | tf_op jit(solution)/shard_map/ppermute | solution.py:604
  25.5 20.6 %copy-start.6 = (s32[24,128]{1,0:T(8,128)}, s32[24,128]{1,0:T(8,128)S(1)}, u32[]{:S(2)}) copy-start(s32[24,128]{1,0:T(8,128)S(1)} %get-tuple-element.70.refs_4_) | copy-start | bytes 36868
  25.5 7.1 %collective-permute-start.4 = (f32[32,128]{1,0:T(8,128)S(1)}, f32[32,128]{1,0:T(8,128)S(1)}, u32[]{:S(2)}, u32[]{:S(2)}) collective-permute-start(f32[32,128]{1,0:T(8,128)S(1)} %get-tuple-element.60), channel_id=1, source_target_pairs={{0,64},{64,0},{128,192},{192,128},{1,65},{65,1},{129,193},{193,129... | collective-permute-start | bytes 49160 | tf_op jit(solution)/shard_map/ppermute | solution.py:604
  27.4 5.2 %collective-permute-start.5 = (f32[32,128]{1,0:T(8,128)S(1)}, f32[32,128]{1,0:T(8,128)S(1)}, u32[]{:S(2)}, u32[]{:S(2)}) collective-permute-start(f32[32,128]{1,0:T(8,128)S(1)} %get-tuple-element.61), channel_id=1, source_target_pairs={{0,192},{64,128},{128,64},{192,0},{1,193},{65,129},{129,65},{193,1... | collective-permute-start | bytes 49160 | tf_op jit(solution)/shard_map/ppermute | solution.py:604
  33.0 7.9 %collective-permute-start.6 = (f32[48,128]{1,0:T(8,128)S(1)}, f32[48,128]{1,0:T(8,128)S(1)}, u32[]{:S(2)}, u32[]{:S(2)}) collective-permute-start(f32[48,128]{1,0:T(8,128)S(1)} %get-tuple-element.68), channel_id=1, source_target_pairs={{0,1},{1,0},{2,3},{3,2},{4,5},{5,4},{6,7},{7,6},{8,9},{9,8},{10,11... | collective-permute-start | bytes 73736 | tf_op jit(solution)/shard_map/ppermute | solution.py:604
  33.1 7.8 %collective-permute-start.7 = (f32[48,128]{1,0:T(8,128)S(1)}, f32[48,128]{1,0:T(8,128)S(1)}, u32[]{:S(2)}, u32[]{:S(2)}) collective-permute-start(f32[48,128]{1,0:T(8,128)S(1)} %get-tuple-element.69), channel_id=1, source_target_pairs={{0,63},{1,2},{2,1},{3,4},{4,3},{5,6},{6,5},{7,8},{8,7},{9,10},{10,... | collective-permute-start | bytes 73736 | tf_op jit(solution)/shard_map/ppermute | solution.py:604
  74.4 16.9 %all-to-all-start.2 = ((f32[32,32,128]{2,1,0:T(8,128)}), f32[32,32,128]{2,1,0:T(8,128)S(1)}, u32[]{:S(2)}, u32[]{:S(2)}) async-start(f32[32,32,128]{2,1,0:T(8,128)} %bitcast.20), calls=%async_computation.2 | async-start | bytes 1048576 | tf_op jit(solution)/shard_map/all_to_all | solution.py:628
  92.0 24.8 %copy-start.4 = (f32[9,128,128]{2,1,0:T(8,128)S(1)}, f32[9,128,128]{2,1,0:T(8,128)}, u32[]{:S(2)}) copy-start(f32[9,128,128]{2,1,0:T(8,128)} %get-tuple-element.94.refs_5_) | copy-start | bytes 1769476
  101.3 15.6 %copy-start = (bf16[384,3072]{1,0:T(8,128)(2,1)S(1)}, bf16[384,3072]{1,0:T(8,128)(2,1)}, u32[]{:S(2)}) copy-start(bf16[384,3072]{1,0:T(8,128)(2,1)} %get-tuple-element.85.refs_12_) | copy-start | bytes 7077892
  101.3 15.6 %copy-start.1 = (bf16[2,128,384]{2,1,0:T(8,128)(2,1)S(1)}, bf16[2,128,384]{2,1,0:T(8,128)(2,1)}, u32[]{:S(2)}) copy-start(bf16[2,128,384]{2,1,0:T(8,128)(2,1)} %refs_4_.3) | copy-start | bytes 589828
  101.3 15.6 %copy-start.2 = (f32[8,24,128]{2,1,0:T(8,128)S(1)}, f32[8,24,128]{2,1,0:T(8,128)}, u32[]{:S(2)}) copy-start(f32[8,24,128]{2,1,0:T(8,128)} %get-tuple-element.71.refs_5_.refs_8_.refs_9_) | copy-start | bytes 294916
  101.3 15.6 %copy-start.3 = (bf16[128,3072]{1,0:T(8,128)(2,1)S(1)}, bf16[128,3072]{1,0:T(8,128)(2,1)}, u32[]{:S(2)}) copy-start(bf16[128,3072]{1,0:T(8,128)(2,1)} %get-tuple-element.98.refs_8_) | copy-start | bytes 2359300
  101.3 15.6 %copy-start.5 = (f32[8,24,128]{2,1,0:T(8,128)S(1)}, f32[8,24,128]{2,1,0:T(8,128)}, u32[]{:S(2)}) copy-start(f32[8,24,128]{2,1,0:T(8,128)} %get-tuple-element.95.refs_0_.refs_11_) | copy-start | bytes 294916
  101.3 2.8 %collective-permute-start.8 = (f32[48,128]{1,0:T(8,128)S(1)}, f32[48,128]{1,0:T(8,128)S(1)}, u32[]{:S(2)}, u32[]{:S(2)}) collective-permute-start(f32[48,128]{1,0:T(8,128)S(1)} %get-tuple-element.89), channel_id=1, source_target_pairs={{0,1},{1,0},{2,3},{3,2},{4,5},{5,4},{6,7},{7,6},{8,9},{9,8},{10,11... | collective-permute-start | bytes 73736 | tf_op jit(solution)/shard_map/ppermute | solution.py:604
  101.7 6.9 %collective-permute-start.9 = (f32[48,128]{1,0:T(8,128)S(1)}, f32[48,128]{1,0:T(8,128)S(1)}, u32[]{:S(2)}, u32[]{:S(2)}) collective-permute-start(f32[48,128]{1,0:T(8,128)S(1)} %get-tuple-element.90), channel_id=1, source_target_pairs={{0,63},{1,2},{2,1},{3,4},{4,3},{5,6},{6,5},{7,8},{8,7},{9,10},{10,... | collective-permute-start | bytes 73736 | tf_op jit(solution)/shard_map/ppermute | solution.py:604
  109.0 7.9 %collective-permute-start.10 = (f32[32,128]{1,0:T(8,128)S(1)}, f32[32,128]{1,0:T(8,128)S(1)}, u32[]{:S(2)}, u32[]{:S(2)}) collective-permute-start(f32[32,128]{1,0:T(8,128)S(1)} %get-tuple-element.92), channel_id=1, source_target_pairs={{0,64},{64,0},{128,192},{192,128},{1,65},{65,1},{129,193},{193,129... | collective-permute-start | bytes 49160 | tf_op jit(solution)/shard_map/ppermute | solution.py:604
  110.8 6.0 %collective-permute-start.11 = (f32[32,128]{1,0:T(8,128)S(1)}, f32[32,128]{1,0:T(8,128)S(1)}, u32[]{:S(2)}, u32[]{:S(2)}) collective-permute-start(f32[32,128]{1,0:T(8,128)S(1)} %get-tuple-element.93), channel_id=1, source_target_pairs={{0,192},{64,128},{128,64},{192,0},{1,193},{65,129},{129,65},{193,1... | collective-permute-start | bytes 49160 | tf_op jit(solution)/shard_map/ppermute | solution.py:604
  121.6 6.8 %collective-permute-start.13 = (f32[8,128]{1,0:T(8,128)S(1)}, f32[8,128]{1,0:T(8,128)S(1)}, u32[]{:S(2)}, u32[]{:S(2)}) collective-permute-start(f32[8,128]{1,0:T(8,128)S(1)} %get-tuple-element.103), channel_id=1, source_target_pairs={{0,63},{1,2},{2,1},{3,4},{4,3},{5,6},{6,5},{7,8},{8,7},{9,10},{10,... | collective-permute-start | bytes 12296 | tf_op jit(solution)/shard_map/ppermute | solution.py:604
  122.9 5.5 %collective-permute-start.12 = (f32[8,128]{1,0:T(8,128)S(1)}, f32[8,128]{1,0:T(8,128)S(1)}, u32[]{:S(2)}, u32[]{:S(2)}) collective-permute-start(f32[8,128]{1,0:T(8,128)S(1)} %get-tuple-element.103), channel_id=1, source_target_pairs={{0,1},{1,0},{2,3},{3,2},{4,5},{5,4},{6,7},{7,6},{8,9},{9,8},{10,11... | collective-permute-start | bytes 12296 | tf_op jit(solution)/shard_map/ppermute | solution.py:604
  128.6 4.6 %collective-permute-start.15 = (f32[8,128]{1,0:T(8,128)S(1)}, f32[8,128]{1,0:T(8,128)S(1)}, u32[]{:S(2)}, u32[]{:S(2)}) collective-permute-start(f32[8,128]{1,0:T(8,128)S(1)} %get-tuple-element.105), channel_id=1, source_target_pairs={{0,192},{64,128},{128,64},{192,0},{1,193},{65,129},{129,65},{193,1... | collective-permute-start | bytes 12296 | tf_op jit(solution)/shard_map/ppermute | solution.py:604
  131.5 1.8 %collective-permute-start.14 = (f32[8,128]{1,0:T(8,128)S(1)}, f32[8,128]{1,0:T(8,128)S(1)}, u32[]{:S(2)}, u32[]{:S(2)}) collective-permute-start(f32[8,128]{1,0:T(8,128)S(1)} %get-tuple-element.105), channel_id=1, source_target_pairs={{0,64},{64,0},{128,192},{192,128},{1,65},{65,1},{129,193},{193,129... | collective-permute-start | bytes 12296 | tf_op jit(solution)/shard_map/ppermute | solution.py:604
  (1 other events, 0.8 us)

commit v3 on v2

--- a/solution.py
+++ b/solution.py
@@ -25,6 +25,7 @@
 EDGES = NB * ATOMS
 TABLE = 384
 NBASIS = 8
+BLOCKS = 4
 K = 1024
 KC = 64
 TILES = 2 * K // 128
@@ -137,7 +138,9 @@
 def radial(layer, geo_ref, w1_ref, w2_ref, w3_ref, r_ref, p_ref):
     w1 = w1_ref[layer].astype(BF16)
     w2 = w2_ref[layer]
-    w3 = w3_ref[layer].astype(F32).T.astype(BF16)
+    w3 = w3_ref[layer]
+    if w3.shape[0] < w3.shape[1]:
+        w3 = w3.astype(F32).T.astype(BF16)
     spacing = CUTOFF / (NBASIS - 1)
     centre = lax.broadcasted_iota(jnp.int32, (NBASIS, WIDE_TILE), 0).astype(F32) * spacing
     for g in range(EDGES // WIDE_TILE):
@@ -193,15 +196,26 @@
     return jnp.where(group == 0, got[0], jnp.where(group == 1, got[1], got[2]))
 
 
+def fetch_kernel(nb_ref, live_ref, emb_ref, w1_ref, w2_ref, w3_ref, mix_ref, wave_ref, nb_out, live_out, emb_out, w1_out, w2_out, w3_out, mix_out, wave_out):
+    wave_out[...] = jnp.concatenate([wave_ref[...].astype(F32), jnp.zeros((5, K), F32)], 0)
+    nb_out[...] = place(nb_ref[...])
+    live_out[...] = live_ref[...].astype(F32)
+    emb_out[...] = jnp.concatenate([emb_ref[...], jnp.zeros((8 - emb_ref.shape[0], C), F32)], 0)
+    w1_out[...] = w1_ref[...]
+    w2_out[...] = w2_ref[...]
+    mix_out[...] = mix_ref[...]
+    for layer in range(2):
+        w3_out[layer] = w3_ref[layer].astype(F32).T.astype(BF16)
+
+
 def first_kernel(
-    box_x, box_y, rows_ref, part_ref, a_in, b_in, raw_ref, live_ref, ix_ref, emb_ref, w1_ref, w2_ref,
-    w3_ref, mix_ref, nb_ref, geo_out, y_out, f_out, a_out, h_ref, h_out, xa_ref, xb_ref, r_ref,
+    box_x, box_y, rows_ref, part_ref, a_in, b_in, nb_ref, live_ref, ix_ref, emb_ref, w1_ref, w2_ref,
+    w3_ref, mix_ref, geo_ref, y_ref, f_out, r_out, a_ref, h_ref, xa_ref, xb_ref,
 ):
-    geo_ref, y_ref, f_ref, a_ref = geo_out.ref, y_out.ref, f_out.ref, a_out.ref
+    f_ref, r_ref = f_out.ref, r_out.ref
     own = rows_ref[...]
     tables = [own, part_ref[...], merge(a_in[...], b_in[...], 64)]
-    nb = place(raw_ref[...])
-    nb_ref[...] = nb
+    nb = nb_ref[...]
     lane, group = nb & 127, nb >> 7
 
     def gathered(row):
@@ -225,7 +239,7 @@
     square = step_x * step_x + step_y * step_y + step_z * step_z
     shifted = square + SOFTEN
     inverse = lax.rsqrt(shifted)
-    live = live_ref[...].astype(F32)
+    live = live_ref[...]
     inside = jnp.maximum(1.0 - square * (1.0 / (CUTOFF * CUTOFF)), 0.0)
     env = inside * inside * live
     ux, uy, uz = step_x * (1.0 / CUTOFF), step_y * (1.0 / CUTOFF), step_z * (1.0 / CUTOFF)
@@ -246,46 +260,62 @@
     y_ref[7] = (2.0 * uz * uz - ux * ux - uy * uy) * (1.0 / ROOT_THREE)
 
     geo_ref[7] = gathered(3)
-    geo_out.send()
-    y_out.send()
-    emb = jnp.concatenate([emb_ref[...], jnp.zeros((8 - emb_ref.shape[0], C), F32)], 0).astype(BF16)
+    emb = emb_ref[...].astype(BF16)
     kinds = lax.broadcasted_iota(jnp.int32, (8, WIDE_TILE), 0).astype(F32)
     for g in range(EDGES // WIDE_TILE):
         cols = slice(g * WIDE_TILE, (g + 1) * WIDE_TILE)
         f_ref[:, cols] = dot(emb, (kinds == flat(geo_ref, 7, g)).astype(F32).astype(BF16), TN).astype(BF16)
     f_out.send()
     radial(0, geo_ref, w1_ref, w2_ref, w3_ref, r_ref, None)
+    r_out.send()
 
     def get_f(r0):
         return lambda n: f_ref[pl.ds(r0, 16), n * 128 : (n + 1) * 128].astype(F32)
 
     aggregate(r_ref, get_f, y_ref, a_ref)
-    a_out.send()
     h_zero = dot(emb, (kinds[:, :128] == own[3:4]).astype(F32).astype(BF16), TN)
     h_one = h_zero + dot(mix_ref[0], invariants(a_ref))
     h_ref[...] = h_one
-    h_out.ref[...] = h_one
-    h_out.send()
     send_rows(pick(h_one, ix_ref[...]), 32, 32, xa_ref, xb_ref)
 
 
-def radial_kernel(geo_ref, w1_ref, w2_ref, w3_ref, r_ref, r_out):
+def radial_kernel(geo_ref, w1_ref, w2_ref, w3_ref, r_ref):
     radial(1, geo_ref, w1_ref, w2_ref, w3_ref, r_ref, None)
-    r_out.ref[...] = r_ref[...]
-
-
-def slope_one_kernel(geo_ref, w1_ref, w2_ref, w3_ref, nb_ref, p_out, oh_out):
+
+
+def slope_kernel(geo_ref, w1_ref, w2_ref, w3_ref, nb_ref, p_out, p_zero_out, oh_out):
+    radial(1, geo_ref, w1_ref, w2_ref, w3_ref, None, p_out.ref)
+    p_out.send()
+    radial(0, geo_ref, w1_ref, w2_ref, w3_ref, None, p_zero_out.ref)
+    p_zero_out.send()
     fill_onehot(nb_ref, oh_out.ref)
-    oh_out.send()
-    radial(1, geo_ref, w1_ref, w2_ref, w3_ref, None, p_out.ref)
-
-
-def slope_zero_kernel(geo_ref, w1_ref, w2_ref, w3_ref, r_ref, p_ref):
-    radial(0, geo_ref, w1_ref, w2_ref, w3_ref, r_ref, p_ref)
-
-
-def waves_kernel(box_x, box_y, rows_ref, wave_ref, cs_out):
-    cs_ref = cs_out.ref
+
+
+def prepare_one_kernel(a_ref, r_in, p_in, f_in, y_ref, w_out, g_out, u_out):
+    def arrived(block):
+        for late in (r_in, p_in, f_in):
+            late.ready(block)
+
+    def ready(block):
+        for out in (w_out, g_out, u_out):
+            out.send(block)
+
+    prepare(a_ref, r_in.ref, p_in.ref, f_in.ref, y_ref, w_out.ref, g_out.ref, u_out.ref, arrived, ready)
+
+
+def prepare_zero_kernel(a_ref, r_in, p_in, f_in, y_ref, g_out, u_out):
+    def arrived(block):
+        for late in (r_in, p_in, f_in):
+            late.ready(block)
+
+    def ready(block):
+        g_out.send(block)
+        u_out.send(block)
+
+    prepare(a_ref, r_in.ref, p_in.ref, f_in.ref, y_ref, None, g_out.ref, u_out.ref, arrived, ready)
+
+
+def waves_kernel(box_x, box_y, rows_ref, wave_ref, cs_ref):
     own = rows_ref[...]
     x, y, z = own[0:1] * (1.0 / box_x), own[1:2] * (1.0 / box_y), own[2:3] * (1.0 / DEPTH_Z)
     turns = jnp.concatenate([x, y, z, jnp.zeros((5, ATOMS), F32)], 0)
@@ -294,7 +324,7 @@
     middle = (turns - high).astype(BF16).astype(F32)
     low = turns - high - middle
     parts = jnp.concatenate([high, middle, low, jnp.zeros((8, ATOMS), F32)], 0).astype(BF16)
-    wave = jnp.concatenate([wave_ref[...].astype(F32), jnp.zeros((5, K), F32)], 0)
+    wave = wave_ref[...]
     wave = jnp.concatenate([wave, wave, wave, jnp.zeros((8, K), F32)], 0).astype(BF16)
     cs_ref[:, :K] = dot(parts, wave, TN)
 
@@ -326,8 +356,8 @@
 
 
 def second_kernel(
-    h_ref, part_ref, a_in, b_in, nb_ref, y_ref, r_ref, cs_in, mix_in,
-    w_charge_ref, f_out, a_out, h2_out, charge_out, s_ref, ypart_ref,
+    h_ref, part_ref, a_in, b_in, nb_ref, y_ref, r_ref, cs_ref, mix_ref,
+    w_charge_ref, geo_ref, a_zero_ref, f_out, a_out, h2_out, charge_out, s_ref, ypart_ref,
 ):
     f_ref, a_ref, h2_ref, charge_ref = f_out.ref, a_out.ref, h2_out.ref, charge_out.ref
     ypart_ref[...] = received(a_in, b_in, 64)
@@ -339,7 +369,7 @@
         def state(n):
             nb = jnp.broadcast_to(nb_ref[n : n + 1, :], (16, 128))
             f = take_lanes(tables, nb & 127, nb >> 7)
-            f_ref[rows, n * 128 : (n + 1) * 128] = f
+            f_ref[rows, n * 128 : (n + 1) * 128] = f.astype(BF16)
             return f
 
         return state
@@ -347,7 +377,6 @@
     aggregate(r_ref, get_f, y_ref, a_ref)
     f_out.send()
     a_out.send()
-    mix_ref, cs_ref = mix_in.ready(), cs_in.ready()
     h_two = h_ref[...] + dot(mix_ref[1], invariants(a_ref))
     h2_ref[...] = h_two
     charge = dot(w_charge_ref[...], h_two.astype(BF16))
@@ -364,40 +393,79 @@
         s_ref[(2 * t + 1) * KC : (2 * t + 2) * KC, :] = part[:, 128:]
 
 
-def backward(ga_ref, r_ref, p_ref, f_ref, y_ref, gf_ref, t_ref):
-    def body(n, carry):
-        cols = pl.ds(pl.multiple_of(n * 128, 128), 128)
-        y = [y_ref[m, pl.ds(n, 1), :] for m in range(8)]
-        acc = [jnp.zeros((16, 128), F32) for _ in range(9)]
+def prepare(a_ref, r_ref, p_ref, f_ref, y_ref, w_ref, g_ref, u_ref, arrived=lambda block: None, ready=lambda block: None):
+    count = NB // BLOCKS
+
+    def block_of(block):
+        def body(cc, carry):
+            r0 = pl.multiple_of(cc * 16, 16)
+            rows = pl.ds(r0, 16)
+            late = [pl.ds(pl.multiple_of(l * 128 + r0, 16), 16) for l in range(3)]
+            a = [a_ref[k, rows, :] for k in range(9)]
+            for n in range(block * count, (block + 1) * count):
+                cols = slice(n * 128, (n + 1) * 128)
+                y = [2.0 * y_ref[m, n : n + 1, :] for m in range(8)]
+                f = f_ref[rows, cols].astype(F32)
+                r = [r_ref[late[l], cols].astype(F32) for l in range(3)]
+                q1 = a[1] * y[0] + a[2] * y[1] + a[3] * y[2]
+                q2 = a[4] * y[3] + a[5] * y[4] + a[6] * y[5] + a[7] * y[6] + a[8] * y[7]
+                g_ref[late[0], cols] = (f * r[1]).astype(BF16)
+                g_ref[late[1], cols] = (f * r[2]).astype(BF16)
+                u_ref[late[0], cols] = (f * p_ref[late[0], cols].astype(F32)).astype(BF16)
+                u_ref[late[1], cols] = (f * q1 * p_ref[late[1], cols].astype(F32)).astype(BF16)
+                u_ref[late[2], cols] = (f * q2 * p_ref[late[2], cols].astype(F32)).astype(BF16)
+                if w_ref is not None:
+                    w_ref[late[0], cols] = r_ref[late[0], cols]
+                    w_ref[late[1], cols] = (q1 * r[1]).astype(BF16)
+                    w_ref[late[2], cols] = (q2 * r[2]).astype(BF16)
+            return carry
+
+        lax.fori_loop(0, 8, body, 0)
+
+    for block in range(BLOCKS):
+        arrived(block)
+        block_of(block)
+        ready(block)
+
+
+TOGETHER = 3
+
+
+def backward(ginv_ref, ga_ref, w_ref, g_ref, u_ref, gf_ref, t_ref, arrived=lambda block: None):
+    def body(b, carry):
+        acc = [[jnp.zeros((8, 128), F32) for _ in range(9)] for _ in range(TOGETHER)]
         for cc in range(8):
             rows = slice(cc * 16, cc * 16 + 16)
-            ga = [ga_ref[k, rows, :] for k in range(9)]
-            f = f_ref[rows, cols].astype(F32)
-            r = [r_ref[l * 128 + cc * 16 : l * 128 + cc * 16 + 16, cols].astype(F32) for l in range(3)]
-            p = [p_ref[l * 128 + cc * 16 : l * 128 + cc * 16 + 16, cols].astype(F32) for l in range(3)]
-            q1 = ga[1] * y[0] + ga[2] * y[1] + ga[3] * y[2]
-            q2 = ga[4] * y[3] + ga[5] * y[4] + ga[6] * y[5] + ga[7] * y[6] + ga[8] * y[7]
-            if gf_ref is not None:
-                gf_ref[rows, cols] = (ga[0] * r[0] + q1 * r[1] + q2 * r[2]).astype(BF16)
-            acc[0] = acc[0] + f * (ga[0] * p[0] + q1 * p[1] + q2 * p[2])
-            g1, g2 = f * r[1], f * r[2]
-            for m in range(3):
-                acc[1 + m] = acc[1 + m] + g1 * ga[1 + m]
-            for m in range(5):
-                acc[4 + m] = acc[4 + m] + g2 * ga[4 + m]
-        for k in range(9):
-            t_ref[k, pl.ds(n, 1), :] = jnp.sum(acc[k], 0, keepdims=True)
+            late = [slice(l * 128 + cc * 16, l * 128 + cc * 16 + 16) for l in range(3)]
+            gi = [ginv_ref[late[l], :] for l in range(3)]
+            ga = [ga_ref[k, rows, :] for k in range(8)]
+            for j in range(TOGETHER):
+                cols = pl.ds(pl.multiple_of((b * TOGETHER + j) * 128, 128), 128)
+                if gf_ref is not None:
+                    w = [w_ref[late[l], cols].astype(F32) for l in range(3)]
+                    gf_ref[rows, cols] = (gi[0] * w[0] + gi[1] * w[1] + gi[2] * w[2]).astype(BF16)
+                u = [u_ref[late[l], cols].astype(F32) for l in range(3)]
+                g1, g2 = g_ref[late[0], cols].astype(F32), g_ref[late[1], cols].astype(F32)
+                terms = [gi[0] * u[0] + gi[1] * u[1] + gi[2] * u[2]]
+                terms += [g1 * ga[m] for m in range(3)] + [g2 * ga[m] for m in range(3, 8)]
+                acc[j] = [old + (new[:8] + new[8:]) for old, new in zip(acc[j], terms)]
+        for j in range(TOGETHER):
+            for k in range(9):
+                t_ref[k, pl.ds(b * TOGETHER + j, 1), :] = jnp.sum(acc[j][k], 0, keepdims=True)
         return carry
 
-    lax.fori_loop(0, NB, body, 0)
-
-
-def pull_invariants(g_inv, a_ref, ga_ref):
-    ga_ref[0] = g_inv[:C]
+    count = NB // TOGETHER // BLOCKS
+    for block in range(BLOCKS):
+        arrived(block)
+        lax.fori_loop(block * count, (block + 1) * count, body, 0)
+
+
+def pull_invariants(g_inv, a_ref, ginv_ref, ga_ref):
+    ginv_ref[...] = g_inv
     for k in range(1, 4):
-        ga_ref[k] = 2.0 * a_ref[k] * g_inv[C : 2 * C]
+        ga_ref[k - 1] = 2.0 * a_ref[k] * g_inv[C : 2 * C]
     for k in range(4, 9):
-        ga_ref[k] = 2.0 * a_ref[k] * g_inv[2 * C :]
+        ga_ref[k - 1] = 2.0 * a_ref[k] * g_inv[2 * C :]
 
 
 def fill_onehot(nb_ref, oh_ref):
@@ -406,9 +474,9 @@
 
 
 def ewald_kernel(
-    box_x, box_y, scale, s_ref, spectral_ref, cs_ref, wave_ref, charge_ref, h_in, h2_in, a_in, y_in, r_in, p_in,
-    f_in, oh_in, mix_in, first_in, last_in, read_hidden_in, w_charge_in,
-    energy_ref, gpos_ref, gown_ref, gpart_ref, ya_ref, yb_ref, t_ref, ga_ref, gf_ref, gphase_ref,
+    box_x, box_y, scale, s_ref, spectral_ref, cs_ref, wave_ref, charge_ref, h_in, h2_in, a_in, w_in, g_in, u_in,
+    oh_in, mix_in, first_in, last_in, read_hidden_in, w_charge_in,
+    energy_ref, gpos_ref, gown_ref, gpart_ref, ya_ref, yb_ref, t_ref, ginv_ref, ga_ref, gf_ref, gphase_ref,
 ):
     charge = charge_ref[...]
     qt_hi, qt_lo = split(charge.T)
@@ -454,9 +522,13 @@
     g_two = dot(w_charge_ref[...], potential.astype(BF16), TN) + dot(read_hidden_ref[...], g_hidden, TN)
     g_two = g_two.astype(BF16)
     g_inv = dot(mix_ref[1], g_two, TN).astype(BF16).astype(F32)
-    a_ref, y_ref, r_ref, p_ref, f_ref = a_in.ready(), y_in.ready(), r_in.ready(), p_in.ready(), f_in.ready()
-    pull_invariants(g_inv, a_ref, ga_ref)
-    backward(ga_ref, r_ref, p_ref, f_ref, y_ref, gf_ref, t_ref)
+    pull_invariants(g_inv, a_in.ready(), ginv_ref, ga_ref)
+
+    def arrived(block):
+        for late in (w_in, g_in, u_in):
+            late.ready(block)
+
+    backward(ginv_ref, ga_ref, w_in.ref, g_in.ref, u_in.ref, gf_ref, t_ref, arrived)
     oh_ref = oh_in.ready()
     grads = dot(gf_ref[...], oh_ref[...], NT)
     gown_ref[...] = grads[:, :128] + g_two.astype(F32) + first
@@ -477,13 +549,13 @@
 
 
 def last_kernel(
-    gown_ref, a_in, b_in, ix_ref, mix_ref, a_ref, r_ref, p_ref, f_ref, y_ref, t1_ref, geo_ref, oh_ref, gpos_ref,
-    own_ref, part_ref, gy_ref, ga_ref, t_ref, rows_ref,
+    gown_ref, a_in, b_in, ix_ref, mix_ref, a_ref, g_ref, u_ref, t1_ref, geo_ref, oh_ref, gpos_ref,
+    own_ref, part_ref, gy_ref, ginv_ref, ga_ref, t_ref, rows_ref,
 ):
     g_one = gown_ref[...] + give_back(received(a_in, b_in, 32), ix_ref[...], 128)
     g_inv = dot(mix_ref[0], g_one.astype(BF16), TN).astype(BF16).astype(F32)
-    pull_invariants(g_inv, a_ref, ga_ref)
-    backward(ga_ref, r_ref, p_ref, f_ref, y_ref, None, t_ref)
+    pull_invariants(g_inv, a_ref, ginv_ref, ga_ref)
+    backward(ginv_ref, ga_ref, None, g_ref, u_ref, None, t_ref)
     t = [t_ref[k] + t1_ref[k] for k in range(9)]
     ux, uy, uz = geo_ref[0], geo_ref[1], geo_ref[2]
     root = 2.0 / ROOT_THREE
@@ -522,38 +594,54 @@
 
 
 class Far:
-    def __init__(self, array, late=False):
+    def __init__(self, array, late=False, blocks=1):
         self.array = array
         self.late = late
+        self.blocks = blocks
 
 
 class Late:
-    def __init__(self, copy, ref):
-        self.copy = copy
+    def __init__(self, copies, ref):
+        self.copies = copies
         self.ref = ref
 
-    def ready(self):
-        self.copy.wait()
+    def ready(self, block=0):
+        self.copies[block].wait()
         return self.ref
 
 
 class Out:
-    def __init__(self, copy, ref):
-        self.copy = copy
+    def __init__(self, copies, ref):
+        self.copies = copies
         self.ref = ref
-        self.sent = False
-
-    def send(self):
-        self.copy.start()
-        self.sent = True
+        self.sent = set()
+
+    def send(self, block=0):
+        self.copies[block].start()
+        self.sent.add(block)
+
+    def finish(self):
+        for block in range(len(self.copies)):
+            if block not in self.sent:
+                self.send(block)
+
+
+def column_copies(source, target, blocks, sems):
+    if blocks == 1:
+        return [pltpu.make_async_copy(source, target, next(sems))]
+    width = source.shape[1] // blocks
+    cols = [pl.ds(b * width, width) for b in range(blocks)]
+    return [pltpu.make_async_copy(source.at[:, c], target.at[:, c], next(sems)) for c in cols]
 
 
 def call(kernel, outs, *operands, scratch=(), flops=0, moved=0):
     n_in, n_out = len(operands), len(outs)
     far_in = [i for i, o in enumerate(operands) if isinstance(o, Far)]
-    far_out = [i for i, o in enumerate(outs) if len(o) == 3]
+    far_out = [i for i, o in enumerate(outs) if len(o) in (3, 5)]
+    forwarded = [i for i, o in enumerate(outs) if len(o) == 4]
     arrays = [pltpu.with_memory_space_constraint(o.array, pltpu.HBM) if isinstance(o, Far) else o for o in operands]
     n_far = len(far_in) + len(far_out)
+    n_sems = sum(operands[i].blocks for i in far_in) + BLOCKS * len(far_out) + len(forwarded)
     buffers = [pltpu.VMEM(arrays[i].shape, arrays[i].dtype) for i in far_in]
     buffers += [pltpu.VMEM(outs[i][0], outs[i][1]) for i in far_out]
 
@@ -561,37 +649,46 @@
         ins, results, rest = list(refs[:n_in]), list(refs[n_in : n_in + n_out]), refs[n_in + n_out :]
         own, held = rest[: len(scratch)], rest[len(scratch) : len(scratch) + n_far]
         sems = rest[-1]
-        waits = []
+        waits, later, sent = [], [], []
+        sem = (sems.at[k] for k in range(n_sems))
         for k, i in enumerate(far_in):
-            copy = pltpu.make_async_copy(ins[i], held[k], sems.at[k])
+            copies = column_copies(ins[i], held[k], operands[i].blocks, sem)
+            if operands[i].late:
+                big = len(copies) == 1 and math.prod(held[k].shape) > 10**6
+                later += [(BLOCKS if big else b, copy) for b, copy in enumerate(copies)]
+                ins[i] = Late(copies, held[k])
+            else:
+                copies[0].start()
+                waits.append(copies[0])
+                ins[i] = held[k]
+        for _, copy in sorted(later, key=lambda item: item[0]):
             copy.start()
-            if operands[i].late:
-                ins[i] = Late(copy, held[k])
-            else:
-                waits.append(copy)
-                ins[i] = held[k]
-        sent = []
         for k, i in enumerate(far_out, len(far_in)):
-            results[i] = Out(pltpu.make_async_copy(held[k], results[i], sems.at[k]), held[k])
+            blocks = outs[i][4] if len(outs[i]) == 5 else 1
+            results[i] = Out(column_copies(held[k], results[i], blocks, sem), held[k])
             sent.append(results[i])
         for copy in waits:
             copy.wait()
-        kernel(*ins, *results, *own)
+        for i in forwarded:
+            out = Out(column_copies(ins[outs[i][3]], results[i], 1, sem), None)
+            out.send()
+            sent.append(out)
+        kernel(*ins, *[r for i, r in enumerate(results) if i not in forwarded], *own)
         for out in sent:
-            if not out.sent:
-                out.send()
+            out.finish()
         for out in sent:
-            out.copy.wait()
+            for copy in out.copies:
+                copy.wait()
 
     def place_of(far):
         return pl.BlockSpec(memory_space=pltpu.HBM if far else pltpu.VMEM)
 
     return pl.pallas_call(
         wrapped,
-        out_shape=[pltpu.HBM(o[0], o[1]) if len(o) == 3 else jax.ShapeDtypeStruct(o[0], o[1]) for o in outs],
+        out_shape=[pltpu.HBM(o[0], o[1]) if len(o) > 2 else jax.ShapeDtypeStruct(o[0], o[1]) for o in outs],
         in_specs=[place_of(isinstance(o, Far)) for o in operands],
-        out_specs=[place_of(len(o) == 3) for o in outs],
-        scratch_shapes=[pltpu.VMEM(s, d) for s, d in scratch] + buffers + [pltpu.SemaphoreType.DMA((max(n_far, 1),))],
+        out_specs=[place_of(len(o) > 2) for o in outs],
+        scratch_shapes=[pltpu.VMEM(s, d) for s, d in scratch] + buffers + [pltpu.SemaphoreType.DMA((max(n_sems, 1),))],
         compiler_params=pltpu.CompilerParams(vmem_limit_bytes=24 * 1024 * 1024),
         cost_estimate=pl.CostEstimate(flops=flops, bytes_accessed=moved, transcendentals=0),
     )(*arrays)
@@ -617,15 +714,6 @@
         return (c - 1) % 64 if c % 2 == 0 else (c + 1) % 64
 
     return swap(a, CELL, lambda c: c ^ 1), swap(b, CELL, other)
-
-
-def reduce_all(partial):
-    rows = partial.shape[0] // NWIDE
-    pieces = lax.all_to_all(partial, WIDE, 0, 0, tiled=True)
-    (mine,) = call(functools.partial(sum_kernel, NWIDE, 8), [((8 * rows, 128), F32)], pieces)
-    mine = lax.all_to_all(mine, ("z",), 0, 0, tiled=True)
-    (spread,) = call(functools.partial(sum_kernel, 8, NWIDE), [((NWIDE * rows, 128), F32, True)], mine)
-    return lax.all_to_all(spread, WIDE, 0, 0, tiled=True)
 
 
 def body(
@@ -648,57 +736,81 @@
 
     rows, ix, strip = call(strip_x_kernel, [small, index, small], Far(positions), Far(species[None]), Far(send_x))
     xa, xb = swap_x(strip, strip)
+    nb, live, emb, *near_nets, mix_near, wave = call(
+        fetch_kernel,
+        [((NB, 128), jnp.int32), ((NB, 128), F32), ((8, C), F32), (w1.shape, F32), (radial_mid.shape, BF16), (radial_out.shape, BF16), (mixing.shape, BF16), ((8, K), F32)],
+        Far(neighbours), Far(live_slots), emb, w1, Far(radial_mid), Far(w3), Far(mixing), Far(wave_ids), flops=10**8, moved=10**6,
+    )
+    xa, xb, nb, live, emb, near_nets, mix_near, wave = lax.optimization_barrier((xa, xb, nb, live, emb, near_nets, mix_near, wave))
     part, iy, strip = call(strip_y_kernel, [small, index, small], rows, xa, xb, Far(send_y))
     ya, yb = swap_y(strip, strip)
     nets = (Far(w1), Far(radial_mid), Far(w3))
-    nb, geo, ylm, f_zero, a_zero, h_one, h_far, xa, xb = call(
+    ylm_shape, a_shape, cs_shape = ((8, NB, 128), F32), ((9, C, 128), F32), ((ATOMS, 2 * K), F32)
+    geo, ylm, f_zero, r_zero, a_zero, h_one, xa, xb = call(
         with_box(first_kernel, box_x, box_y),
-        [
-            ((NB, 128), jnp.int32), ((8, NB, 128), F32, True), ((8, NB, 128), F32, True),
-            ((C, EDGES), BF16, True), ((9, C, 128), F32, True), square, square + (True,), strip_32, strip_32,
-        ],
-        rows, part, ya, yb, Far(neighbours), Far(live_slots), ix, Far(emb), *nets, Far(mixing),
-        scratch=[edge3],
+        [ylm_shape, ylm_shape, ((C, EDGES), BF16, True), edge3 + (True,), a_shape, square, strip_32, strip_32],
+        rows, part, ya, yb, nb, live, ix, emb, *near_nets, mix_near,
     )
-    rows_later, geo_soon, _, _ = lax.optimization_barrier((rows, geo, xa, xb))
+    rows_later, _, _ = lax.optimization_barrier((rows, xa, xb))
     xa, xb = swap_x(xa, xb)
-    (cs,) = call(
-        with_box(waves_kernel, box_x, box_y), [((ATOMS, 2 * K), F32, True)], rows_later, Far(wave_ids), flops=10**8, moved=10**6
-    )
+    (cs,) = call(with_box(waves_kernel, box_x, box_y), [cs_shape], rows_later, wave, flops=10**8, moved=10**6)
     xa, xb, cs = lax.optimization_barrier((xa, xb, cs))
     fpart, ya, yb = call(feature_strip_kernel, [square, strip_48, strip_48], h_one, xa, xb, iy)
-    geo_soon, _, _ = lax.optimization_barrier((geo_soon, ya, yb))
+    geo_soon, _, _ = lax.optimization_barrier((geo, ya, yb))
     ya, yb = swap_y(ya, yb)
-    r_one, r_far = call(radial_kernel, [edge3, edge3 + (True,)], Far(geo_soon), *nets, flops=5 * 10**8, moved=10**7)
-    f_one, a_one, h_two, charge, s_part = call(
+    (r_one,) = call(radial_kernel, [edge3], geo_soon, *near_nets, flops=5 * 10**8, moved=10**7)
+    f_one, a_one, h_two, charge, s_part, h_far, ylm, r_far, cs, geo, a_zero = call(
         second_kernel,
-        [((C, EDGES), F32, True), ((9, C, 128), F32, True), square + (True,), ((KC, ATOMS), F32, True), ((TILES * KC, 128), F32)],
-        h_one, fpart, ya, yb, nb, Far(ylm), r_one, Far(cs, True), Far(mixing, True), Far(w_charge),
+        [
+            ((C, EDGES), BF16, True), a_shape + (True,), square + (True,), ((KC, ATOMS), F32, True), ((TILES * KC, 128), F32),
+            square + (True, 0), ylm_shape + (True, 5), edge3 + (True, 6), cs_shape + (True, 7), ylm_shape + (True, 10),
+            a_shape + (True, 11),
+        ],
+        h_one, fpart, ya, yb, nb, ylm, r_one, cs, mix_near, w_charge, geo, a_zero,
         scratch=[square],
     )
+    late = lambda array: Far(array, True)
+    edge2 = ((2 * C, EDGES), BF16)
+    blocked = (True, None, BLOCKS)
     geo_later, _ = lax.optimization_barrier((geo, s_part))
-    p_one, oh = call(
-        slope_one_kernel, [edge3 + (True,), ((TABLE, EDGES), BF16, True)], Far(geo_later), *nets, Far(nb), flops=10**9, moved=10**7
+    p_one, p_zero, oh = call(
+        slope_kernel, [edge3 + (True,), edge3 + (True,), ((TABLE, EDGES), BF16, True)], Far(geo_later), *nets, Far(nb), flops=10**9, moved=2 * 10**7
     )
-    s_all = reduce_all(s_part)
-    late = lambda array: Far(array, True)
+    rows_each = s_part.shape[0] // NWIDE
+    pieces = lax.all_to_all(s_part, WIDE, 0, 0, tiled=True)
+    pieces, p_one, p_zero, oh = lax.optimization_barrier((pieces, p_one, p_zero, oh))
+    (mine,) = call(functools.partial(sum_kernel, NWIDE, 8), [((8 * rows_each, 128), F32)], pieces)
+    a_later, _ = lax.optimization_barrier((a_zero, mine))
+    g_zero, u_zero = call(
+        prepare_zero_kernel, [edge2 + blocked, edge3 + blocked],
+        Far(a_later), Far(r_zero, True, BLOCKS), Far(p_zero, True, BLOCKS), Far(f_zero, True, BLOCKS), Far(ylm), flops=10**9, moved=2 * 10**7,
+    )
+    mine = lax.all_to_all(mine, ("z",), 0, 0, tiled=True)
+    mine, g_zero, u_zero = lax.optimization_barrier((mine, g_zero, u_zero))
+    (spread,) = call(functools.partial(sum_kernel, 8, NWIDE), [((NWIDE * rows_each, 128), F32, True)], mine)
+    a_later, _ = lax.optimization_barrier((a_one, spread))
+    w_one, g_one, u_one = call(
+        prepare_one_kernel, [edge3 + blocked, edge2 + blocked, edge3 + blocked],
+        Far(a_later), Far(r_far, True, BLOCKS), Far(p_one, True, BLOCKS), Far(f_one, True, BLOCKS), Far(ylm), flops=10**9, moved=2 * 10**7,
+    )
+    s_all = lax.all_to_all(spread, WIDE, 0, 0, tiled=True)
+    s_all, w_one, g_one, u_one = lax.optimization_barrier((s_all, w_one, g_one, u_one))
     energy, gpos, gown, gpart, ya, yb, t_one = call(
         with_box(ewald_kernel, box_x, box_y, scale),
         [((1, 128), F32), small, square, square, strip_48, strip_48, ((9, NB, 128), F32)],
-        Far(s_all), Far(spectral), Far(cs), Far(wave_ids), Far(charge), late(h_far), late(h_two), late(a_one), late(ylm), late(r_far),
-        late(p_one), late(f_one), late(oh), late(mixing), late(read_first[None]), late(read_last[None]), late(read_hidden), late(w_charge),
-        scratch=[((9, C, 128), F32), ((C, EDGES), BF16), ((2 * ATOMS, K), BF16)],
+        s_all, Far(spectral), Far(cs), Far(wave_ids), Far(charge), late(h_far), late(h_two), late(a_one),
+        Far(w_one, True, BLOCKS), Far(g_one, True, BLOCKS), Far(u_one, True, BLOCKS), late(oh), late(mixing), late(read_first[None]), late(read_last[None]), late(read_hidden),
+        late(w_charge),
+        scratch=[((3 * C, 128), F32), ((8, C, 128), F32), ((C, EDGES), BF16), ((2 * ATOMS, K), BF16)],
     )
-    geo_last, _, _ = lax.optimization_barrier((geo, ya, yb))
     ya, yb = swap_y(ya, yb)
-    r_zero, p_zero = call(slope_zero_kernel, [edge3, edge3], Far(geo_last), *nets, flops=10**9, moved=10**7)
     gown, xa, xb = call(return_features_kernel, [square, strip_32, strip_32], gown, gpart, ya, yb, iy)
     xa, xb = swap_x(xa, xb)
     own, part, gy = call(
         last_kernel,
         [small, small, small],
-        gown, xa, xb, ix, mixing, a_zero, r_zero, p_zero, f_zero, ylm, t_one, geo, oh, gpos,
-        scratch=[((9, C, 128), F32), ((9, NB, 128), F32), ((16, EDGES), F32)],
+        gown, xa, xb, ix, mixing, a_zero, g_zero, u_zero, t_one, geo, oh, gpos,
+        scratch=[((3 * C, 128), F32), ((8, C, 128), F32), ((9, NB, 128), F32), ((16, EDGES), F32)],
     )
     ya, yb = swap_y(gy, gy)
     own, part = call(return_y_kernel, [small, small], own, part, ya, yb, iy)

time: 135 us -> 129 us (0.956)
  blocking collectives: 27.3 us -> 0 us
  waiting for transfers between devices: 18.2 us -> 31.9 us
  starting transfers between devices: 36.7 us -> 45.1 us
    all_to_all x2 -> x0, blocking collectives: 27.3 us -> none  [the longest x1 15.4 us: reduce_all(): pieces = lax.all_to_all(partial, WIDE, 0, 0, tiled=True)]
    all_to_all x1 -> x3, starting transfers between devices: 5.77 us -> 15.4 us  [the longest x1 6.04 us: body(): s_all = lax.all_to_all(spread, WIDE, 0, 0, tiled=True)]
    ppermute x16, waiting for transfers between devices: 13.9 us -> 21.1 us  [swap(): return lax.ppermute(value, axes, [(i, of(i)) for i in range(count)])]
    all_to_all x1 -> x3, waiting for transfers between devices: 4.39 us -> 10.8 us  [the longest x1 5.02 us: body(): s_all = lax.all_to_all(spread, WIDE, 0, 0, tiled=True)]
    pallas_call x16 -> x18, Pallas kernels: 47.5 us -> 48.7 us  [call(): pl.pallas_call(wrapped, out_shape=[pltpu.HBM(o[0], o[1]) if len(o) > 2 el...]
  transfers between devices with their start and end apart: 17 -> 19, of which waited for: 6 -> 12; matrix products, arithmetic and copies ran while one was open for 2% -> 1% of each run, Pallas kernels for 13% -> 18%
where the time goes in v3:
time: 129 us; the launch traced here: 128 us
  Pallas kernels  48.7 us (38%)
  starting transfers between devices  45.1 us (35%)
  waiting for transfers between devices  31.9 us (25%)
  other arithmetic  1.37 us (1%)
    pallas_call x18, Pallas kernels, call(): pl.pallas_call(wrapped, out_shape=[pltpu.HBM(o[0], o[1]) if len(o) > 2 el...  48.7 us
    ppermute x16, starting transfers between devices, swap(): return lax.ppermute(value, axes, [(i, of(i)) for i in range(count)])  29.7 us
    ppermute x16, waiting for transfers between devices, swap(): return lax.ppermute(value, axes, [(i, of(i)) for i in range(count)])  21.1 us
    all_to_all x1, starting transfers between devices, body(): s_all = lax.all_to_all(spread, WIDE, 0, 0, tiled=True)  6.04 us
    all_to_all x1, starting transfers between devices, body(): pieces = lax.all_to_all(s_part, WIDE, 0, 0, tiled=True)  5.05 us
    all_to_all x1, waiting for transfers between devices, body(): s_all = lax.all_to_all(spread, WIDE, 0, 0, tiled=True)  5.02 us
    all_to_all x1, starting transfers between devices, body(): mine = lax.all_to_all(mine, ('z',), 0, 0, tiled=True)  4.33 us
    all_to_all x1, waiting for transfers between devices, body(): mine = lax.all_to_all(mine, ('z',), 0, 0, tiled=True)  2.96 us
  transfers between devices with their start and end apart: 19, of which 12 were waited for; matrix products, arithmetic and copies ran while one was open for 1% of the time, Pallas kernels for 18%

profile of v3, /device:TPU:1, one launch (start us, length us, event | category | flops | bytes accessed | tf_op | source)
XLA Modules:
  0.0 128.3 jit_solution(4138382022922437222)
XLA Ops:
  1.6 4.2 %collective-permute-start.1 = (f32[8,128]{1,0:T(8,128)S(1)}, f32[8,128]{1,0:T(8,128)S(1)}, u32[]{:S(2)}, u32[]{:S(2)}) collective-permute-start(f32[8,128]{1,0:T(8,128)S(1)} %get-tuple-element.91), channel_id=1, source_target_pairs={{0,192},{64,128},{128,64},{192,0},{1,193},{65,129},{129,65},{193,1... | collective-permute-start | bytes 12296 | tf_op jit(solution)/shard_map/ppermute | solution.py:701
  9.5 8.1 %collective-permute-start.3 = (f32[8,128]{1,0:T(8,128)S(1)}, f32[8,128]{1,0:T(8,128)S(1)}, u32[]{:S(2)}, u32[]{:S(2)}) collective-permute-start(f32[8,128]{1,0:T(8,128)S(1)} %get-tuple-element.103), channel_id=1, source_target_pairs={{0,63},{1,2},{2,1},{3,4},{4,3},{5,6},{6,5},{7,8},{8,7},{9,10},{10,... | collective-permute-start | bytes 12296 | tf_op jit(solution)/shard_map/ppermute | solution.py:701
  20.1 4.1 %shard_map.179 = (f32[8,24,128]{2,1,0:T(8,128)S(1)}, f32[8,24,128]{2,1,0:T(8,128)S(1)}, bf16[128,3072]{1,0:T(8,128)(2,1)}, bf16[384,3072]{1,0:T(8,128)(2,1)}, f3...) custom-call(f32[8,128]{1,0:T(8,128)S(1)} %get-tuple-element.115.refs_0_, ...), custom_call_target="tpu_custom_call" | custom-call | tf_op jit(solution)/shard_map/pallas_call | solution.py:686
  24.2 2.0 %collective-permute-start.4 = (f32[32,128]{1,0:T(8,128)S(1)}, f32[32,128]{1,0:T(8,128)S(1)}, u32[]{:S(2)}, u32[]{:S(2)}) collective-permute-start(f32[32,128]{1,0:T(8,128)S(1)} %get-tuple-element.113), channel_id=1, source_target_pairs={{0,64},{64,0},{128,192},{192,128},{1,65},{65,1},{129,193},{193,129... | collective-permute-start | bytes 49160 | tf_op jit(solution)/shard_map/ppermute | solution.py:701
  26.2 2.1 %collective-permute-start.5 = (f32[32,128]{1,0:T(8,128)S(1)}, f32[32,128]{1,0:T(8,128)S(1)}, u32[]{:S(2)}, u32[]{:S(2)}) collective-permute-start(f32[32,128]{1,0:T(8,128)S(1)} %get-tuple-element.114), channel_id=1, source_target_pairs={{0,192},{64,128},{128,64},{192,0},{1,193},{65,129},{129,65},{193,1... | collective-permute-start | bytes 49160 | tf_op jit(solution)/shard_map/ppermute | solution.py:701
  31.4 4.0 %collective-permute-start.7 = (f32[48,128]{1,0:T(8,128)S(1)}, f32[48,128]{1,0:T(8,128)S(1)}, u32[]{:S(2)}, u32[]{:S(2)}) collective-permute-start(f32[48,128]{1,0:T(8,128)S(1)} %get-tuple-element.122), channel_id=1, source_target_pairs={{0,63},{1,2},{2,1},{3,4},{4,3},{5,6},{6,5},{7,8},{8,7},{9,10},{10,... | collective-permute-start | bytes 73736 | tf_op jit(solution)/shard_map/ppermute | solution.py:701
  35.4 1.8 %shard_map.182.refs_6_ = bf16[384,3072]{1,0:T(8,128)(2,1)S(1)} custom-call(f32[8,24,128]{2,1,0:T(8,128)S(1)} %get-tuple-element.125.refs_0_.refs_10_, f32[2,8,64]{2,1,0:T(8,128)S(1)} %get-tuple-element.108.refs_8_.refs_1_, bf16[2,64,64]{2,1,0:T(8,128)(2,1)S(1)} %get-tuple-element.109.refs_9_.refs_2_, bf16[2,384,64]{2,1,0:T(8,128)(2,1)S(1)} %get-tuple-element.110.refs_10_.refs_3_), custom_call_target="tpu_custom_call" | custom-call | flops 500000000 | bytes 10000000 | tf_op jit(solution)/shard_map/pallas_call | solution.py:686
  38.4 5.2 %shard_map.183 = (bf16[128,3072]{1,0:T(8,128)(2,1)}, f32[9,128,128]{2,1,0:T(8,128)}, f32[128,128]{1,0:T(8,128)}, f32[64,128]{1,0:T(8,128)}, f32[1024,128]{1,0:T(...) custom-call(f32[128,128]{1,0:T(8,128)S(1)} %get-tuple-element.112.re, ...), custom_call_target="tpu_custom_call" | custom-call | tf_op jit(solution)/shard_map/pallas_call | solution.py:686
  43.6 5.1 %all-to-all-start = ((f32[32,32,128]{2,1,0:T(8,128)}), f32[32,32,128]{2,1,0:T(8,128)S(1)}, u32[]{:S(2)}, u32[]{:S(2)}) async-start(f32[32,32,128]{2,1,0:T(8,128)} %bitcast.4), calls=%async_computation | async-start | bytes 1048576 | tf_op jit(solution)/shard_map/all_to_all | solution.py:780
  48.7 8.3 %shard_map.184 = (bf16[384,3072]{1,0:T(8,128)(2,1)}, bf16[384,3072]{1,0:T(8,128)(2,1)}, bf16[384,3072]{1,0:T(8,128)(2,1)}) custom-call(f32[8,24,128]{2,1,0:T(8,128)} %get-tuple-element.130.refs_0_.refs_9_, f32[2,8,64]{2,1,0:T(8,128)} %copy-done.8, bf16[2,64,64]{2,1,0:T(8,128)(2,1)} %refs_2_.3, bf16[2,64,384]{2,1,0:T(8,128)(2,1)} %bitcast.20, s32[24,128]{1,0:T(8,128)} %copy-done.7), custom_call_target="tpu_custom_call" | custom-call | flops 1000000000 | bytes 20000000 | tf_op jit(solution)/shard_map/pallas_call | solution.py:686
  57.0 2.8 %all-to-all-done = f32[32,32,128]{2,1,0:T(8,128)S(1)} async-done(((f32[32,32,128]{2,1,0:T(8,128)}), f32[32,32,128]{2,1,0:T(8,128)S(1)}, u32[]{:S(2)}, u32[]{:S(2)}) %all-to-all-start) | async-done | bytes 524320 | tf_op jit(solution)/shard_map/all_to_all | solution.py:780
  60.5 4.3 %all-to-all-start.1 = ((f32[8,32,128]{2,1,0:T(8,128)}), f32[8,32,128]{2,1,0:T(8,128)S(1)}, u32[]{:S(2)}, u32[]{:S(2)}) async-start(f32[8,32,128]{2,1,0:T(8,128)} %bitcast.6), calls=%async_computation.1 | async-start | bytes 262144 | tf_op jit(solution)/shard_map/all_to_all | solution.py:788
  64.8 5.2 %shard_map.186 = (bf16[256,3072]{1,0:T(8,128)(2,1)}, bf16[384,3072]{1,0:T(8,128)(2,1)}) custom-call(f32[9,128,128]{2,1,0:T(8,128)} %get-tuple-element.136.refs_0_.refs_5_, bf16[384,3072]{1,0:T(8,128)(2,1)} %get-tuple-element.137.refs_1_, bf16[384,3072]{1,0:T(8,128)(2,1)} %get-tuple-element.138.refs_2_, bf16[128,3072]{1,0:T(8,128)(2,1)} %get-tuple-element.139.refs_3_, ...), custom_call_target="tpu_custom_call" | custom-call | flops 1000000000 | bytes 20000000 | tf_op jit(solution)/shard_map/pallas_call | solution.py:686
  70.1 3.0 %all-to-all-done.1 = f32[8,32,128]{2,1,0:T(8,128)S(1)} async-done(((f32[8,32,128]{2,1,0:T(8,128)}), f32[8,32,128]{2,1,0:T(8,128)S(1)}, u32[]{:S(2)}, u32[]{:S(2)}) %all-to-all-start.1) | async-done | bytes 131104 | tf_op jit(solution)/shard_map/all_to_all | solution.py:788
  74.0 6.0 %all-to-all-start.2 = ((f32[32,32,128]{2,1,0:T(8,128)}), f32[32,32,128]{2,1,0:T(8,128)S(1)}, u32[]{:S(2)}, u32[]{:S(2)}) async-start(f32[32,32,128]{2,1,0:T(8,128)} %bitcast.18), calls=%async_computation.2 | async-start | bytes 1048576 | tf_op jit(solution)/shard_map/all_to_all | solution.py:796
  80.0 6.1 %shard_map.188 = (bf16[384,3072]{1,0:T(8,128)(2,1)}, bf16[256,3072]{1,0:T(8,128)(2,1)}, bf16[384,3072]{1,0:T(8,128)(2,1)}) custom-call(f32[9,128,128]{2,1,0:T(8,128)} %get-tuple-element.145.refs_0_.refs_7_, bf16[384,3072]{1,0:T(8,128)(2,1)} %get-tuple-element.146.refs_1_, bf16[384,3072]{1,0:T(8,128)(2,1)} %get-tuple-element.147.refs_2_, ...), custom_call_target="tpu_custom_call" | custom-call | flops 1000000000 | bytes 20000000 | tf_op jit(solution)/shard_map/pallas_call | solution.py:686
  86.1 5.0 %all-to-all-done.2 = f32[32,32,128]{2,1,0:T(8,128)S(1)} async-done(((f32[32,32,128]{2,1,0:T(8,128)}), f32[32,32,128]{2,1,0:T(8,128)S(1)}, u32[]{:S(2)}, u32[]{:S(2)}) %all-to-all-start.2) | async-done | bytes 524320 | tf_op jit(solution)/shard_map/all_to_all | solution.py:796
  91.1 6.8 %shard_map.189 = (f32[1,128]{1,0:T(1,128)}, f32[8,128]{1,0:T(8,128)S(1)}, f32[128,128]{1,0:T(8,128)S(1)}, f32[128,128]{1,0:T(8,128)S(1)}, f32[48,128]{1,0:T(8,12...) custom-call(f32[1024,128]{1,0:T(8,128)S(1)} %bitcast.15, f32[64,1024]{1,0:T(8,128)} %refs_1_.3, ...), custom_call_target="tpu_custom_call" | custom-call | tf_op jit(solution)/shard_map/pallas_call | solution.py:686
  100.7 4.5 %collective-permute-done.9.refs_3_ = f32[48,128]{1,0:T(8,128)S(1)} collective-permute-done((f32[48,128]{1,0:T(8,128)S(1)}, f32[48,128]{1,0:T(8,128)S(1)}, u32[]{:S(2)}, u32[]{:S(2)}) %collective-permute-start.9) | collective-permute-done | bytes 24608 | tf_op jit(solution)/shard_map/ppermute | solution.py:701
  107.4 1.8 %collective-permute-start.11 = (f32[32,128]{1,0:T(8,128)S(1)}, f32[32,128]{1,0:T(8,128)S(1)}, u32[]{:S(2)}, u32[]{:S(2)}) collective-permute-start(f32[32,128]{1,0:T(8,128)S(1)} %get-tuple-element.168), channel_id=1, source_target_pairs={{0,192},{64,128},{128,64},{192,0},{1,193},{65,129},{129,65},{193,1... | collective-permute-start | bytes 49160 | tf_op jit(solution)/shard_map/ppermute | solution.py:701
  109.3 2.8 %collective-permute-done.11.refs_2_ = f32[32,128]{1,0:T(8,128)S(1)} collective-permute-done((f32[32,128]{1,0:T(8,128)S(1)}, f32[32,128]{1,0:T(8,128)S(1)}, u32[]{:S(2)}, u32[]{:S(2)}) %collective-permute-start.11) | collective-permute-done | bytes 16416 | tf_op jit(solution)/shard_map/ppermute | solution.py:701
  112.2 3.5 %shard_map.191 = (f32[8,128]{1,0:T(8,128)S(1)}, f32[8,128]{1,0:T(8,128)S(1)}, f32[8,128]{1,0:T(8,128)S(1)}) custom-call(f32[128,128]{1,0:T(8,128)S(1)} %get-tuple-element.166.refs_0_, f32[32,128]{1,0:T(8,128)S(1)} %collective-permute-done.10.refs_1_, f32[32,128]{1,0:T(8,128)S(1)} %collective-permute-done.11.refs_2_, ...), custom_call_target="tpu_custom_call" | custom-call | tf_op jit(solution)/shard_map/pallas_call | solution.py:686
  116.9 5.5 %collective-permute-done.13.refs_3_ = f32[8,128]{1,0:T(8,128)S(1)} collective-permute-done((f32[8,128]{1,0:T(8,128)S(1)}, f32[8,128]{1,0:T(8,128)S(1)}, u32[]{:S(2)}, u32[]{:S(2)}) %collective-permute-start.13) | collective-permute-done | bytes 4128 | tf_op jit(solution)/shard_map/ppermute | solution.py:701
  122.7 3.1 %collective-permute-start.15 = (f32[8,128]{1,0:T(8,128)S(1)}, f32[8,128]{1,0:T(8,128)S(1)}, u32[]{:S(2)}, u32[]{:S(2)}) collective-permute-start(f32[8,128]{1,0:T(8,128)S(1)} %get-tuple-element.177), channel_id=1, source_target_pairs={{0,192},{64,128},{128,64},{192,0},{1,193},{65,129},{129,65},{193,1... | collective-permute-start | bytes 12296 | tf_op jit(solution)/shard_map/ppermute | solution.py:701
  (52 shorter events, 21.7 us)
Async XLA Ops:
  1.6 6.9 %collective-permute-start.1 = (f32[8,128]{1,0:T(8,128)S(1)}, f32[8,128]{1,0:T(8,128)S(1)}, u32[]{:S(2)}, u32[]{:S(2)}) collective-permute-start(f32[8,128]{1,0:T(8,128)S(1)} %get-tuple-element.91), channel_id=1, source_target_pairs={{0,192},{64,128},{128,64},{192,0},{1,193},{65,129},{129,65},{193,1... | collective-permute-start | bytes 12296 | tf_op jit(solution)/shard_map/ppermute | solution.py:701
  5.8 2.7 %collective-permute-start = (f32[8,128]{1,0:T(8,128)S(1)}, f32[8,128]{1,0:T(8,128)S(1)}, u32[]{:S(2)}, u32[]{:S(2)}) collective-permute-start(f32[8,128]{1,0:T(8,128)S(1)} %get-tuple-element.91), channel_id=1, source_target_pairs={{0,64},{64,0},{128,192},{192,128},{1,65},{65,1},{129,193},{193,129... | collective-permute-start | bytes 12296 | tf_op jit(solution)/shard_map/ppermute | solution.py:701
  7.2 30.1 %copy-start.8 = (f32[2,8,64]{2,1,0:T(8,128)}, f32[2,8,64]{2,1,0:T(8,128)S(1)}, u32[]{:S(2)}) copy-start(f32[2,8,64]{2,1,0:T(8,128)S(1)} %convert_bitcast_fusion.refs_3_.refs_1_) | copy-start | bytes 12292
  7.2 31.2 %copy-start.6 = (bf16[64,128]{1,0:T(8,128)(2,1)S(1)}, bf16[64,128]{1,0:T(8,128)(2,1)}, u32[]{:S(2)}) copy-start(bf16[64,128]{1,0:T(8,128)(2,1)} %refs_16_.1) | copy-start | bytes 49156
  8.5 35.1 %copy-start.7 = (s32[24,128]{1,0:T(8,128)}, s32[24,128]{1,0:T(8,128)S(1)}, u32[]{:S(2)}) copy-start(s32[24,128]{1,0:T(8,128)S(1)} %get-tuple-element.104.refs_4_) | copy-start | bytes 36868
  9.5 9.1 %collective-permute-start.3 = (f32[8,128]{1,0:T(8,128)S(1)}, f32[8,128]{1,0:T(8,128)S(1)}, u32[]{:S(2)}, u32[]{:S(2)}) collective-permute-start(f32[8,128]{1,0:T(8,128)S(1)} %get-tuple-element.103), channel_id=1, source_target_pairs={{0,63},{1,2},{2,1},{3,4},{4,3},{5,6},{6,5},{7,8},{8,7},{9,10},{10,... | collective-permute-start | bytes 12296 | tf_op jit(solution)/shard_map/ppermute | solution.py:701
  17.6 2.5 %collective-permute-start.2 = (f32[8,128]{1,0:T(8,128)S(1)}, f32[8,128]{1,0:T(8,128)S(1)}, u32[]{:S(2)}, u32[]{:S(2)}) collective-permute-start(f32[8,128]{1,0:T(8,128)S(1)} %get-tuple-element.103), channel_id=1, source_target_pairs={{0,1},{1,0},{2,3},{3,2},{4,5},{5,4},{6,7},{7,6},{8,9},{9,8},{10,11... | collective-permute-start | bytes 12296 | tf_op jit(solution)/shard_map/ppermute | solution.py:701
  24.2 5.2 %collective-permute-start.4 = (f32[32,128]{1,0:T(8,128)S(1)}, f32[32,128]{1,0:T(8,128)S(1)}, u32[]{:S(2)}, u32[]{:S(2)}) collective-permute-start(f32[32,128]{1,0:T(8,128)S(1)} %get-tuple-element.113), channel_id=1, source_target_pairs={{0,64},{64,0},{128,192},{192,128},{1,65},{65,1},{129,193},{193,129... | collective-permute-start | bytes 49160 | tf_op jit(solution)/shard_map/ppermute | solution.py:701
  26.2 4.7 %collective-permute-start.5 = (f32[32,128]{1,0:T(8,128)S(1)}, f32[32,128]{1,0:T(8,128)S(1)}, u32[]{:S(2)}, u32[]{:S(2)}) collective-permute-start(f32[32,128]{1,0:T(8,128)S(1)} %get-tuple-element.114), channel_id=1, source_target_pairs={{0,192},{64,128},{128,64},{192,0},{1,193},{65,129},{129,65},{193,1... | collective-permute-start | bytes 49160 | tf_op jit(solution)/shard_map/ppermute | solution.py:701
  31.3 6.0 %collective-permute-start.6 = (f32[48,128]{1,0:T(8,128)S(1)}, f32[48,128]{1,0:T(8,128)S(1)}, u32[]{:S(2)}, u32[]{:S(2)}) collective-permute-start(f32[48,128]{1,0:T(8,128)S(1)} %get-tuple-element.121), channel_id=1, source_target_pairs={{0,1},{1,0},{2,3},{3,2},{4,5},{5,4},{6,7},{7,6},{8,9},{9,8},{10,11... | collective-permute-start | bytes 73736 | tf_op jit(solution)/shard_map/ppermute | solution.py:701
  31.4 7.0 %collective-permute-start.7 = (f32[48,128]{1,0:T(8,128)S(1)}, f32[48,128]{1,0:T(8,128)S(1)}, u32[]{:S(2)}, u32[]{:S(2)}) collective-permute-start(f32[48,128]{1,0:T(8,128)S(1)} %get-tuple-element.122), channel_id=1, source_target_pairs={{0,63},{1,2},{2,1},{3,4},{4,3},{5,6},{6,5},{7,8},{8,7},{9,10},{10,... | collective-permute-start | bytes 73736 | tf_op jit(solution)/shard_map/ppermute | solution.py:701
  43.6 16.2 %all-to-all-start = ((f32[32,32,128]{2,1,0:T(8,128)}), f32[32,32,128]{2,1,0:T(8,128)S(1)}, u32[]{:S(2)}, u32[]{:S(2)}) async-start(f32[32,32,128]{2,1,0:T(8,128)} %bitcast.4), calls=%async_computation | async-start | bytes 1048576 | tf_op jit(solution)/shard_map/all_to_all | solution.py:780
  60.5 12.5 %all-to-all-start.1 = ((f32[8,32,128]{2,1,0:T(8,128)}), f32[8,32,128]{2,1,0:T(8,128)S(1)}, u32[]{:S(2)}, u32[]{:S(2)}) async-start(f32[8,32,128]{2,1,0:T(8,128)} %bitcast.6), calls=%async_computation.1 | async-start | bytes 262144 | tf_op jit(solution)/shard_map/all_to_all | solution.py:788
  74.0 17.2 %all-to-all-start.2 = ((f32[32,32,128]{2,1,0:T(8,128)}), f32[32,32,128]{2,1,0:T(8,128)S(1)}, u32[]{:S(2)}, u32[]{:S(2)}) async-start(f32[32,32,128]{2,1,0:T(8,128)} %bitcast.18), calls=%async_computation.2 | async-start | bytes 1048576 | tf_op jit(solution)/shard_map/all_to_all | solution.py:796
  91.1 21.0 %copy-start.4 = (bf16[256,3072]{1,0:T(8,128)(2,1)S(1)}, bf16[256,3072]{1,0:T(8,128)(2,1)}, u32[]{:S(2)}) copy-start(bf16[256,3072]{1,0:T(8,128)(2,1)} %get-tuple-element.169.refs_6_) | copy-start | bytes 4718596
  91.1 21.0 %copy-start.5 = (f32[8,24,128]{2,1,0:T(8,128)S(1)}, f32[8,24,128]{2,1,0:T(8,128)}, u32[]{:S(2)}) copy-start(f32[8,24,128]{2,1,0:T(8,128)} %get-tuple-element.130.refs_0_.refs_9_) | copy-start | bytes 294916
  97.9 2.8 %collective-permute-start.8 = (f32[48,128]{1,0:T(8,128)S(1)}, f32[48,128]{1,0:T(8,128)S(1)}, u32[]{:S(2)}, u32[]{:S(2)}) collective-permute-start(f32[48,128]{1,0:T(8,128)S(1)} %get-tuple-element.164), channel_id=1, source_target_pairs={{0,1},{1,0},{2,3},{3,2},{4,5},{5,4},{6,7},{7,6},{8,9},{9,8},{10,11... | collective-permute-start | bytes 73736 | tf_op jit(solution)/shard_map/ppermute | solution.py:701
  98.3 6.9 %collective-permute-start.9 = (f32[48,128]{1,0:T(8,128)S(1)}, f32[48,128]{1,0:T(8,128)S(1)}, u32[]{:S(2)}, u32[]{:S(2)}) collective-permute-start(f32[48,128]{1,0:T(8,128)S(1)} %get-tuple-element.165), channel_id=1, source_target_pairs={{0,63},{1,2},{2,1},{3,4},{4,3},{5,6},{6,5},{7,8},{8,7},{9,10},{10,... | collective-permute-start | bytes 73736 | tf_op jit(solution)/shard_map/ppermute | solution.py:701
  105.6 3.7 %collective-permute-start.10 = (f32[32,128]{1,0:T(8,128)S(1)}, f32[32,128]{1,0:T(8,128)S(1)}, u32[]{:S(2)}, u32[]{:S(2)}) collective-permute-start(f32[32,128]{1,0:T(8,128)S(1)} %get-tuple-element.167), channel_id=1, source_target_pairs={{0,64},{64,0},{128,192},{192,128},{1,65},{65,1},{129,193},{193,129... | collective-permute-start | bytes 49160 | tf_op jit(solution)/shard_map/ppermute | solution.py:701
  107.4 4.7 %collective-permute-start.11 = (f32[32,128]{1,0:T(8,128)S(1)}, f32[32,128]{1,0:T(8,128)S(1)}, u32[]{:S(2)}, u32[]{:S(2)}) collective-permute-start(f32[32,128]{1,0:T(8,128)S(1)} %get-tuple-element.168), channel_id=1, source_target_pairs={{0,192},{64,128},{128,64},{192,0},{1,193},{65,129},{129,65},{193,1... | collective-permute-start | bytes 49160 | tf_op jit(solution)/shard_map/ppermute | solution.py:701
  115.6 6.8 %collective-permute-start.13 = (f32[8,128]{1,0:T(8,128)S(1)}, f32[8,128]{1,0:T(8,128)S(1)}, u32[]{:S(2)}, u32[]{:S(2)}) collective-permute-start(f32[8,128]{1,0:T(8,128)S(1)} %get-tuple-element.175), channel_id=1, source_target_pairs={{0,63},{1,2},{2,1},{3,4},{4,3},{5,6},{6,5},{7,8},{8,7},{9,10},{10,... | collective-permute-start | bytes 12296 | tf_op jit(solution)/shard_map/ppermute | solution.py:701
  116.9 5.5 %collective-permute-start.12 = (f32[8,128]{1,0:T(8,128)S(1)}, f32[8,128]{1,0:T(8,128)S(1)}, u32[]{:S(2)}, u32[]{:S(2)}) collective-permute-start(f32[8,128]{1,0:T(8,128)S(1)} %get-tuple-element.175), channel_id=1, source_target_pairs={{0,1},{1,0},{2,3},{3,2},{4,5},{5,4},{6,7},{7,6},{8,9},{9,8},{10,11... | collective-permute-start | bytes 12296 | tf_op jit(solution)/shard_map/ppermute | solution.py:701
  122.7 4.6 %collective-permute-start.15 = (f32[8,128]{1,0:T(8,128)S(1)}, f32[8,128]{1,0:T(8,128)S(1)}, u32[]{:S(2)}, u32[]{:S(2)}) collective-permute-start(f32[8,128]{1,0:T(8,128)S(1)} %get-tuple-element.177), channel_id=1, source_target_pairs={{0,192},{64,128},{128,64},{192,0},{1,193},{65,129},{129,65},{193,1... | collective-permute-start | bytes 12296 | tf_op jit(solution)/shard_map/ppermute | solution.py:701
  125.7 1.5 %collective-permute-start.14 = (f32[8,128]{1,0:T(8,128)S(1)}, f32[8,128]{1,0:T(8,128)S(1)}, u32[]{:S(2)}, u32[]{:S(2)}) collective-permute-start(f32[8,128]{1,0:T(8,128)S(1)} %get-tuple-element.177), channel_id=1, source_target_pairs={{0,64},{64,0},{128,192},{192,128},{1,65},{65,1},{129,193},{193,129... | collective-permute-start | bytes 12296 | tf_op jit(solution)/shard_map/ppermute | solution.py:701
  (4 other events, 84.0 us)

commit v4 on v3

--- a/solution.py
+++ b/solution.py
@@ -196,7 +196,8 @@
     return jnp.where(group == 0, got[0], jnp.where(group == 1, got[1], got[2]))
 
 
-def fetch_kernel(nb_ref, live_ref, emb_ref, w1_ref, w2_ref, w3_ref, mix_ref, wave_ref, nb_out, live_out, emb_out, w1_out, w2_out, w3_out, mix_out, wave_out):
+def fetch_kernel(nb_ref, live_ref, emb_ref, w1_ref, w2_ref, w3_ref, mix_ref, wave_ref, send_ref, nb_out, live_out, emb_out, w1_out, w2_out, w3_out, mix_out, wave_out, send_out):
+    send_out[...] = send_ref[...]
     wave_out[...] = jnp.concatenate([wave_ref[...].astype(F32), jnp.zeros((5, K), F32)], 0)
     nb_out[...] = place(nb_ref[...])
     live_out[...] = live_ref[...].astype(F32)
@@ -474,7 +475,7 @@
 
 
 def ewald_kernel(
-    box_x, box_y, scale, s_ref, spectral_ref, cs_ref, wave_ref, charge_ref, h_in, h2_in, a_in, w_in, g_in, u_in,
+    box_x, box_y, scale, s_own_ref, s_other_ref, spectral_ref, cs_ref, wave_ref, charge_ref, h_in, h2_in, a_in, w_in, g_in, u_in,
     oh_in, mix_in, first_in, last_in, read_hidden_in, w_charge_in,
     energy_ref, gpos_ref, gown_ref, gpart_ref, ya_ref, yb_ref, t_ref, ginv_ref, ga_ref, gf_ref, gphase_ref,
 ):
@@ -482,12 +483,19 @@
     qt_hi, qt_lo = split(charge.T)
     q_three = jnp.concatenate([qt_hi.astype(F32), qt_lo.astype(F32), qt_hi.astype(F32)], 1).astype(BF16)
     total = jnp.zeros((2 * KC, 2 * ATOMS), F32)
+    core = lax.axis_index("co")
+
+    def structure(t):
+        half = t // 8 * 4 + t % 4
+        rows = slice(half * KC, (half + 1) * KC)
+        return jnp.where(core == t // 4 % 2, s_own_ref[rows, :], s_other_ref[rows, :])
+
     for t in range(TILES // 2):
         cols = slice(t * 128, (t + 1) * 128)
         late = slice(K + t * 128, K + (t + 1) * 128)
         filt = spectral_ref[:, cols] * scale
-        gc = filt * s_ref[t * KC : (t + 1) * KC, :]
-        gs = filt * s_ref[(TILES // 2 + t) * KC : (TILES // 2 + t + 1) * KC, :]
+        gc = filt * structure(t)
+        gs = filt * structure(TILES // 2 + t)
         cos, sin = cs_ref[:, cols], cs_ref[:, late]
         g_hi, g_lo = split(jnp.concatenate([gc, gs], 1))
         c_hi, c_lo = split(jnp.concatenate([cos, sin], 1))
@@ -736,13 +744,15 @@
 
     rows, ix, strip = call(strip_x_kernel, [small, index, small], Far(positions), Far(species[None]), Far(send_x))
     xa, xb = swap_x(strip, strip)
-    nb, live, emb, *near_nets, mix_near, wave = call(
+    nb, live, emb, *near_nets, mix_near, wave, send_near = call(
         fetch_kernel,
-        [((NB, 128), jnp.int32), ((NB, 128), F32), ((8, C), F32), (w1.shape, F32), (radial_mid.shape, BF16), (radial_out.shape, BF16), (mixing.shape, BF16), ((8, K), F32)],
-        Far(neighbours), Far(live_slots), emb, w1, Far(radial_mid), Far(w3), Far(mixing), Far(wave_ids), flops=10**8, moved=10**6,
-    )
-    xa, xb, nb, live, emb, near_nets, mix_near, wave = lax.optimization_barrier((xa, xb, nb, live, emb, near_nets, mix_near, wave))
-    part, iy, strip = call(strip_y_kernel, [small, index, small], rows, xa, xb, Far(send_y))
+        [((NB, 128), jnp.int32), ((NB, 128), F32), ((8, C), F32), (w1.shape, F32), (radial_mid.shape, BF16), (radial_out.shape, BF16), (mixing.shape, BF16), ((8, K), F32), (send_y.shape, jnp.int32)],
+        Far(neighbours), Far(live_slots), emb, w1, Far(radial_mid), Far(w3), Far(mixing), Far(wave_ids), Far(send_y), flops=10**8, moved=10**6,
+    )
+    xa, xb, nb, live, emb, near_nets, mix_near, wave, send_near = lax.optimization_barrier(
+        (xa, xb, nb, live, emb, near_nets, mix_near, wave, send_near)
+    )
+    part, iy, strip = call(strip_y_kernel, [small, index, small], rows, xa, xb, send_near)
     ya, yb = swap_y(strip, strip)
     nets = (Far(w1), Far(radial_mid), Far(w3))
     ylm_shape, a_shape, cs_shape = ((8, NB, 128), F32), ((9, C, 128), F32), ((ATOMS, 2 * K), F32)
@@ -787,18 +797,19 @@
     )
     mine = lax.all_to_all(mine, ("z",), 0, 0, tiled=True)
     mine, g_zero, u_zero = lax.optimization_barrier((mine, g_zero, u_zero))
-    (spread,) = call(functools.partial(sum_kernel, 8, NWIDE), [((NWIDE * rows_each, 128), F32, True)], mine)
+    (spread,) = call(functools.partial(sum_kernel, 8, NWIDE // 2), [((NWIDE // 2 * rows_each, 128), F32, True)], mine)
     a_later, _ = lax.optimization_barrier((a_one, spread))
     w_one, g_one, u_one = call(
         prepare_one_kernel, [edge3 + blocked, edge2 + blocked, edge3 + blocked],
         Far(a_later), Far(r_far, True, BLOCKS), Far(p_one, True, BLOCKS), Far(f_one, True, BLOCKS), Far(ylm), flops=10**9, moved=2 * 10**7,
     )
-    s_all = lax.all_to_all(spread, WIDE, 0, 0, tiled=True)
-    s_all, w_one, g_one, u_one = lax.optimization_barrier((s_all, w_one, g_one, u_one))
+    s_own = lax.all_to_all(spread, ("xh", "y", "xl"), 0, 0, tiled=True)
+    s_own, w_one, g_one, u_one = lax.optimization_barrier((s_own, w_one, g_one, u_one))
+    s_other = swap(s_own, ("co",), lambda i: i ^ 1)
     energy, gpos, gown, gpart, ya, yb, t_one = call(
         with_box(ewald_kernel, box_x, box_y, scale),
         [((1, 128), F32), small, square, square, strip_48, strip_48, ((9, NB, 128), F32)],
-        s_all, Far(spectral), Far(cs), Far(wave_ids), Far(charge), late(h_far), late(h_two), late(a_one),
+        s_own, s_other, Far(spectral), Far(cs), Far(wave_ids), Far(charge), late(h_far), late(h_two), late(a_one),
         Far(w_one, True, BLOCKS), Far(g_one, True, BLOCKS), Far(u_one, True, BLOCKS), late(oh), late(mixing), late(read_first[None]), late(read_last[None]), late(read_hidden),
         late(w_charge),
         scratch=[((3 * C, 128), F32), ((8, C, 128), F32), ((C, EDGES), BF16), ((2 * ATOMS, K), BF16)],

time: 129 us -> 127 us (0.984)
  waiting for transfers between devices: 31.9 us -> 29.6 us
    all_to_all x1, waiting for transfers between devices: 5.02 us -> 1.48 us  [body(): s_own = lax.all_to_all(spread, ('xh', 'y', 'xl'), 0, 0, tiled=True)]
    ppermute x16 -> x17, starting transfers between devices: 29.7 us -> 33.2 us  [swap(): return lax.ppermute(value, axes, [(i, of(i)) for i in range(count)])]
    all_to_all x1, starting transfers between devices: 6.04 us -> 3.71 us  [body(): s_own = lax.all_to_all(spread, ('xh', 'y', 'xl'), 0, 0, tiled=True)]
    ppermute x16 -> x17, waiting for transfers between devices: 21.1 us -> 22.3 us  [swap(): return lax.ppermute(value, axes, [(i, of(i)) for i in range(count)])]
  transfers between devices with their start and end apart: 19 -> 20, of which waited for: 12 -> 13; matrix products, arithmetic and copies ran while one was open for 1% -> 1% of each run, Pallas kernels for 18% -> 19%
where the time goes in v4:
time: 127 us; the launch traced here: 126 us
  Pallas kernels  47.8 us (38%)
  starting transfers between devices  46.3 us (36%)
  waiting for transfers between devices  29.6 us (23%)
  other arithmetic  1.37 us (1%)
    pallas_call x18, Pallas kernels, call(): pl.pallas_call(wrapped, out_shape=[pltpu.HBM(o[0], o[1]) if len(o) > 2 el...  47.8 us
    ppermute x17, starting transfers between devices, swap(): return lax.ppermute(value, axes, [(i, of(i)) for i in range(count)])  33.2 us
    ppermute x17, waiting for transfers between devices, swap(): return lax.ppermute(value, axes, [(i, of(i)) for i in range(count)])  22.3 us
    all_to_all x1, starting transfers between devices, body(): pieces = lax.all_to_all(s_part, WIDE, 0, 0, tiled=True)  5.04 us
    all_to_all x1, starting transfers between devices, body(): mine = lax.all_to_all(mine, ('z',), 0, 0, tiled=True)  4.33 us
    all_to_all x1, starting transfers between devices, body(): s_own = lax.all_to_all(spread, ('xh', 'y', 'xl'), 0, 0, tiled=True)  3.71 us
    all_to_all x1, waiting for transfers between devices, body(): mine = lax.all_to_all(mine, ('z',), 0, 0, tiled=True)  3.01 us
    all_to_all x1, waiting for transfers between devices, body(): pieces = lax.all_to_all(s_part, WIDE, 0, 0, tiled=True)  2.83 us
  transfers between devices with their start and end apart: 20, of which 13 were waited for; matrix products, arithmetic and copies ran while one was open for 1% of the time, Pallas kernels for 19%

profile of v4, /device:TPU:1, one launch (start us, length us, event | category | flops | bytes accessed | tf_op | source)
XLA Modules:
  0.0 126.2 jit_solution(6575893663671147134)
XLA Ops:
  1.6 4.2 %collective-permute-start.1 = (f32[8,128]{1,0:T(8,128)S(1)}, f32[8,128]{1,0:T(8,128)S(1)}, u32[]{:S(2)}, u32[]{:S(2)}) collective-permute-start(f32[8,128]{1,0:T(8,128)S(1)} %get-tuple-element.93), channel_id=1, source_target_pairs={{0,192},{64,128},{128,64},{192,0},{1,193},{65,129},{129,65},{193,1... | collective-permute-start | bytes 12296 | tf_op jit(solution)/shard_map/ppermute | solution.py:709
  8.8 8.1 %collective-permute-start.3 = (f32[8,128]{1,0:T(8,128)S(1)}, f32[8,128]{1,0:T(8,128)S(1)}, u32[]{:S(2)}, u32[]{:S(2)}) collective-permute-start(f32[8,128]{1,0:T(8,128)S(1)} %get-tuple-element.107), channel_id=1, source_target_pairs={{0,63},{1,2},{2,1},{3,4},{4,3},{5,6},{6,5},{7,8},{8,7},{9,10},{10,... | collective-permute-start | bytes 12296 | tf_op jit(solution)/shard_map/ppermute | solution.py:709
  19.4 4.1 %shard_map.179 = (f32[8,24,128]{2,1,0:T(8,128)S(1)}, f32[8,24,128]{2,1,0:T(8,128)S(1)}, bf16[128,3072]{1,0:T(8,128)(2,1)}, bf16[384,3072]{1,0:T(8,128)(2,1)}, f3...) custom-call(f32[8,128]{1,0:T(8,128)S(1)} %get-tuple-element.119.refs_0_, ...), custom_call_target="tpu_custom_call" | custom-call | tf_op jit(solution)/shard_map/pallas_call | solution.py:694
  23.5 2.0 %collective-permute-start.4 = (f32[32,128]{1,0:T(8,128)S(1)}, f32[32,128]{1,0:T(8,128)S(1)}, u32[]{:S(2)}, u32[]{:S(2)}) collective-permute-start(f32[32,128]{1,0:T(8,128)S(1)} %get-tuple-element.117), channel_id=1, source_target_pairs={{0,64},{64,0},{128,192},{192,128},{1,65},{65,1},{129,193},{193,129... | collective-permute-start | bytes 49160 | tf_op jit(solution)/shard_map/ppermute | solution.py:709
  25.5 2.1 %collective-permute-start.5 = (f32[32,128]{1,0:T(8,128)S(1)}, f32[32,128]{1,0:T(8,128)S(1)}, u32[]{:S(2)}, u32[]{:S(2)}) collective-permute-start(f32[32,128]{1,0:T(8,128)S(1)} %get-tuple-element.118), channel_id=1, source_target_pairs={{0,192},{64,128},{128,64},{192,0},{1,193},{65,129},{129,65},{193,1... | collective-permute-start | bytes 49160 | tf_op jit(solution)/shard_map/ppermute | solution.py:709
  30.7 4.0 %collective-permute-start.7 = (f32[48,128]{1,0:T(8,128)S(1)}, f32[48,128]{1,0:T(8,128)S(1)}, u32[]{:S(2)}, u32[]{:S(2)}) collective-permute-start(f32[48,128]{1,0:T(8,128)S(1)} %get-tuple-element.126), channel_id=1, source_target_pairs={{0,63},{1,2},{2,1},{3,4},{4,3},{5,6},{6,5},{7,8},{8,7},{9,10},{10,... | collective-permute-start | bytes 73736 | tf_op jit(solution)/shard_map/ppermute | solution.py:709
  37.7 5.2 %shard_map.183 = (bf16[128,3072]{1,0:T(8,128)(2,1)}, f32[9,128,128]{2,1,0:T(8,128)}, f32[128,128]{1,0:T(8,128)}, f32[64,128]{1,0:T(8,128)}, f32[1024,128]{1,0:T(...) custom-call(f32[128,128]{1,0:T(8,128)S(1)} %get-tuple-element.116.re, ...), custom_call_target="tpu_custom_call" | custom-call | tf_op jit(solution)/shard_map/pallas_call | solution.py:694
  43.0 5.0 %all-to-all-start = ((f32[32,32,128]{2,1,0:T(8,128)}), f32[32,32,128]{2,1,0:T(8,128)S(1)}, u32[]{:S(2)}, u32[]{:S(2)}) async-start(f32[32,32,128]{2,1,0:T(8,128)} %bitcast.4), calls=%async_computation | async-start | bytes 1048576 | tf_op jit(solution)/shard_map/all_to_all | solution.py:790
  48.0 8.3 %shard_map.184 = (bf16[384,3072]{1,0:T(8,128)(2,1)}, bf16[384,3072]{1,0:T(8,128)(2,1)}, bf16[384,3072]{1,0:T(8,128)(2,1)}) custom-call(f32[8,24,128]{2,1,0:T(8,128)} %get-tuple-element.134.refs_0_.refs_9_, f32[2,8,64]{2,1,0:T(8,128)} %copy-done.8, bf16[2,64,64]{2,1,0:T(8,128)(2,1)} %refs_2_.4, bf16[2,64,384]{2,1,0:T(8,128)(2,1)} %bitcast.21, s32[24,128]{1,0:T(8,128)} %copy-done.7), custom_call_target="tpu_custom_call" | custom-call | flops 1000000000 | bytes 20000000 | tf_op jit(solution)/shard_map/pallas_call | solution.py:694
  56.3 2.8 %all-to-all-done = f32[32,32,128]{2,1,0:T(8,128)S(1)} async-done(((f32[32,32,128]{2,1,0:T(8,128)}), f32[32,32,128]{2,1,0:T(8,128)S(1)}, u32[]{:S(2)}, u32[]{:S(2)}) %all-to-all-start) | async-done | bytes 524320 | tf_op jit(solution)/shard_map/all_to_all | solution.py:790
  59.8 4.3 %all-to-all-start.1 = ((f32[8,32,128]{2,1,0:T(8,128)}), f32[8,32,128]{2,1,0:T(8,128)S(1)}, u32[]{:S(2)}, u32[]{:S(2)}) async-start(f32[8,32,128]{2,1,0:T(8,128)} %bitcast.6), calls=%async_computation.1 | async-start | bytes 262144 | tf_op jit(solution)/shard_map/all_to_all | solution.py:798
  64.2 5.2 %shard_map.186 = (bf16[256,3072]{1,0:T(8,128)(2,1)}, bf16[384,3072]{1,0:T(8,128)(2,1)}) custom-call(f32[9,128,128]{2,1,0:T(8,128)} %get-tuple-element.140.refs_0_.refs_5_, bf16[384,3072]{1,0:T(8,128)(2,1)} %get-tuple-element.141.refs_1_, bf16[384,3072]{1,0:T(8,128)(2,1)} %get-tuple-element.142.refs_2_, bf16[128,3072]{1,0:T(8,128)(2,1)} %get-tuple-element.143.refs_3_, ...), custom_call_target="tpu_custom_call" | custom-call | flops 1000000000 | bytes 20000000 | tf_op jit(solution)/shard_map/pallas_call | solution.py:694
  69.4 3.0 %all-to-all-done.1 = f32[8,32,128]{2,1,0:T(8,128)S(1)} async-done(((f32[8,32,128]{2,1,0:T(8,128)}), f32[8,32,128]{2,1,0:T(8,128)S(1)}, u32[]{:S(2)}, u32[]{:S(2)}) %all-to-all-start.1) | async-done | bytes 131104 | tf_op jit(solution)/shard_map/all_to_all | solution.py:798
  73.2 3.7 %all-to-all-start.2 = ((f32[16,32,128]{2,1,0:T(8,128)}), f32[16,32,128]{2,1,0:T(8,128)S(1)}, u32[]{:S(2)}, u32[]{:S(2)}) async-start(f32[16,32,128]{2,1,0:T(8,128)} %bitcast.19), calls=%async_computation.2 | async-start | bytes 524288 | tf_op jit(solution)/shard_map/all_to_all | solution.py:806
  76.9 6.1 %shard_map.188 = (bf16[384,3072]{1,0:T(8,128)(2,1)}, bf16[256,3072]{1,0:T(8,128)(2,1)}, bf16[384,3072]{1,0:T(8,128)(2,1)}) custom-call(f32[9,128,128]{2,1,0:T(8,128)} %get-tuple-element.149.refs_0_.refs_8_, bf16[384,3072]{1,0:T(8,128)(2,1)} %get-tuple-element.150.refs_1_, bf16[384,3072]{1,0:T(8,128)(2,1)} %get-tuple-element.151.refs_2_, ...), custom_call_target="tpu_custom_call" | custom-call | flops 1000000000 | bytes 20000000 | tf_op jit(solution)/shard_map/pallas_call | solution.py:694
  84.4 3.4 %collective-permute-start.8 = (f32[512,128]{1,0:T(8,128)S(1)}, f32[512,128]{1,0:T(8,128)S(1)}, u32[]{:S(2)}, u32[]{:S(2)}) collective-permute-start(f32[512,128]{1,0:T(8,128)S(1)} %bitcast.16), channel_id=1, source_target_pairs={{0,64},{64,0},{1,65},{65,1},{2,66},{66,2},{3,67},{67,3},{4,68},{68... | collective-permute-start | bytes 786440 | tf_op jit(solution)/shard_map/ppermute | solution.py:709
  89.0 6.8 %shard_map.189 = (f32[1,128]{1,0:T(1,128)}, f32[8,128]{1,0:T(8,128)S(1)}, f32[128,128]{1,0:T(8,128)S(1)}, f32[128,128]{1,0:T(8,128)S(1)}, f32[48,128]{1,0:T(8,12...) custom-call(f32[512,128]{1,0:T(8,128)S(1)} %bitcast.17, f32[512,128]{1,0:T(8,128)S(1)} %collective-permute-done.8.refs_1_, ...), custom_call_target="tpu_custom_call" | custom-call | tf_op jit(solution)/shard_map/pallas_call | solution.py:694
  98.6 4.5 %collective-permute-done.10.refs_3_ = f32[48,128]{1,0:T(8,128)S(1)} collective-permute-done((f32[48,128]{1,0:T(8,128)S(1)}, f32[48,128]{1,0:T(8,128)S(1)}, u32[]{:S(2)}, u32[]{:S(2)}) %collective-permute-start.10) | collective-permute-done | bytes 24608 | tf_op jit(solution)/shard_map/ppermute | solution.py:709
  103.5 1.9 %collective-permute-start.11 = (f32[32,128]{1,0:T(8,128)S(1)}, f32[32,128]{1,0:T(8,128)S(1)}, u32[]{:S(2)}, u32[]{:S(2)}) collective-permute-start(f32[32,128]{1,0:T(8,128)S(1)} %get-tuple-element.171), channel_id=1, source_target_pairs={{0,64},{64,0},{128,192},{192,128},{1,65},{65,1},{129,193},{193,129... | collective-permute-start | bytes 49160 | tf_op jit(solution)/shard_map/ppermute | solution.py:709
  105.4 2.0 %collective-permute-start.12 = (f32[32,128]{1,0:T(8,128)S(1)}, f32[32,128]{1,0:T(8,128)S(1)}, u32[]{:S(2)}, u32[]{:S(2)}) collective-permute-start(f32[32,128]{1,0:T(8,128)S(1)} %get-tuple-element.172), channel_id=1, source_target_pairs={{0,192},{64,128},{128,64},{192,0},{1,193},{65,129},{129,65},{193,1... | collective-permute-start | bytes 49160 | tf_op jit(solution)/shard_map/ppermute | solution.py:709
  107.4 2.7 %collective-permute-done.12.refs_2_ = f32[32,128]{1,0:T(8,128)S(1)} collective-permute-done((f32[32,128]{1,0:T(8,128)S(1)}, f32[32,128]{1,0:T(8,128)S(1)}, u32[]{:S(2)}, u32[]{:S(2)}) %collective-permute-start.12) | collective-permute-done | bytes 16416 | tf_op jit(solution)/shard_map/ppermute | solution.py:709
  110.1 3.5 %shard_map.191 = (f32[8,128]{1,0:T(8,128)S(1)}, f32[8,128]{1,0:T(8,128)S(1)}, f32[8,128]{1,0:T(8,128)S(1)}) custom-call(f32[128,128]{1,0:T(8,128)S(1)} %get-tuple-element.170.refs_0_, f32[32,128]{1,0:T(8,128)S(1)} %collective-permute-done.11.refs_1_, f32[32,128]{1,0:T(8,128)S(1)} %collective-permute-done.12.refs_2_, ...), custom_call_target="tpu_custom_call" | custom-call | tf_op jit(solution)/shard_map/pallas_call | solution.py:694
  114.5 5.8 %collective-permute-done.14.refs_3_ = f32[8,128]{1,0:T(8,128)S(1)} collective-permute-done((f32[8,128]{1,0:T(8,128)S(1)}, f32[8,128]{1,0:T(8,128)S(1)}, u32[]{:S(2)}, u32[]{:S(2)}) %collective-permute-start.14) | collective-permute-done | bytes 4128 | tf_op jit(solution)/shard_map/ppermute | solution.py:709
  120.6 3.2 %collective-permute-start.16 = (f32[8,128]{1,0:T(8,128)S(1)}, f32[8,128]{1,0:T(8,128)S(1)}, u32[]{:S(2)}, u32[]{:S(2)}) collective-permute-start(f32[8,128]{1,0:T(8,128)S(1)} %get-tuple-element.181), channel_id=1, source_target_pairs={{0,192},{64,128},{128,64},{192,0},{1,193},{65,129},{129,65},{193,1... | collective-permute-start | bytes 12296 | tf_op jit(solution)/shard_map/ppermute | solution.py:709
  (54 shorter events, 23.0 us)
Async XLA Ops:
  1.6 6.9 %collective-permute-start.1 = (f32[8,128]{1,0:T(8,128)S(1)}, f32[8,128]{1,0:T(8,128)S(1)}, u32[]{:S(2)}, u32[]{:S(2)}) collective-permute-start(f32[8,128]{1,0:T(8,128)S(1)} %get-tuple-element.93), channel_id=1, source_target_pairs={{0,192},{64,128},{128,64},{192,0},{1,193},{65,129},{129,65},{193,1... | collective-permute-start | bytes 12296 | tf_op jit(solution)/shard_map/ppermute | solution.py:709
  5.8 2.7 %collective-permute-start = (f32[8,128]{1,0:T(8,128)S(1)}, f32[8,128]{1,0:T(8,128)S(1)}, u32[]{:S(2)}, u32[]{:S(2)}) collective-permute-start(f32[8,128]{1,0:T(8,128)S(1)} %get-tuple-element.93), channel_id=1, source_target_pairs={{0,64},{64,0},{128,192},{192,128},{1,65},{65,1},{129,193},{193,129... | collective-permute-start | bytes 12296 | tf_op jit(solution)/shard_map/ppermute | solution.py:709
  7.2 29.4 %copy-start.8 = (f32[2,8,64]{2,1,0:T(8,128)}, f32[2,8,64]{2,1,0:T(8,128)S(1)}, u32[]{:S(2)}) copy-start(f32[2,8,64]{2,1,0:T(8,128)S(1)} %convert_bitcast_fusion.refs_3_.refs_1_) | copy-start | bytes 12292
  7.2 30.5 %copy-start.6 = (bf16[64,128]{1,0:T(8,128)(2,1)S(1)}, bf16[64,128]{1,0:T(8,128)(2,1)}, u32[]{:S(2)}) copy-start(bf16[64,128]{1,0:T(8,128)(2,1)} %refs_17_.1) | copy-start | bytes 49156
  8.5 34.5 %copy-start.7 = (s32[24,128]{1,0:T(8,128)}, s32[24,128]{1,0:T(8,128)S(1)}, u32[]{:S(2)}) copy-start(s32[24,128]{1,0:T(8,128)S(1)} %get-tuple-element.108.refs_4_) | copy-start | bytes 36868
  8.8 9.1 %collective-permute-start.3 = (f32[8,128]{1,0:T(8,128)S(1)}, f32[8,128]{1,0:T(8,128)S(1)}, u32[]{:S(2)}, u32[]{:S(2)}) collective-permute-start(f32[8,128]{1,0:T(8,128)S(1)} %get-tuple-element.107), channel_id=1, source_target_pairs={{0,63},{1,2},{2,1},{3,4},{4,3},{5,6},{6,5},{7,8},{8,7},{9,10},{10,... | collective-permute-start | bytes 12296 | tf_op jit(solution)/shard_map/ppermute | solution.py:709
  17.0 2.5 %collective-permute-start.2 = (f32[8,128]{1,0:T(8,128)S(1)}, f32[8,128]{1,0:T(8,128)S(1)}, u32[]{:S(2)}, u32[]{:S(2)}) collective-permute-start(f32[8,128]{1,0:T(8,128)S(1)} %get-tuple-element.107), channel_id=1, source_target_pairs={{0,1},{1,0},{2,3},{3,2},{4,5},{5,4},{6,7},{7,6},{8,9},{9,8},{10,11... | collective-permute-start | bytes 12296 | tf_op jit(solution)/shard_map/ppermute | solution.py:709
  23.5 5.2 %collective-permute-start.4 = (f32[32,128]{1,0:T(8,128)S(1)}, f32[32,128]{1,0:T(8,128)S(1)}, u32[]{:S(2)}, u32[]{:S(2)}) collective-permute-start(f32[32,128]{1,0:T(8,128)S(1)} %get-tuple-element.117), channel_id=1, source_target_pairs={{0,64},{64,0},{128,192},{192,128},{1,65},{65,1},{129,193},{193,129... | collective-permute-start | bytes 49160 | tf_op jit(solution)/shard_map/ppermute | solution.py:709
  25.5 4.7 %collective-permute-start.5 = (f32[32,128]{1,0:T(8,128)S(1)}, f32[32,128]{1,0:T(8,128)S(1)}, u32[]{:S(2)}, u32[]{:S(2)}) collective-permute-start(f32[32,128]{1,0:T(8,128)S(1)} %get-tuple-element.118), channel_id=1, source_target_pairs={{0,192},{64,128},{128,64},{192,0},{1,193},{65,129},{129,65},{193,1... | collective-permute-start | bytes 49160 | tf_op jit(solution)/shard_map/ppermute | solution.py:709
  30.6 6.0 %collective-permute-start.6 = (f32[48,128]{1,0:T(8,128)S(1)}, f32[48,128]{1,0:T(8,128)S(1)}, u32[]{:S(2)}, u32[]{:S(2)}) collective-permute-start(f32[48,128]{1,0:T(8,128)S(1)} %get-tuple-element.125), channel_id=1, source_target_pairs={{0,1},{1,0},{2,3},{3,2},{4,5},{5,4},{6,7},{7,6},{8,9},{9,8},{10,11... | collective-permute-start | bytes 73736 | tf_op jit(solution)/shard_map/ppermute | solution.py:709
  30.7 7.0 %collective-permute-start.7 = (f32[48,128]{1,0:T(8,128)S(1)}, f32[48,128]{1,0:T(8,128)S(1)}, u32[]{:S(2)}, u32[]{:S(2)}) collective-permute-start(f32[48,128]{1,0:T(8,128)S(1)} %get-tuple-element.126), channel_id=1, source_target_pairs={{0,63},{1,2},{2,1},{3,4},{4,3},{5,6},{6,5},{7,8},{8,7},{9,10},{10,... | collective-permute-start | bytes 73736 | tf_op jit(solution)/shard_map/ppermute | solution.py:709
  43.0 16.1 %all-to-all-start = ((f32[32,32,128]{2,1,0:T(8,128)}), f32[32,32,128]{2,1,0:T(8,128)S(1)}, u32[]{:S(2)}, u32[]{:S(2)}) async-start(f32[32,32,128]{2,1,0:T(8,128)} %bitcast.4), calls=%async_computation | async-start | bytes 1048576 | tf_op jit(solution)/shard_map/all_to_all | solution.py:790
  59.8 12.5 %all-to-all-start.1 = ((f32[8,32,128]{2,1,0:T(8,128)}), f32[8,32,128]{2,1,0:T(8,128)S(1)}, u32[]{:S(2)}, u32[]{:S(2)}) async-start(f32[8,32,128]{2,1,0:T(8,128)} %bitcast.6), calls=%async_computation.1 | async-start | bytes 262144 | tf_op jit(solution)/shard_map/all_to_all | solution.py:798
  73.2 11.3 %all-to-all-start.2 = ((f32[16,32,128]{2,1,0:T(8,128)}), f32[16,32,128]{2,1,0:T(8,128)S(1)}, u32[]{:S(2)}, u32[]{:S(2)}) async-start(f32[16,32,128]{2,1,0:T(8,128)} %bitcast.19), calls=%async_computation.2 | async-start | bytes 524288 | tf_op jit(solution)/shard_map/all_to_all | solution.py:806
  84.4 4.6 %collective-permute-start.8 = (f32[512,128]{1,0:T(8,128)S(1)}, f32[512,128]{1,0:T(8,128)S(1)}, u32[]{:S(2)}, u32[]{:S(2)}) collective-permute-start(f32[512,128]{1,0:T(8,128)S(1)} %bitcast.16), channel_id=1, source_target_pairs={{0,64},{64,0},{1,65},{65,1},{2,66},{66,2},{3,67},{67,3},{4,68},{68... | collective-permute-start | bytes 786440 | tf_op jit(solution)/shard_map/ppermute | solution.py:709
  89.0 21.1 %copy-start.5 = (f32[8,24,128]{2,1,0:T(8,128)S(1)}, f32[8,24,128]{2,1,0:T(8,128)}, u32[]{:S(2)}) copy-start(f32[8,24,128]{2,1,0:T(8,128)} %get-tuple-element.134.refs_0_.refs_9_) | copy-start | bytes 294916
  95.8 2.8 %collective-permute-start.9 = (f32[48,128]{1,0:T(8,128)S(1)}, f32[48,128]{1,0:T(8,128)S(1)}, u32[]{:S(2)}, u32[]{:S(2)}) collective-permute-start(f32[48,128]{1,0:T(8,128)S(1)} %get-tuple-element.168), channel_id=1, source_target_pairs={{0,1},{1,0},{2,3},{3,2},{4,5},{5,4},{6,7},{7,6},{8,9},{9,8},{10,11... | collective-permute-start | bytes 73736 | tf_op jit(solution)/shard_map/ppermute | solution.py:709
  96.2 6.9 %collective-permute-start.10 = (f32[48,128]{1,0:T(8,128)S(1)}, f32[48,128]{1,0:T(8,128)S(1)}, u32[]{:S(2)}, u32[]{:S(2)}) collective-permute-start(f32[48,128]{1,0:T(8,128)S(1)} %get-tuple-element.169), channel_id=1, source_target_pairs={{0,63},{1,2},{2,1},{3,4},{4,3},{5,6},{6,5},{7,8},{8,7},{9,10},{10,... | collective-permute-start | bytes 73736 | tf_op jit(solution)/shard_map/ppermute | solution.py:709
  103.5 3.9 %collective-permute-start.11 = (f32[32,128]{1,0:T(8,128)S(1)}, f32[32,128]{1,0:T(8,128)S(1)}, u32[]{:S(2)}, u32[]{:S(2)}) collective-permute-start(f32[32,128]{1,0:T(8,128)S(1)} %get-tuple-element.171), channel_id=1, source_target_pairs={{0,64},{64,0},{128,192},{192,128},{1,65},{65,1},{129,193},{193,129... | collective-permute-start | bytes 49160 | tf_op jit(solution)/shard_map/ppermute | solution.py:709
  105.4 4.7 %collective-permute-start.12 = (f32[32,128]{1,0:T(8,128)S(1)}, f32[32,128]{1,0:T(8,128)S(1)}, u32[]{:S(2)}, u32[]{:S(2)}) collective-permute-start(f32[32,128]{1,0:T(8,128)S(1)} %get-tuple-element.172), channel_id=1, source_target_pairs={{0,192},{64,128},{128,64},{192,0},{1,193},{65,129},{129,65},{193,1... | collective-permute-start | bytes 49160 | tf_op jit(solution)/shard_map/ppermute | solution.py:709
  113.6 6.8 %collective-permute-start.14 = (f32[8,128]{1,0:T(8,128)S(1)}, f32[8,128]{1,0:T(8,128)S(1)}, u32[]{:S(2)}, u32[]{:S(2)}) collective-permute-start(f32[8,128]{1,0:T(8,128)S(1)} %get-tuple-element.179), channel_id=1, source_target_pairs={{0,63},{1,2},{2,1},{3,4},{4,3},{5,6},{6,5},{7,8},{8,7},{9,10},{10,... | collective-permute-start | bytes 12296 | tf_op jit(solution)/shard_map/ppermute | solution.py:709
  114.5 5.9 %collective-permute-start.13 = (f32[8,128]{1,0:T(8,128)S(1)}, f32[8,128]{1,0:T(8,128)S(1)}, u32[]{:S(2)}, u32[]{:S(2)}) collective-permute-start(f32[8,128]{1,0:T(8,128)S(1)} %get-tuple-element.179), channel_id=1, source_target_pairs={{0,1},{1,0},{2,3},{3,2},{4,5},{5,4},{6,7},{7,6},{8,9},{9,8},{10,11... | collective-permute-start | bytes 12296 | tf_op jit(solution)/shard_map/ppermute | solution.py:709
  120.6 4.6 %collective-permute-start.16 = (f32[8,128]{1,0:T(8,128)S(1)}, f32[8,128]{1,0:T(8,128)S(1)}, u32[]{:S(2)}, u32[]{:S(2)}) collective-permute-start(f32[8,128]{1,0:T(8,128)S(1)} %get-tuple-element.181), channel_id=1, source_target_pairs={{0,192},{64,128},{128,64},{192,0},{1,193},{65,129},{129,65},{193,1... | collective-permute-start | bytes 12296 | tf_op jit(solution)/shard_map/ppermute | solution.py:709
  123.8 1.4 %collective-permute-start.15 = (f32[8,128]{1,0:T(8,128)S(1)}, f32[8,128]{1,0:T(8,128)S(1)}, u32[]{:S(2)}, u32[]{:S(2)}) collective-permute-start(f32[8,128]{1,0:T(8,128)S(1)} %get-tuple-element.181), channel_id=1, source_target_pairs={{0,64},{64,0},{128,192},{192,128},{1,65},{65,1},{129,193},{193,129... | collective-permute-start | bytes 12296 | tf_op jit(solution)/shard_map/ppermute | solution.py:709
  (5 other events, 105.4 us)

commit v5 on v4

--- a/solution.py
+++ b/solution.py
@@ -358,8 +358,10 @@
 
 def second_kernel(
     h_ref, part_ref, a_in, b_in, nb_ref, y_ref, r_ref, cs_ref, mix_ref,
-    w_charge_ref, geo_ref, a_zero_ref, f_out, a_out, h2_out, charge_out, s_ref, ypart_ref,
+    w_charge_ref, geo_ref, a_zero_ref, f_out, a_out, h2_out, charge_out, s_ref, ypart_ref, lane_ref, group_ref,
 ):
+    lane_ref[...] = nb_ref[...] & 127
+    group_ref[...] = nb_ref[...] >> 7
     f_ref, a_ref, h2_ref, charge_ref = f_out.ref, a_out.ref, h2_out.ref, charge_out.ref
     ypart_ref[...] = received(a_in, b_in, 64)
 
@@ -368,8 +370,9 @@
         tables = [h_ref[rows, :], part_ref[rows, :], ypart_ref[rows, :]]
 
         def state(n):
-            nb = jnp.broadcast_to(nb_ref[n : n + 1, :], (16, 128))
-            f = take_lanes(tables, nb & 127, nb >> 7)
+            lane = jnp.broadcast_to(lane_ref[n : n + 1, :], (8, 128))
+            group = jnp.broadcast_to(group_ref[n : n + 1, :], (8, 128))
+            f = jnp.concatenate([take_lanes([t[half : half + 8] for t in tables], lane, group) for half in (0, 8)], 0)
             f_ref[rows, n * 128 : (n + 1) * 128] = f.astype(BF16)
             return f
 
@@ -777,7 +780,7 @@
             a_shape + (True, 11),
         ],
         h_one, fpart, ya, yb, nb, ylm, r_one, cs, mix_near, w_charge, geo, a_zero,
-        scratch=[square],
+        scratch=[square, ((NB, 128), jnp.int32), ((NB, 128), jnp.int32)],
     )
     late = lambda array: Far(array, True)
     edge2 = ((2 * C, EDGES), BF16)

time: 127 us -> 127 us (level)
  no operation moved by 1% of the time
where the time goes in v5:
time: 127 us; the launch traced here: 126 us
  Pallas kernels  47.8 us (38%)
  starting transfers between devices  46.3 us (36%)
  waiting for transfers between devices  29.6 us (23%)
  other arithmetic  1.37 us (1%)
    pallas_call x18, Pallas kernels, call(): pl.pallas_call(wrapped, out_shape=[pltpu.HBM(o[0], o[1]) if len(o) > 2 el...  47.8 us
    ppermute x17, starting transfers between devices, swap(): return lax.ppermute(value, axes, [(i, of(i)) for i in range(count)])  33.2 us
    ppermute x17, waiting for transfers between devices, swap(): return lax.ppermute(value, axes, [(i, of(i)) for i in range(count)])  22.3 us
    all_to_all x1, starting transfers between devices, body(): pieces = lax.all_to_all(s_part, WIDE, 0, 0, tiled=True)  5.04 us
    all_to_all x1, starting transfers between devices, body(): mine = lax.all_to_all(mine, ('z',), 0, 0, tiled=True)  4.33 us
    all_to_all x1, starting transfers between devices, body(): s_own = lax.all_to_all(spread, ('xh', 'y', 'xl'), 0, 0, tiled=True)  3.71 us
    all_to_all x1, waiting for transfers between devices, body(): mine = lax.all_to_all(mine, ('z',), 0, 0, tiled=True)  3.01 us
    all_to_all x1, waiting for transfers between devices, body(): pieces = lax.all_to_all(s_part, WIDE, 0, 0, tiled=True)  2.83 us
  transfers between devices with their start and end apart: 20, of which 13 were waited for; matrix products, arithmetic and copies ran while one was open for 1% of the time, Pallas kernels for 19%

profile of v5, /device:TPU:1, one launch (start us, length us, event | category | flops | bytes accessed | tf_op | source)
XLA Modules:
  0.0 126.2 jit_solution(2098605942331836454)
XLA Ops:
  1.6 4.2 %collective-permute-start.1 = (f32[8,128]{1,0:T(8,128)S(1)}, f32[8,128]{1,0:T(8,128)S(1)}, u32[]{:S(2)}, u32[]{:S(2)}) collective-permute-start(f32[8,128]{1,0:T(8,128)S(1)} %get-tuple-element.93), channel_id=1, source_target_pairs={{0,192},{64,128},{128,64},{192,0},{1,193},{65,129},{129,65},{193,1... | collective-permute-start | bytes 12296 | tf_op jit(solution)/shard_map/ppermute | solution.py:712
  8.8 8.1 %collective-permute-start.3 = (f32[8,128]{1,0:T(8,128)S(1)}, f32[8,128]{1,0:T(8,128)S(1)}, u32[]{:S(2)}, u32[]{:S(2)}) collective-permute-start(f32[8,128]{1,0:T(8,128)S(1)} %get-tuple-element.107), channel_id=1, source_target_pairs={{0,63},{1,2},{2,1},{3,4},{4,3},{5,6},{6,5},{7,8},{8,7},{9,10},{10,... | collective-permute-start | bytes 12296 | tf_op jit(solution)/shard_map/ppermute | solution.py:712
  19.4 4.1 %shard_map.179 = (f32[8,24,128]{2,1,0:T(8,128)S(1)}, f32[8,24,128]{2,1,0:T(8,128)S(1)}, bf16[128,3072]{1,0:T(8,128)(2,1)}, bf16[384,3072]{1,0:T(8,128)(2,1)}, f3...) custom-call(f32[8,128]{1,0:T(8,128)S(1)} %get-tuple-element.119.refs_0_, ...), custom_call_target="tpu_custom_call" | custom-call | tf_op jit(solution)/shard_map/pallas_call | solution.py:697
  23.5 2.0 %collective-permute-start.4 = (f32[32,128]{1,0:T(8,128)S(1)}, f32[32,128]{1,0:T(8,128)S(1)}, u32[]{:S(2)}, u32[]{:S(2)}) collective-permute-start(f32[32,128]{1,0:T(8,128)S(1)} %get-tuple-element.117), channel_id=1, source_target_pairs={{0,64},{64,0},{128,192},{192,128},{1,65},{65,1},{129,193},{193,129... | collective-permute-start | bytes 49160 | tf_op jit(solution)/shard_map/ppermute | solution.py:712
  25.5 2.1 %collective-permute-start.5 = (f32[32,128]{1,0:T(8,128)S(1)}, f32[32,128]{1,0:T(8,128)S(1)}, u32[]{:S(2)}, u32[]{:S(2)}) collective-permute-start(f32[32,128]{1,0:T(8,128)S(1)} %get-tuple-element.118), channel_id=1, source_target_pairs={{0,192},{64,128},{128,64},{192,0},{1,193},{65,129},{129,65},{193,1... | collective-permute-start | bytes 49160 | tf_op jit(solution)/shard_map/ppermute | solution.py:712
  30.7 4.0 %collective-permute-start.7 = (f32[48,128]{1,0:T(8,128)S(1)}, f32[48,128]{1,0:T(8,128)S(1)}, u32[]{:S(2)}, u32[]{:S(2)}) collective-permute-start(f32[48,128]{1,0:T(8,128)S(1)} %get-tuple-element.126), channel_id=1, source_target_pairs={{0,63},{1,2},{2,1},{3,4},{4,3},{5,6},{6,5},{7,8},{8,7},{9,10},{10,... | collective-permute-start | bytes 73736 | tf_op jit(solution)/shard_map/ppermute | solution.py:712
  37.7 5.2 %shard_map.183 = (bf16[128,3072]{1,0:T(8,128)(2,1)}, f32[9,128,128]{2,1,0:T(8,128)}, f32[128,128]{1,0:T(8,128)}, f32[64,128]{1,0:T(8,128)}, f32[1024,128]{1,0:T(...) custom-call(f32[128,128]{1,0:T(8,128)S(1)} %get-tuple-element.116.re, ...), custom_call_target="tpu_custom_call" | custom-call | tf_op jit(solution)/shard_map/pallas_call | solution.py:697
  42.9 5.0 %all-to-all-start = ((f32[32,32,128]{2,1,0:T(8,128)}), f32[32,32,128]{2,1,0:T(8,128)S(1)}, u32[]{:S(2)}, u32[]{:S(2)}) async-start(f32[32,32,128]{2,1,0:T(8,128)} %bitcast.4), calls=%async_computation | async-start | bytes 1048576 | tf_op jit(solution)/shard_map/all_to_all | solution.py:793
  48.0 8.3 %shard_map.184 = (bf16[384,3072]{1,0:T(8,128)(2,1)}, bf16[384,3072]{1,0:T(8,128)(2,1)}, bf16[384,3072]{1,0:T(8,128)(2,1)}) custom-call(f32[8,24,128]{2,1,0:T(8,128)} %get-tuple-element.134.refs_0_.refs_9_, f32[2,8,64]{2,1,0:T(8,128)} %copy-done.8, bf16[2,64,64]{2,1,0:T(8,128)(2,1)} %refs_2_.4, bf16[2,64,384]{2,1,0:T(8,128)(2,1)} %bitcast.21, s32[24,128]{1,0:T(8,128)} %copy-done.7), custom_call_target="tpu_custom_call" | custom-call | flops 1000000000 | bytes 20000000 | tf_op jit(solution)/shard_map/pallas_call | solution.py:697
  56.3 2.8 %all-to-all-done = f32[32,32,128]{2,1,0:T(8,128)S(1)} async-done(((f32[32,32,128]{2,1,0:T(8,128)}), f32[32,32,128]{2,1,0:T(8,128)S(1)}, u32[]{:S(2)}, u32[]{:S(2)}) %all-to-all-start) | async-done | bytes 524320 | tf_op jit(solution)/shard_map/all_to_all | solution.py:793
  59.8 4.3 %all-to-all-start.1 = ((f32[8,32,128]{2,1,0:T(8,128)}), f32[8,32,128]{2,1,0:T(8,128)S(1)}, u32[]{:S(2)}, u32[]{:S(2)}) async-start(f32[8,32,128]{2,1,0:T(8,128)} %bitcast.6), calls=%async_computation.1 | async-start | bytes 262144 | tf_op jit(solution)/shard_map/all_to_all | solution.py:801
  64.1 5.2 %shard_map.186 = (bf16[256,3072]{1,0:T(8,128)(2,1)}, bf16[384,3072]{1,0:T(8,128)(2,1)}) custom-call(f32[9,128,128]{2,1,0:T(8,128)} %get-tuple-element.140.refs_0_.refs_5_, bf16[384,3072]{1,0:T(8,128)(2,1)} %get-tuple-element.141.refs_1_, bf16[384,3072]{1,0:T(8,128)(2,1)} %get-tuple-element.142.refs_2_, bf16[128,3072]{1,0:T(8,128)(2,1)} %get-tuple-element.143.refs_3_, ...), custom_call_target="tpu_custom_call" | custom-call | flops 1000000000 | bytes 20000000 | tf_op jit(solution)/shard_map/pallas_call | solution.py:697
  69.3 3.0 %all-to-all-done.1 = f32[8,32,128]{2,1,0:T(8,128)S(1)} async-done(((f32[8,32,128]{2,1,0:T(8,128)}), f32[8,32,128]{2,1,0:T(8,128)S(1)}, u32[]{:S(2)}, u32[]{:S(2)}) %all-to-all-start.1) | async-done | bytes 131104 | tf_op jit(solution)/shard_map/all_to_all | solution.py:801
  73.1 3.7 %all-to-all-start.2 = ((f32[16,32,128]{2,1,0:T(8,128)}), f32[16,32,128]{2,1,0:T(8,128)S(1)}, u32[]{:S(2)}, u32[]{:S(2)}) async-start(f32[16,32,128]{2,1,0:T(8,128)} %bitcast.19), calls=%async_computation.2 | async-start | bytes 524288 | tf_op jit(solution)/shard_map/all_to_all | solution.py:809
  76.9 6.1 %shard_map.188 = (bf16[384,3072]{1,0:T(8,128)(2,1)}, bf16[256,3072]{1,0:T(8,128)(2,1)}, bf16[384,3072]{1,0:T(8,128)(2,1)}) custom-call(f32[9,128,128]{2,1,0:T(8,128)} %get-tuple-element.149.refs_0_.refs_8_, bf16[384,3072]{1,0:T(8,128)(2,1)} %get-tuple-element.150.refs_1_, bf16[384,3072]{1,0:T(8,128)(2,1)} %get-tuple-element.151.refs_2_, ...), custom_call_target="tpu_custom_call" | custom-call | flops 1000000000 | bytes 20000000 | tf_op jit(solution)/shard_map/pallas_call | solution.py:697
  84.4 3.4 %collective-permute-start.8 = (f32[512,128]{1,0:T(8,128)S(1)}, f32[512,128]{1,0:T(8,128)S(1)}, u32[]{:S(2)}, u32[]{:S(2)}) collective-permute-start(f32[512,128]{1,0:T(8,128)S(1)} %bitcast.16), channel_id=1, source_target_pairs={{0,64},{64,0},{1,65},{65,1},{2,66},{66,2},{3,67},{67,3},{4,68},{68... | collective-permute-start | bytes 786440 | tf_op jit(solution)/shard_map/ppermute | solution.py:712
  89.0 6.8 %shard_map.189 = (f32[1,128]{1,0:T(1,128)}, f32[8,128]{1,0:T(8,128)S(1)}, f32[128,128]{1,0:T(8,128)S(1)}, f32[128,128]{1,0:T(8,128)S(1)}, f32[48,128]{1,0:T(8,12...) custom-call(f32[512,128]{1,0:T(8,128)S(1)} %bitcast.17, f32[512,128]{1,0:T(8,128)S(1)} %collective-permute-done.8.refs_1_, ...), custom_call_target="tpu_custom_call" | custom-call | tf_op jit(solution)/shard_map/pallas_call | solution.py:697
  98.6 4.5 %collective-permute-done.10.refs_3_ = f32[48,128]{1,0:T(8,128)S(1)} collective-permute-done((f32[48,128]{1,0:T(8,128)S(1)}, f32[48,128]{1,0:T(8,128)S(1)}, u32[]{:S(2)}, u32[]{:S(2)}) %collective-permute-start.10) | collective-permute-done | bytes 24608 | tf_op jit(solution)/shard_map/ppermute | solution.py:712
  103.5 1.9 %collective-permute-start.11 = (f32[32,128]{1,0:T(8,128)S(1)}, f32[32,128]{1,0:T(8,128)S(1)}, u32[]{:S(2)}, u32[]{:S(2)}) collective-permute-start(f32[32,128]{1,0:T(8,128)S(1)} %get-tuple-element.171), channel_id=1, source_target_pairs={{0,64},{64,0},{128,192},{192,128},{1,65},{65,1},{129,193},{193,129... | collective-permute-start | bytes 49160 | tf_op jit(solution)/shard_map/ppermute | solution.py:712
  105.4 2.0 %collective-permute-start.12 = (f32[32,128]{1,0:T(8,128)S(1)}, f32[32,128]{1,0:T(8,128)S(1)}, u32[]{:S(2)}, u32[]{:S(2)}) collective-permute-start(f32[32,128]{1,0:T(8,128)S(1)} %get-tuple-element.172), channel_id=1, source_target_pairs={{0,192},{64,128},{128,64},{192,0},{1,193},{65,129},{129,65},{193,1... | collective-permute-start | bytes 49160 | tf_op jit(solution)/shard_map/ppermute | solution.py:712
  107.4 2.7 %collective-permute-done.12.refs_2_ = f32[32,128]{1,0:T(8,128)S(1)} collective-permute-done((f32[32,128]{1,0:T(8,128)S(1)}, f32[32,128]{1,0:T(8,128)S(1)}, u32[]{:S(2)}, u32[]{:S(2)}) %collective-permute-start.12) | collective-permute-done | bytes 16416 | tf_op jit(solution)/shard_map/ppermute | solution.py:712
  110.1 3.5 %shard_map.191 = (f32[8,128]{1,0:T(8,128)S(1)}, f32[8,128]{1,0:T(8,128)S(1)}, f32[8,128]{1,0:T(8,128)S(1)}) custom-call(f32[128,128]{1,0:T(8,128)S(1)} %get-tuple-element.170.refs_0_, f32[32,128]{1,0:T(8,128)S(1)} %collective-permute-done.11.refs_1_, f32[32,128]{1,0:T(8,128)S(1)} %collective-permute-done.12.refs_2_, ...), custom_call_target="tpu_custom_call" | custom-call | tf_op jit(solution)/shard_map/pallas_call | solution.py:697
  114.5 5.8 %collective-permute-done.14.refs_3_ = f32[8,128]{1,0:T(8,128)S(1)} collective-permute-done((f32[8,128]{1,0:T(8,128)S(1)}, f32[8,128]{1,0:T(8,128)S(1)}, u32[]{:S(2)}, u32[]{:S(2)}) %collective-permute-start.14) | collective-permute-done | bytes 4128 | tf_op jit(solution)/shard_map/ppermute | solution.py:712
  120.6 3.2 %collective-permute-start.16 = (f32[8,128]{1,0:T(8,128)S(1)}, f32[8,128]{1,0:T(8,128)S(1)}, u32[]{:S(2)}, u32[]{:S(2)}) collective-permute-start(f32[8,128]{1,0:T(8,128)S(1)} %get-tuple-element.181), channel_id=1, source_target_pairs={{0,192},{64,128},{128,64},{192,0},{1,193},{65,129},{129,65},{193,1... | collective-permute-start | bytes 12296 | tf_op jit(solution)/shard_map/ppermute | solution.py:712
  (54 shorter events, 23.0 us)
Async XLA Ops:
  1.6 6.9 %collective-permute-start.1 = (f32[8,128]{1,0:T(8,128)S(1)}, f32[8,128]{1,0:T(8,128)S(1)}, u32[]{:S(2)}, u32[]{:S(2)}) collective-permute-start(f32[8,128]{1,0:T(8,128)S(1)} %get-tuple-element.93), channel_id=1, source_target_pairs={{0,192},{64,128},{128,64},{192,0},{1,193},{65,129},{129,65},{193,1... | collective-permute-start | bytes 12296 | tf_op jit(solution)/shard_map/ppermute | solution.py:712
  5.8 2.7 %collective-permute-start = (f32[8,128]{1,0:T(8,128)S(1)}, f32[8,128]{1,0:T(8,128)S(1)}, u32[]{:S(2)}, u32[]{:S(2)}) collective-permute-start(f32[8,128]{1,0:T(8,128)S(1)} %get-tuple-element.93), channel_id=1, source_target_pairs={{0,64},{64,0},{128,192},{192,128},{1,65},{65,1},{129,193},{193,129... | collective-permute-start | bytes 12296 | tf_op jit(solution)/shard_map/ppermute | solution.py:712
  7.2 29.4 %copy-start.8 = (f32[2,8,64]{2,1,0:T(8,128)}, f32[2,8,64]{2,1,0:T(8,128)S(1)}, u32[]{:S(2)}) copy-start(f32[2,8,64]{2,1,0:T(8,128)S(1)} %convert_bitcast_fusion.refs_3_.refs_1_) | copy-start | bytes 12292
  7.2 30.5 %copy-start.6 = (bf16[64,128]{1,0:T(8,128)(2,1)S(1)}, bf16[64,128]{1,0:T(8,128)(2,1)}, u32[]{:S(2)}) copy-start(bf16[64,128]{1,0:T(8,128)(2,1)} %refs_17_.1) | copy-start | bytes 49156
  8.5 34.4 %copy-start.7 = (s32[24,128]{1,0:T(8,128)}, s32[24,128]{1,0:T(8,128)S(1)}, u32[]{:S(2)}) copy-start(s32[24,128]{1,0:T(8,128)S(1)} %get-tuple-element.108.refs_4_) | copy-start | bytes 36868
  8.8 9.1 %collective-permute-start.3 = (f32[8,128]{1,0:T(8,128)S(1)}, f32[8,128]{1,0:T(8,128)S(1)}, u32[]{:S(2)}, u32[]{:S(2)}) collective-permute-start(f32[8,128]{1,0:T(8,128)S(1)} %get-tuple-element.107), channel_id=1, source_target_pairs={{0,63},{1,2},{2,1},{3,4},{4,3},{5,6},{6,5},{7,8},{8,7},{9,10},{10,... | collective-permute-start | bytes 12296 | tf_op jit(solution)/shard_map/ppermute | solution.py:712
  17.0 2.5 %collective-permute-start.2 = (f32[8,128]{1,0:T(8,128)S(1)}, f32[8,128]{1,0:T(8,128)S(1)}, u32[]{:S(2)}, u32[]{:S(2)}) collective-permute-start(f32[8,128]{1,0:T(8,128)S(1)} %get-tuple-element.107), channel_id=1, source_target_pairs={{0,1},{1,0},{2,3},{3,2},{4,5},{5,4},{6,7},{7,6},{8,9},{9,8},{10,11... | collective-permute-start | bytes 12296 | tf_op jit(solution)/shard_map/ppermute | solution.py:712
  23.5 5.2 %collective-permute-start.4 = (f32[32,128]{1,0:T(8,128)S(1)}, f32[32,128]{1,0:T(8,128)S(1)}, u32[]{:S(2)}, u32[]{:S(2)}) collective-permute-start(f32[32,128]{1,0:T(8,128)S(1)} %get-tuple-element.117), channel_id=1, source_target_pairs={{0,64},{64,0},{128,192},{192,128},{1,65},{65,1},{129,193},{193,129... | collective-permute-start | bytes 49160 | tf_op jit(solution)/shard_map/ppermute | solution.py:712
  25.5 4.7 %collective-permute-start.5 = (f32[32,128]{1,0:T(8,128)S(1)}, f32[32,128]{1,0:T(8,128)S(1)}, u32[]{:S(2)}, u32[]{:S(2)}) collective-permute-start(f32[32,128]{1,0:T(8,128)S(1)} %get-tuple-element.118), channel_id=1, source_target_pairs={{0,192},{64,128},{128,64},{192,0},{1,193},{65,129},{129,65},{193,1... | collective-permute-start | bytes 49160 | tf_op jit(solution)/shard_map/ppermute | solution.py:712
  30.6 6.0 %collective-permute-start.6 = (f32[48,128]{1,0:T(8,128)S(1)}, f32[48,128]{1,0:T(8,128)S(1)}, u32[]{:S(2)}, u32[]{:S(2)}) collective-permute-start(f32[48,128]{1,0:T(8,128)S(1)} %get-tuple-element.125), channel_id=1, source_target_pairs={{0,1},{1,0},{2,3},{3,2},{4,5},{5,4},{6,7},{7,6},{8,9},{9,8},{10,11... | collective-permute-start | bytes 73736 | tf_op jit(solution)/shard_map/ppermute | solution.py:712
  30.7 7.0 %collective-permute-start.7 = (f32[48,128]{1,0:T(8,128)S(1)}, f32[48,128]{1,0:T(8,128)S(1)}, u32[]{:S(2)}, u32[]{:S(2)}) collective-permute-start(f32[48,128]{1,0:T(8,128)S(1)} %get-tuple-element.126), channel_id=1, source_target_pairs={{0,63},{1,2},{2,1},{3,4},{4,3},{5,6},{6,5},{7,8},{8,7},{9,10},{10,... | collective-permute-start | bytes 73736 | tf_op jit(solution)/shard_map/ppermute | solution.py:712
  42.9 16.1 %all-to-all-start = ((f32[32,32,128]{2,1,0:T(8,128)}), f32[32,32,128]{2,1,0:T(8,128)S(1)}, u32[]{:S(2)}, u32[]{:S(2)}) async-start(f32[32,32,128]{2,1,0:T(8,128)} %bitcast.4), calls=%async_computation | async-start | bytes 1048576 | tf_op jit(solution)/shard_map/all_to_all | solution.py:793
  59.8 12.5 %all-to-all-start.1 = ((f32[8,32,128]{2,1,0:T(8,128)}), f32[8,32,128]{2,1,0:T(8,128)S(1)}, u32[]{:S(2)}, u32[]{:S(2)}) async-start(f32[8,32,128]{2,1,0:T(8,128)} %bitcast.6), calls=%async_computation.1 | async-start | bytes 262144 | tf_op jit(solution)/shard_map/all_to_all | solution.py:801
  73.1 11.3 %all-to-all-start.2 = ((f32[16,32,128]{2,1,0:T(8,128)}), f32[16,32,128]{2,1,0:T(8,128)S(1)}, u32[]{:S(2)}, u32[]{:S(2)}) async-start(f32[16,32,128]{2,1,0:T(8,128)} %bitcast.19), calls=%async_computation.2 | async-start | bytes 524288 | tf_op jit(solution)/shard_map/all_to_all | solution.py:809
  84.4 4.6 %collective-permute-start.8 = (f32[512,128]{1,0:T(8,128)S(1)}, f32[512,128]{1,0:T(8,128)S(1)}, u32[]{:S(2)}, u32[]{:S(2)}) collective-permute-start(f32[512,128]{1,0:T(8,128)S(1)} %bitcast.16), channel_id=1, source_target_pairs={{0,64},{64,0},{1,65},{65,1},{2,66},{66,2},{3,67},{67,3},{4,68},{68... | collective-permute-start | bytes 786440 | tf_op jit(solution)/shard_map/ppermute | solution.py:712
  89.0 21.1 %copy-start.5 = (f32[8,24,128]{2,1,0:T(8,128)S(1)}, f32[8,24,128]{2,1,0:T(8,128)}, u32[]{:S(2)}) copy-start(f32[8,24,128]{2,1,0:T(8,128)} %get-tuple-element.134.refs_0_.refs_9_) | copy-start | bytes 294916
  95.8 2.8 %collective-permute-start.9 = (f32[48,128]{1,0:T(8,128)S(1)}, f32[48,128]{1,0:T(8,128)S(1)}, u32[]{:S(2)}, u32[]{:S(2)}) collective-permute-start(f32[48,128]{1,0:T(8,128)S(1)} %get-tuple-element.168), channel_id=1, source_target_pairs={{0,1},{1,0},{2,3},{3,2},{4,5},{5,4},{6,7},{7,6},{8,9},{9,8},{10,11... | collective-permute-start | bytes 73736 | tf_op jit(solution)/shard_map/ppermute | solution.py:712
  96.2 6.9 %collective-permute-start.10 = (f32[48,128]{1,0:T(8,128)S(1)}, f32[48,128]{1,0:T(8,128)S(1)}, u32[]{:S(2)}, u32[]{:S(2)}) collective-permute-start(f32[48,128]{1,0:T(8,128)S(1)} %get-tuple-element.169), channel_id=1, source_target_pairs={{0,63},{1,2},{2,1},{3,4},{4,3},{5,6},{6,5},{7,8},{8,7},{9,10},{10,... | collective-permute-start | bytes 73736 | tf_op jit(solution)/shard_map/ppermute | solution.py:712
  103.5 3.9 %collective-permute-start.11 = (f32[32,128]{1,0:T(8,128)S(1)}, f32[32,128]{1,0:T(8,128)S(1)}, u32[]{:S(2)}, u32[]{:S(2)}) collective-permute-start(f32[32,128]{1,0:T(8,128)S(1)} %get-tuple-element.171), channel_id=1, source_target_pairs={{0,64},{64,0},{128,192},{192,128},{1,65},{65,1},{129,193},{193,129... | collective-permute-start | bytes 49160 | tf_op jit(solution)/shard_map/ppermute | solution.py:712
  105.4 4.7 %collective-permute-start.12 = (f32[32,128]{1,0:T(8,128)S(1)}, f32[32,128]{1,0:T(8,128)S(1)}, u32[]{:S(2)}, u32[]{:S(2)}) collective-permute-start(f32[32,128]{1,0:T(8,128)S(1)} %get-tuple-element.172), channel_id=1, source_target_pairs={{0,192},{64,128},{128,64},{192,0},{1,193},{65,129},{129,65},{193,1... | collective-permute-start | bytes 49160 | tf_op jit(solution)/shard_map/ppermute | solution.py:712
  113.6 6.8 %collective-permute-start.14 = (f32[8,128]{1,0:T(8,128)S(1)}, f32[8,128]{1,0:T(8,128)S(1)}, u32[]{:S(2)}, u32[]{:S(2)}) collective-permute-start(f32[8,128]{1,0:T(8,128)S(1)} %get-tuple-element.179), channel_id=1, source_target_pairs={{0,63},{1,2},{2,1},{3,4},{4,3},{5,6},{6,5},{7,8},{8,7},{9,10},{10,... | collective-permute-start | bytes 12296 | tf_op jit(solution)/shard_map/ppermute | solution.py:712
  114.5 5.9 %collective-permute-start.13 = (f32[8,128]{1,0:T(8,128)S(1)}, f32[8,128]{1,0:T(8,128)S(1)}, u32[]{:S(2)}, u32[]{:S(2)}) collective-permute-start(f32[8,128]{1,0:T(8,128)S(1)} %get-tuple-element.179), channel_id=1, source_target_pairs={{0,1},{1,0},{2,3},{3,2},{4,5},{5,4},{6,7},{7,6},{8,9},{9,8},{10,11... | collective-permute-start | bytes 12296 | tf_op jit(solution)/shard_map/ppermute | solution.py:712
  120.6 4.6 %collective-permute-start.16 = (f32[8,128]{1,0:T(8,128)S(1)}, f32[8,128]{1,0:T(8,128)S(1)}, u32[]{:S(2)}, u32[]{:S(2)}) collective-permute-start(f32[8,128]{1,0:T(8,128)S(1)} %get-tuple-element.181), channel_id=1, source_target_pairs={{0,192},{64,128},{128,64},{192,0},{1,193},{65,129},{129,65},{193,1... | collective-permute-start | bytes 12296 | tf_op jit(solution)/shard_map/ppermute | solution.py:712
  123.8 1.4 %collective-permute-start.15 = (f32[8,128]{1,0:T(8,128)S(1)}, f32[8,128]{1,0:T(8,128)S(1)}, u32[]{:S(2)}, u32[]{:S(2)}) collective-permute-start(f32[8,128]{1,0:T(8,128)S(1)} %get-tuple-element.181), channel_id=1, source_target_pairs={{0,64},{64,0},{128,192},{192,128},{1,65},{65,1},{129,193},{193,129... | collective-permute-start | bytes 12296 | tf_op jit(solution)/shard_map/ppermute | solution.py:712
  (5 other events, 105.4 us)
